TPU v7x, 128 devices: a whole 4x4x4 slice. The times are simulated.
128 devices in a mesh: dp: 32 (over x, z, core), row: 2 (over y_hi), col: 2 (over y_lo).
Axes of the slice: x: 4, y: 4 (y_hi: 2, y_lo: 2; y = y_hi * 2 + y_lo), z: 4, core: 2. Of those that a mesh axis runs over, the one named last changes fastest.
Arguments:
- tokens: bfloat16 [32768, 768], P(('dp', 'row'), 'col'), may hold values from -1.796875 to 1.796875
- ln1_gain: float32 [2, 768], P(None, 'col'), may hold values from 0.25 to 3.5
- ln1_shift: float32 [2, 768], P(None, 'col'), may hold values from -3 to 3
- w_query: bfloat16 [2, 768, 768], P(None, 'col', 'row'), may hold values from -0.21875 to 0.21875
- w_key: bfloat16 [2, 768, 768], P(None, 'col', 'row'), may hold values from -0.21875 to 0.21875
- w_value: bfloat16 [2, 768, 768], P(None, 'col', 'row'), may hold values from -0.21875 to 0.21875
- query_gain: float32 [2, 64], replicated, may hold values from 0.25 to 1.75
- key_gain: float32 [2, 64], replicated, may hold values from 0.25 to 1.75
- w_out: bfloat16 [2, 768, 768], P(None, 'row', 'col'), may hold values from -0.875 to 0.875
- ln2_gain: float32 [2, 768], P(None, 'col'), may hold values from 0.25 to 3.5
- ln2_shift: float32 [2, 768], P(None, 'col'), may hold values from -3 to 3
- w_up: bfloat16 [2, 768, 3072], P(None, 'col', 'row'), may hold values from -0.21875 to 0.21875
- up_bias: float32 [2, 3072], P(None, 'row'), may hold values from -3 to 3
- w_down: bfloat16 [2, 3072, 768], P(None, 'row', 'col'), may hold values from -0.109375 to 0.109375
- down_bias: float32 [2, 768], P(None, 'col'), may hold values from -3 to 3
- cotangent: bfloat16 [32768, 768], P(('dp', 'row'), 'col'), may hold values from -6 to 6
Outputs:
- out: bfloat16 [32768, 768], P(('dp', 'row'), 'col')
- grad_tokens: float32 [32768, 768], P(('dp', 'row'), 'col')
- grad_ln1_gain: float32 [2, 768], P(None, 'col')
- grad_ln1_shift: float32 [2, 768], P(None, 'col')
- grad_w_query: float32 [2, 768, 768], P(None, 'col', 'row')
- grad_w_key: float32 [2, 768, 768], P(None, 'col', 'row')
- grad_w_value: float32 [2, 768, 768], P(None, 'col', 'row')
- grad_query_gain: float32 [2, 64], replicated
- grad_key_gain: float32 [2, 64], replicated
- grad_w_out: float32 [2, 768, 768], P(None, 'row', 'col')
- grad_ln2_gain: float32 [2, 768], P(None, 'col')
- grad_ln2_shift: float32 [2, 768], P(None, 'col')
- grad_w_up: float32 [2, 768, 3072], P(None, 'col', 'row')
- grad_up_bias: float32 [2, 3072], P(None, 'row')
- grad_w_down: float32 [2, 3072, 768], P(None, 'row', 'col')
- grad_down_bias: float32 [2, 768], P(None, 'col')
All inputs are finite; a program needn't handle non-finite values.
Results may differ from a plain program's by a relative error of at most 0.04.
Values may be sent and summed in bfloat16 or wider, within the bound.
A program may use at most 256 MiB of HBM per device.

v0:
```python
import jax
import jax.numpy as jnp
from jax import lax
from jax.sharding import PartitionSpec as P

HEAD_DIM = 64


EPS = 1e-06


def spread_rows(value):
    return lax.all_gather(value, "row", axis=0, tiled=True)


def spread_cols(value):
    return lax.all_gather(value, "col", axis=0, tiled=True)


def total_cols(whole, product):

    def term(start, count):
        return product(whole)

    return lax.psum_scatter(
        term(jnp.int32(0), lax.axis_size("col") * (whole.shape[0] // lax.axis_size("col"))).astype(
            jnp.bfloat16
        ),
        "col",
        scatter_dimension=0,
        tiled=True,
    ).astype(jnp.float32)


def total_rows(whole, product):

    def term(start, count):
        return product(whole)

    return lax.psum_scatter(
        term(jnp.int32(0), lax.axis_size("row") * (whole.shape[0] // lax.axis_size("row"))).astype(
            jnp.bfloat16
        ),
        "row",
        scatter_dimension=0,
        tiled=True,
    ).astype(jnp.float32)


def times_weight(weight):
    return lambda piece: jnp.dot(piece, weight, preferred_element_type=jnp.float32)


def times_transpose(weight):
    return lambda piece: lax.dot_general(
        piece, weight, (((1,), (1,)), ((), ())), preferred_element_type=jnp.float32
    )


def inner_rows(left, right):
    return lax.dot_general(
        left, right, (((0,), (0,)), ((), ())), preferred_element_type=jnp.float32
    )


def norm_stats(resid, gain, shift):
    width = resid.shape[1] * lax.axis_size("col")
    first, second = lax.psum((jnp.sum(resid, axis=1), jnp.sum(resid * resid, axis=1)), "col")
    mean = first[:, None] / width
    factor = lax.rsqrt(second[:, None] / width - mean * mean + EPS)
    normal = (resid - mean) * factor
    return (normal, factor, normal * gain + shift)


def norm_back(grad, normal, factor, gain):
    width = grad.shape[1] * lax.axis_size("col")
    scaled = grad * gain
    first, second = lax.psum((jnp.sum(scaled, axis=1), jnp.sum(scaled * normal, axis=1)), "col")
    return factor * (scaled - first[:, None] / width - normal * second[:, None] / width)


def head_norm(values, gain):
    heads = values.shape[1] // gain.shape[0]
    split = values.reshape(values.shape[0], heads, gain.shape[0])
    mean = jnp.mean(split, axis=-1, keepdims=True)
    centred = split - mean
    spread = jnp.mean(centred * centred, axis=-1, keepdims=True)
    return (centred * lax.rsqrt(spread + EPS) * gain).reshape(values.shape)


def attend(queries, keys, values, heads):
    rows = queries.shape[0]
    block = min(512, rows)
    factor = HEAD_DIM ** (-0.5)
    key_heads = keys.reshape(keys.shape[0], heads, HEAD_DIM)
    value_heads = values.reshape(values.shape[0], heads, HEAD_DIM)
    query_blocks = queries.reshape(rows // block, block, heads, HEAD_DIM)

    def one_block(query_block):
        scores = (
            jnp.einsum("qhd,khd->hqk", query_block, key_heads, preferred_element_type=jnp.float32)
            * factor
        )
        top = jnp.max(scores, axis=-1, keepdims=True)
        expo = jnp.exp(scores - top)
        total = jnp.sum(expo, axis=-1, keepdims=True)
        probs = (expo / total).astype(jnp.bfloat16)
        mixed = jnp.einsum("hqk,khd->qhd", probs, value_heads, preferred_element_type=jnp.float32)
        return (mixed, (top + jnp.log(total))[:, :, 0])

    mixed, log_total = lax.map(one_block, query_blocks)
    return (mixed.reshape(rows, heads * HEAD_DIM), log_total)


def attend_back(queries, keys, values, log_total, grad_mixed, heads):
    rows = queries.shape[0]
    block = min(512, rows)
    factor = HEAD_DIM ** (-0.5)
    key_heads = keys.reshape(keys.shape[0], heads, HEAD_DIM)
    value_heads = values.reshape(values.shape[0], heads, HEAD_DIM)
    query_blocks = queries.reshape(rows // block, block, heads, HEAD_DIM)
    grad_blocks = grad_mixed.reshape(rows // block, block, heads, HEAD_DIM)

    def step(carry, inputs):
        key_sum, value_sum = carry
        query_block, grad_block, totals = inputs
        scores = (
            jnp.einsum("qhd,khd->hqk", query_block, key_heads, preferred_element_type=jnp.float32)
            * factor
        )
        probs = jnp.exp(scores - totals[:, :, None])
        value_dots = jnp.einsum(
            "qhd,khd->hqk", grad_block, value_heads, preferred_element_type=jnp.float32
        )
        score_grad = (
            probs * (value_dots - jnp.sum(probs * value_dots, axis=-1, keepdims=True))
        ).astype(jnp.bfloat16)
        query_part = (
            jnp.einsum("hqk,khd->qhd", score_grad, key_heads, preferred_element_type=jnp.float32)
            * factor
        )
        key_sum = (
            key_sum
            + jnp.einsum(
                "hqk,qhd->khd", score_grad, query_block, preferred_element_type=jnp.float32
            )
            * factor
        )
        value_sum = value_sum + jnp.einsum(
            "hqk,qhd->khd",
            probs.astype(jnp.bfloat16),
            grad_block,
            preferred_element_type=jnp.float32,
        )
        return ((key_sum, value_sum), query_part)

    zeros = jnp.zeros(key_heads.shape, jnp.float32)
    (key_sum, value_sum), query_parts = lax.scan(
        step, (zeros, zeros), (query_blocks, grad_blocks, log_total)
    )
    return (
        query_parts.reshape(rows, heads * HEAD_DIM),
        key_sum.reshape(keys.shape[0], heads * HEAD_DIM),
        value_sum.reshape(values.shape[0], heads * HEAD_DIM),
    )


def layer_forward(resid, weights):
    (
        gain_one,
        shift_one,
        w_query,
        w_key,
        w_value,
        query_gain,
        key_gain,
        w_out,
        gain_two,
        shift_two,
        w_up,
        up_bias,
        w_down,
        down_bias,
    ) = weights
    width = w_query.shape[1]
    heads = width // HEAD_DIM
    joined = jnp.concatenate((w_query, w_key, w_value), axis=1)
    normal_one, factor_one, normed_one = norm_stats(resid, gain_one, shift_one)
    seen_one = spread_rows(normed_one.astype(jnp.bfloat16))
    projected = total_cols(seen_one, times_weight(joined))
    query_raw = projected[:, :width]
    key_raw = projected[:, width : 2 * width]
    value_raw = projected[:, 2 * width :]
    query_low = head_norm(query_raw, query_gain).astype(jnp.bfloat16)
    key_low = head_norm(key_raw, key_gain).astype(jnp.bfloat16)
    keys, values = (
        lax.all_gather(key_low, "col", axis=0, tiled=True),
        lax.all_gather(value_raw.astype(jnp.bfloat16), "col", axis=0, tiled=True),
    )
    mixed, log_total = attend(query_low, keys, values, heads)
    seen_mixed = spread_cols(mixed.astype(jnp.bfloat16))
    resid_two = resid + total_rows(seen_mixed, times_weight(w_out))
    normal_two, factor_two, normed_two = norm_stats(resid_two, gain_two, shift_two)
    seen_two = spread_rows(normed_two.astype(jnp.bfloat16))
    hidden = total_cols(seen_two, times_weight(w_up)) + up_bias
    active = jax.nn.gelu(hidden, approximate=True).astype(jnp.bfloat16)
    seen_active = spread_cols(active)
    result = resid_two + (total_rows(seen_active, times_weight(w_down)) + down_bias)
    cache = (
        normal_one,
        factor_one,
        seen_one,
        query_raw,
        key_raw,
        query_low,
        keys,
        values,
        log_total,
        seen_mixed,
        normal_two,
        factor_two,
        seen_two,
        hidden,
        seen_active,
    )
    return (result, cache)


def layer_backward(grad, cache, weights):
    (
        gain_one,
        shift_one,
        w_query,
        w_key,
        w_value,
        query_gain,
        key_gain,
        w_out,
        gain_two,
        shift_two,
        w_up,
        up_bias,
        w_down,
        down_bias,
    ) = weights
    (
        normal_one,
        factor_one,
        seen_one,
        query_raw,
        key_raw,
        query_low,
        keys,
        values,
        log_total,
        seen_mixed,
        normal_two,
        factor_two,
        seen_two,
        hidden,
        seen_active,
    ) = cache
    width = w_query.shape[1]
    heads = width // HEAD_DIM
    joined = jnp.concatenate((w_query, w_key, w_value), axis=1)
    branch_low = grad.astype(jnp.bfloat16)
    bias_down = jnp.sum(branch_low.astype(jnp.float32), axis=0)
    seen_branch = spread_rows(branch_low)
    grad_down = inner_rows(seen_active, seen_branch)
    active_grad = total_cols(seen_branch, times_transpose(w_down))
    gelu_pull = jax.vjp(lambda inner: jax.nn.gelu(inner, approximate=True), hidden)[1]
    hidden_low = gelu_pull(active_grad)[0].astype(jnp.bfloat16)
    bias_up = jnp.sum(hidden_low.astype(jnp.float32), axis=0)
    seen_hidden = spread_cols(hidden_low)
    grad_up = inner_rows(seen_two, seen_hidden)
    normed_two_grad = total_rows(seen_hidden, times_transpose(w_up))
    gain_two_grad = jnp.sum(normed_two_grad * normal_two, axis=0)
    shift_two_grad = jnp.sum(normed_two_grad, axis=0)
    resid_two_grad = grad + norm_back(normed_two_grad, normal_two, factor_two, gain_two)
    proj_low = resid_two_grad.astype(jnp.bfloat16)
    seen_proj = spread_rows(proj_low)
    grad_out = inner_rows(seen_mixed, seen_proj)
    mixed_grad = total_cols(seen_proj, times_transpose(w_out)).astype(jnp.bfloat16)
    query_norm_grad, key_part, value_part = attend_back(
        query_low, keys, values, log_total, mixed_grad, heads
    )
    key_norm_grad, value_grad = (
        lax.psum_scatter(
            key_part.astype(jnp.bfloat16), "col", scatter_dimension=0, tiled=True
        ).astype(jnp.float32),
        lax.psum_scatter(
            value_part.astype(jnp.bfloat16), "col", scatter_dimension=0, tiled=True
        ).astype(jnp.float32),
    )
    query_grad, query_gain_grad = jax.vjp(head_norm, query_raw, query_gain)[1](query_norm_grad)
    key_grad, key_gain_grad = jax.vjp(head_norm, key_raw, key_gain)[1](key_norm_grad)
    joined_low = jnp.concatenate((query_grad, key_grad, value_grad), axis=1).astype(jnp.bfloat16)
    seen_joined = spread_cols(joined_low)
    grad_joined = inner_rows(seen_one, seen_joined)
    normed_one_grad = total_rows(seen_joined, times_transpose(joined))
    gain_one_grad = jnp.sum(normed_one_grad * normal_one, axis=0)
    shift_one_grad = jnp.sum(normed_one_grad, axis=0)
    resid_grad = resid_two_grad + norm_back(normed_one_grad, normal_one, factor_one, gain_one)
    grads = (
        gain_one_grad,
        shift_one_grad,
        grad_joined[:, :width],
        grad_joined[:, width : 2 * width],
        grad_joined[:, 2 * width :],
        query_gain_grad,
        key_gain_grad,
        grad_out,
        gain_two_grad,
        shift_two_grad,
        grad_up,
        bias_up,
        grad_down,
        bias_down,
    )
    return (resid_grad, grads)


def settle(grads):
    (
        gain_one,
        shift_one,
        grad_query,
        grad_key,
        grad_value,
        query_gain,
        key_gain,
        grad_out,
        gain_two,
        shift_two,
        grad_up,
        bias_up,
        grad_down,
        bias_down,
    ) = grads
    col_at = lax.axis_index("col")
    row_at = lax.axis_index("row")
    narrow = gain_one.shape[-1]
    slender = bias_up.shape[-1]
    by_col = jnp.stack((gain_one, shift_one, gain_two, shift_two, bias_down))
    by_col = lax.dynamic_update_slice_in_dim(
        jnp.zeros(by_col.shape[:-1] + (narrow * lax.axis_size("col"),), jnp.float32),
        by_col,
        col_at * narrow,
        2,
    )
    by_row = lax.dynamic_update_slice_in_dim(
        jnp.zeros(bias_up.shape[:-1] + (slender * lax.axis_size("row"),), jnp.float32),
        bias_up,
        row_at * slender,
        1,
    )
    shared = jnp.stack((query_gain, key_gain))
    by_col, by_row, shared = (
        lax.psum(by_col.astype(jnp.bfloat16), ("row", "col")).astype(jnp.float32),
        lax.psum(by_row.astype(jnp.bfloat16), ("row", "col")).astype(jnp.float32),
        lax.psum(shared.astype(jnp.bfloat16), ("row", "col")).astype(jnp.float32),
    )
    by_col = lax.dynamic_slice_in_dim(by_col, col_at * narrow, narrow, 2)
    by_row = lax.dynamic_slice_in_dim(by_row, row_at * slender, slender, 1)
    grad_query, grad_key, grad_value, grad_out, grad_up, grad_down, by_col, by_row, shared = (
        lax.psum(grad_query.astype(jnp.bfloat16), "dp").astype(jnp.float32),
        lax.psum(grad_key.astype(jnp.bfloat16), "dp").astype(jnp.float32),
        lax.psum(grad_value.astype(jnp.bfloat16), "dp").astype(jnp.float32),
        lax.psum(grad_out.astype(jnp.bfloat16), "dp").astype(jnp.float32),
        lax.psum(grad_up.astype(jnp.bfloat16), "dp").astype(jnp.float32),
        lax.psum(grad_down.astype(jnp.bfloat16), "dp").astype(jnp.float32),
        lax.psum(by_col.astype(jnp.bfloat16), "dp").astype(jnp.float32),
        lax.psum(by_row.astype(jnp.bfloat16), "dp").astype(jnp.float32),
        lax.psum(shared.astype(jnp.bfloat16), "dp").astype(jnp.float32),
    )
    return (
        by_col[0],
        by_col[1],
        grad_query,
        grad_key,
        grad_value,
        shared[0],
        shared[1],
        grad_out,
        by_col[2],
        by_col[3],
        grad_up,
        by_row,
        grad_down,
        by_col[4],
    )


def shards(
    tokens,
    ln1_gain,
    ln1_shift,
    w_query,
    w_key,
    w_value,
    query_gain,
    key_gain,
    w_out,
    ln2_gain,
    ln2_shift,
    w_up,
    up_bias,
    w_down,
    down_bias,
    cotangent,
):
    params = (
        ln1_gain,
        ln1_shift,
        w_query,
        w_key,
        w_value,
        query_gain,
        key_gain,
        w_out,
        ln2_gain,
        ln2_shift,
        w_up,
        up_bias,
        w_down,
        down_bias,
    )
    layers = w_query.shape[0]
    resid = tokens.astype(jnp.float32)
    inputs = []
    caches = []
    for layer_at in range(layers):
        inputs.append(resid)
        resid, cache = layer_forward(resid, tuple((item[layer_at] for item in params)))
        caches.append(cache)
    result = resid.astype(jnp.bfloat16)
    grad = cotangent.astype(jnp.float32)
    per_layer = [None] * layers
    for layer_at in reversed(range(layers)):
        weights = tuple((item[layer_at] for item in params))
        cache = layer_forward(inputs[layer_at], weights)[1]
        grad, grads = layer_backward(grad, cache, weights)
        per_layer[layer_at] = grads
    stacked = tuple(
        (jnp.stack([per_layer[layer_at][slot] for layer_at in range(layers)]) for slot in range(14))
    )
    stacked = settle(stacked)
    return (
        result,
        grad,
        stacked[0],
        stacked[1],
        stacked[2],
        stacked[3],
        stacked[4],
        stacked[5],
        stacked[6],
        stacked[7],
        stacked[8],
        stacked[9],
        stacked[10],
        stacked[11],
        stacked[12],
        stacked[13],
    )


def solution(mesh):
    in_specs = (
        P(("dp", "row"), "col"),
        P(None, "col"),
        P(None, "col"),
        P(None, "col", "row"),
        P(None, "col", "row"),
        P(None, "col", "row"),
        P(),
        P(),
        P(None, "row", "col"),
        P(None, "col"),
        P(None, "col"),
        P(None, "col", "row"),
        P(None, "row"),
        P(None, "row", "col"),
        P(None, "col"),
        P(("dp", "row"), "col"),
    )
    out_specs = (
        P(("dp", "row"), "col"),
        P(("dp", "row"), "col"),
        P(None, "col"),
        P(None, "col"),
        P(None, "col", "row"),
        P(None, "col", "row"),
        P(None, "col", "row"),
        P(),
        P(),
        P(None, "row", "col"),
        P(None, "col"),
        P(None, "col"),
        P(None, "col", "row"),
        P(None, "row"),
        P(None, "row", "col"),
        P(None, "col"),
    )
    return jax.shard_map(shards, mesh=mesh, in_specs=in_specs, out_specs=out_specs, check_vma=False)
```

profile of v0, /device:TPU:1, one launch (start us, length us, event | category | flops | bytes accessed | tf_op | source)
XLA Modules:
  0.0 1397.2 jit_solution(17875070907239235870)
XLA Ops:
  15.6 11.1 all_gather.72
  36.6 38.9 %reduce-scatter.21.cloned.1.call-done = bf16[512,1152]{1,0:T(8,128)(2,1)} async-done(((bf16[1024,1152]{1,0:T(8,128)(2,1)}), bf16[512,1152]{1,0:T(8,128)(2,1)}) %reduce-scatter.21.cloned.1.call-update) | async-done | bytes 1179664 | tf_op jit(solution)/shard_map/reduce_scatter | solution.py:25
  76.6 10.7 all_gather.73
  106.2 9.7 all_gather.74
  126.6 8.9 all_gather.75
  138.7 24.6 %reduce-scatter.23.cloned.1.call-done = bf16[512,384]{1,0:T(8,128)(2,1)} async-done(((bf16[1024,384]{1,0:T(8,128)(2,1)}), bf16[512,384]{1,0:T(8,128)(2,1)}) %reduce-scatter.23.cloned.1.call-update) | async-done | bytes 393232 | tf_op jit(solution)/shard_map/reduce_scatter | solution.py:40
  170.2 11.1 all_gather.76
  187.1 46.2 %reduce-scatter.25.cloned.1.call-done = bf16[512,1536]{1,0:T(8,128)(2,1)} async-done(((bf16[1024,1536]{1,0:T(8,128)(2,1)}), bf16[512,1536]{1,0:T(8,128)(2,1)}) %reduce-scatter.25.cloned.1.call-update) | async-done | bytes 1572880 | tf_op jit(solution)/shard_map/reduce_scatter | solution.py:25
  237.1 48.5 %all-gather.7.cloned.1.call-done = bf16[1024,1536]{1,0:T(8,128)(2,1)} async-done(((bf16[512,1536]{1,0:T(8,128)(2,1)}), bf16[1024,1536]{1,0:T(8,128)(2,1)}) %all-gather.7.cloned.1.call-update) | async-done | bytes 3145744 | tf_op jit(solution)/shard_map/all_gather | solution.py:17
  291.2 22.0 %reduce-scatter.27.cloned.1.call-done = bf16[512,384]{1,0:T(8,128)(2,1)} async-done(((bf16[1024,384]{1,0:T(8,128)(2,1)}), bf16[512,384]{1,0:T(8,128)(2,1)}) %reduce-scatter.27.cloned.1.call-update) | async-done | bytes 393232 | tf_op jit(solution)/shard_map/reduce_scatter | solution.py:40
  318.5 11.0 all_gather.78
  333.8 37.5 %reduce-scatter.29.cloned.1.call-done = bf16[512,1152]{1,0:T(8,128)(2,1)} async-done(((bf16[1024,1152]{1,0:T(8,128)(2,1)}), bf16[512,1152]{1,0:T(8,128)(2,1)}) %reduce-scatter.29.cloned.1.call-update) | async-done | bytes 1179664 | tf_op jit(solution)/shard_map/reduce_scatter | solution.py:25
  372.4 10.7 all_gather.79
  402.0 10.0 all_gather.80
  426.8 8.9 all_gather.81
  438.3 9.4 all_gather.84
  453.4 10.2 reduce-scatter.31.cloned.1.call-done
  472.1 17.7 %all_gather.82 = bf16[1024,384]{1,0:T(8,128)(2,1)S(1)} all-gather(bf16[512,384]{1,0:T(8,128)(2,1)S(1)} %add_convert_fusion.3), channel_id=1, replica_groups=mesh['dp'=32,'row'=2,'col'=2] {'row'}, dimensions={0}, use_global_device_ids=true | all-gather | bytes 1179648 | tf_op jit(solution)/shard_map/all_gather | solution.py:13
  495.5 23.8 %reduce-scatter.37.cloned.1.call-done = bf16[512,1536]{1,0:T(8,128)(2,1)} async-done(((bf16[1024,1536]{1,0:T(8,128)(2,1)}), bf16[512,1536]{1,0:T(8,128)(2,1)}) %reduce-scatter.37.cloned.1.call-update) | async-done | bytes 1572880 | tf_op jit(solution)/shard_map/reduce_scatter | solution.py:25
  519.2 49.7 %reduce-scatter.33.cloned.1.call-done = bf16[512,1536]{1,0:T(8,128)(2,1)} async-done(((bf16[1024,1536]{1,0:T(8,128)(2,1)}), bf16[512,1536]{1,0:T(8,128)(2,1)}) %reduce-scatter.33.cloned.1.call-update) | async-done | bytes 1572880 | tf_op jit(solution)/shard_map/reduce_scatter | solution.py:25
  568.9 5.9 convert_reduce_fusion
  575.6 47.8 %all-gather.11.cloned.1.call-done = bf16[1024,1536]{1,0:T(8,128)(2,1)} async-done(((bf16[512,1536]{1,0:T(8,128)(2,1)}), bf16[1024,1536]{1,0:T(8,128)(2,1)}) %all-gather.11.cloned.1.call-update) | async-done | bytes 3145744 | tf_op jit(solution)/shard_map/all_gather | solution.py:17
  628.4 45.7 %all-gather.9.cloned.1.call-done = bf16[1024,1536]{1,0:T(8,128)(2,1)} async-done(((bf16[512,1536]{1,0:T(8,128)(2,1)}), bf16[1024,1536]{1,0:T(8,128)(2,1)}) %all-gather.9.cloned.1.call-update) | async-done | bytes 3145744 | tf_op jit(solution)/shard_map/all_gather | solution.py:17
  679.5 19.9 %reduce-scatter.39.cloned.1.call-done = bf16[512,384]{1,0:T(8,128)(2,1)} async-done(((bf16[1024,384]{1,0:T(8,128)(2,1)}), bf16[512,384]{1,0:T(8,128)(2,1)}) %reduce-scatter.39.cloned.1.call-update) | async-done | bytes 393232 | tf_op jit(solution)/shard_map/reduce_scatter | solution.py:40
  707.2 16.2 %reduce-scatter.35.cloned.1.call-done = bf16[512,384]{1,0:T(8,128)(2,1)} async-done(((bf16[1024,384]{1,0:T(8,128)(2,1)}), bf16[512,384]{1,0:T(8,128)(2,1)}) %reduce-scatter.35.cloned.1.call-update) | async-done | bytes 393232 | tf_op jit(solution)/shard_map/reduce_scatter | solution.py:40
  726.8 12.3 all_gather.86
  741.6 20.3 %reduce-scatter.41.cloned.1.call-done = bf16[512,384]{1,0:T(8,128)(2,1)} async-done(((bf16[1024,384]{1,0:T(8,128)(2,1)}), bf16[512,384]{1,0:T(8,128)(2,1)}) %reduce-scatter.41.cloned.1.call-update) | async-done | bytes 393232 | tf_op jit(solution)/shard_map/reduce_scatter | solution.py:25
  763.1 11.1 multiply_reduce_fusion.1
  776.0 6.5 multiply_convert_fusion.1
  787.8 6.9 fusion.42
  816.7 14.6 %reduce-scatter.45.cloned.1.call-done = bf16[512,384]{1,0:T(8,128)(2,1)} async-done(((bf16[1024,384]{1,0:T(8,128)(2,1)}), bf16[512,384]{1,0:T(8,128)(2,1)}) %reduce-scatter.45.cloned.1.call-update) | async-done | bytes 393232 | tf_op jit(solution)/shard_map/reduce_scatter | solution.py:291
  833.6 39.6 %all-gather.13.cloned.1.call-done = bf16[1024,1152]{1,0:T(8,128)(2,1)} async-done(((bf16[512,1152]{1,0:T(8,128)(2,1)}), bf16[1024,1152]{1,0:T(8,128)(2,1)}) %all-gather.13.cloned.1.call-update) | async-done | bytes 2359312 | tf_op jit(solution)/shard_map/all_gather | solution.py:17
  877.3 22.6 %reduce-scatter.47.cloned.1.call-done = bf16[512,384]{1,0:T(8,128)(2,1)} async-done(((bf16[1024,384]{1,0:T(8,128)(2,1)}), bf16[512,384]{1,0:T(8,128)(2,1)}) %reduce-scatter.47.cloned.1.call-update) | async-done | bytes 393232 | tf_op jit(solution)/shard_map/reduce_scatter | solution.py:40
  907.7 10.9 all_gather.88
  923.1 47.5 %reduce-scatter.49.cloned.1.call-done = bf16[512,1536]{1,0:T(8,128)(2,1)} async-done(((bf16[1024,1536]{1,0:T(8,128)(2,1)}), bf16[512,1536]{1,0:T(8,128)(2,1)}) %reduce-scatter.49.cloned.1.call-update) | async-done | bytes 1572880 | tf_op jit(solution)/shard_map/reduce_scatter | solution.py:25
  975.9 48.5 %all-gather.15.cloned.1.call-done = bf16[1024,1536]{1,0:T(8,128)(2,1)} async-done(((bf16[512,1536]{1,0:T(8,128)(2,1)}), bf16[1024,1536]{1,0:T(8,128)(2,1)}) %all-gather.15.cloned.1.call-update) | async-done | bytes 3145744 | tf_op jit(solution)/shard_map/all_gather | solution.py:17
  1029.3 22.6 %reduce-scatter.51.cloned.1.call-done = bf16[512,384]{1,0:T(8,128)(2,1)} async-done(((bf16[1024,384]{1,0:T(8,128)(2,1)}), bf16[512,384]{1,0:T(8,128)(2,1)}) %reduce-scatter.51.cloned.1.call-update) | async-done | bytes 393232 | tf_op jit(solution)/shard_map/reduce_scatter | solution.py:40
  1060.1 10.9 all_gather.90
  1073.8 21.3 %reduce-scatter.53.cloned.1.call-done = bf16[512,384]{1,0:T(8,128)(2,1)} async-done(((bf16[1024,384]{1,0:T(8,128)(2,1)}), bf16[512,384]{1,0:T(8,128)(2,1)}) %reduce-scatter.53.cloned.1.call-update) | async-done | bytes 393232 | tf_op jit(solution)/shard_map/reduce_scatter | solution.py:25
  1096.4 11.5 multiply_reduce_fusion
  1108.2 6.5 multiply_convert_fusion
  1118.6 6.1 fusion.45
  1133.0 6.6 reduce-scatter.55.cloned.1.call-done
  1146.4 17.0 %reduce-scatter.57.cloned.1.call-done = bf16[512,384]{1,0:T(8,128)(2,1)} async-done(((bf16[1024,384]{1,0:T(8,128)(2,1)}), bf16[512,384]{1,0:T(8,128)(2,1)}) %reduce-scatter.57.cloned.1.call-update) | async-done | bytes 393232 | tf_op jit(solution)/shard_map/reduce_scatter | solution.py:291
  1182.6 22.7 %all-gather.17.cloned.1.call-done = bf16[1024,1152]{1,0:T(8,128)(2,1)} async-done(((bf16[512,1152]{1,0:T(8,128)(2,1)}), bf16[1024,1152]{1,0:T(8,128)(2,1)}) %all-gather.17.cloned.1.call-update) | async-done | bytes 2359312 | tf_op jit(solution)/shard_map/all_gather | solution.py:17
  1219.5 12.4 reduce-scatter.59.cloned.1.call-done
  1233.6 11.8 all-reduce.10
  1245.4 124.4 %all-reduce.8 = (bf16[5,2,384]{2,1,0:T(2,128)(2,1)S(1)}, bf16[2,2,64]{2,1,0:T(2,128)(2,1)S(1)}, bf16[2,1536]{1,0:T(2,128)(2,1)S(1)}) all-reduce(bf16[5,2,384]{2,1,0:T(2,128)(2,1)S(1)} %convert_convert_fusion, bf16[2,2,64]{2,1,0:T(2,128)(2,1)S(1)} %get-tuple-element.202, ...), channel_id=1, replica_groups=mesh['dp'=32,'row'=2,'col'=2] {'dp'}, use_global_device_ids=true, to_apply=%region_85.86 | all-reduce | flops 7168 | bytes 28672 | tf_op jit(solution)/shard_map/psum | solution.py:372
  (634 shorter events, 309.3 us)
Async XLA Ops:
  7.2 68.3 %reduce-scatter.21.cloned.1.call-start = ((), (), s32[]{:S(2)}) async-start(), calls=%async_computation.20 | async-start | bytes 3538944 | tf_op jit(solution)/shard_map/reduce_scatter | solution.py:25
  33.6 129.7 %reduce-scatter.23.cloned.1.call-start = ((), (), s32[]{:S(2)}) async-start(), calls=%async_computation.21 | async-start | bytes 1179648 | tf_op jit(solution)/shard_map/reduce_scatter | solution.py:40
  136.4 45.9 %copy-start.169 = (bf16[2,384,1536]{2,1,0:T(8,128)(2,1)S(1)}, bf16[2,384,1536]{2,1,0:T(8,128)(2,1)}, u32[]{:S(2)}) copy-start(bf16[2,384,1536]{2,1,0:T(8,128)(2,1)} %param.27) | copy-start | bytes 7077892
  138.0 95.3 %reduce-scatter.25.cloned.1.call-start = ((), (), s32[]{:S(2)}) async-start(), calls=%async_computation.22 | async-start | bytes 4718592 | tf_op jit(solution)/shard_map/reduce_scatter | solution.py:25
  138.7 47.0 %copy-start.125 = (f32[384]{0:T(512)}, f32[384]{0:T(512)S(1)}, u32[]{:S(2)}) copy-start(f32[384]{0:T(512)S(1)} %get-tuple-element.281) | copy-start | bytes 4612
  185.8 99.8 %all-gather.7.cloned.1.call-start = ((), (), s32[]{:S(2)}) async-start(), calls=%async_computation.23 | async-start | bytes 4718592 | tf_op jit(solution)/shard_map/all_gather | solution.py:17
  187.1 49.9 %copy-start.109 = (f32[1536]{0:T(1024)}, f32[1536]{0:T(1024)S(1)}, u32[]{:S(2)}) copy-start(f32[1536]{0:T(1024)S(1)} %get-tuple-element.165) | copy-start | bytes 18436
  237.0 53.5 %copy-start.160 = (f32[2,384]{1,0:T(2,128)S(1)}, f32[2,384]{1,0:T(2,128)}, u32[]{:S(2)}) copy-start(f32[2,384]{1,0:T(2,128)} %param.30) | copy-start | bytes 9220
  237.0 76.1 %copy-start.9 = (bf16[512,384]{1,0:T(8,128)(2,1)S(1)}, bf16[512,384]{1,0:T(8,128)(2,1)}, u32[]{:S(2)}) copy-start(bf16[512,384]{1,0:T(8,128)(2,1)} %reduce-scatter.23.cloned.1.call-done) | copy-start | bytes 1179652
  237.1 81.2 %copy-start.115 = (f32[384]{0:T(512)S(1)}, f32[384]{0:T(512)}, u32[]{:S(2)}) copy-start(f32[384]{0:T(512)} %get-tuple-element.278) | copy-start | bytes 4612
  237.1 81.2 %copy-start.143 = (f32[384]{0:T(512)S(1)}, f32[384]{0:T(512)}, u32[]{:S(2)}) copy-start(f32[384]{0:T(512)} %get-tuple-element.174) | copy-start | bytes 4612
  237.1 76.1 %reduce-scatter.27.cloned.1.call-start = ((), (), s32[]{:S(2)}) async-start(), calls=%async_computation.24 | async-start | bytes 1179648 | tf_op jit(solution)/shard_map/reduce_scatter | solution.py:40
  290.5 80.7 %reduce-scatter.29.cloned.1.call-start = ((), (), s32[]{:S(2)}) async-start(), calls=%async_computation.25 | async-start | bytes 3538944 | tf_op jit(solution)/shard_map/reduce_scatter | solution.py:25
  332.4 131.2 %reduce-scatter.31.cloned.1.call-start = ((), (), s32[]{:S(2)}) async-start(), calls=%async_computation.26 | async-start | bytes 1179648 | tf_op jit(solution)/shard_map/reduce_scatter | solution.py:40
  438.2 81.0 %reduce-scatter.37.cloned.1.call-start = ((), (), s32[]{:S(2)}) async-start(), calls=%async_computation.30 | async-start | bytes 4718592 | tf_op jit(solution)/shard_map/reduce_scatter | solution.py:25
  453.3 115.6 %reduce-scatter.33.cloned.1.call-start = ((), (), s32[]{:S(2)}) async-start(), calls=%async_computation.27 | async-start | bytes 4718592 | tf_op jit(solution)/shard_map/reduce_scatter | solution.py:25
  495.4 128.0 %all-gather.11.cloned.1.call-start = ((), (), s32[]{:S(2)}) async-start(), calls=%async_computation.31 | async-start | bytes 4718592 | tf_op jit(solution)/shard_map/all_gather | solution.py:17
  574.8 99.3 %all-gather.9.cloned.1.call-start = ((), (), s32[]{:S(2)}) async-start(), calls=%async_computation.28 | async-start | bytes 4718592 | tf_op jit(solution)/shard_map/all_gather | solution.py:17
  575.6 123.8 %reduce-scatter.39.cloned.1.call-start = ((), (), s32[]{:S(2)}) async-start(), calls=%async_computation.32 | async-start | bytes 1179648 | tf_op jit(solution)/shard_map/reduce_scatter | solution.py:40
  628.3 95.0 %reduce-scatter.35.cloned.1.call-start = ((), (), s32[]{:S(2)}) async-start(), calls=%async_computation.29 | async-start | bytes 1179648 | tf_op jit(solution)/shard_map/reduce_scatter | solution.py:40
  679.0 82.8 %reduce-scatter.41.cloned.1.call-start = ((), (), s32[]{:S(2)}) async-start(), calls=%async_computation.33 | async-start | bytes 1179648 | tf_op jit(solution)/shard_map/reduce_scatter | solution.py:25
  741.5 66.1 %reduce-scatter.43.cloned.1.call-start = ((), (), s32[]{:S(2)}) async-start(), calls=%async_computation.34 | async-start | bytes 1179648 | tf_op jit(solution)/shard_map/reduce_scatter | solution.py:288
  786.5 44.9 %reduce-scatter.45.cloned.1.call-start = ((), (), s32[]{:S(2)}) async-start(), calls=%async_computation.35 | async-start | bytes 1179648 | tf_op jit(solution)/shard_map/reduce_scatter | solution.py:291
  801.7 71.5 %all-gather.13.cloned.1.call-start = ((), (), s32[]{:S(2)}) async-start(), calls=%async_computation.36 | async-start | bytes 3538944 | tf_op jit(solution)/shard_map/all_gather | solution.py:17
  816.7 56.5 %copy-start.85 = (bf16[384,384]{1,0:T(8,128)(2,1)S(1)}, bf16[384,384]{1,0:T(8,128)(2,1)}, u32[]{:S(2)}) copy-start(bf16[384,384]{1,0:T(8,128)(2,1)} %get-tuple-element.241) | copy-start | bytes 884740
  816.7 56.5 %copy-start.87 = (bf16[384,384]{1,0:T(8,128)(2,1)S(1)}, bf16[384,384]{1,0:T(8,128)(2,1)}, u32[]{:S(2)}) copy-start(bf16[384,384]{1,0:T(8,128)(2,1)} %get-tuple-element.280) | copy-start | bytes 884740
  833.5 66.4 %copy-start.116 = (f32[384]{0:T(512)S(1)}, f32[384]{0:T(512)}, u32[]{:S(2)}) copy-start(f32[384]{0:T(512)} %get-tuple-element.278) | copy-start | bytes 4612
  833.5 66.4 %copy-start.118 = (f32[512]{0:T(512)S(1)}, f32[512]{0:T(512)}, u32[]{:S(2)}) copy-start(f32[512]{0:T(512)} %copy-done.117) | copy-start | bytes 6148
  833.5 66.3 %copy-start.120 = (f32[512]{0:T(512)S(1)}, f32[512]{0:T(512)}, u32[]{:S(2)}) copy-start(f32[512]{0:T(512)} %copy-done.119) | copy-start | bytes 6148
  833.5 72.1 %copy-start.43 = (f32[512,384]{1,0:T(8,128)S(1)}, f32[512,384]{1,0:T(8,128)}, u32[]{:S(2)}) copy-start(f32[512,384]{1,0:T(8,128)} %get-tuple-element.214) | copy-start | bytes 2359300
  833.5 66.3 %reduce-scatter.47.cloned.1.call-start = ((), (), s32[]{:S(2)}) async-start(), calls=%async_computation.37 | async-start | bytes 1179648 | tf_op jit(solution)/shard_map/reduce_scatter | solution.py:40
  877.2 93.4 %reduce-scatter.49.cloned.1.call-start = ((), (), s32[]{:S(2)}) async-start(), calls=%async_computation.38 | async-start | bytes 4718592 | tf_op jit(solution)/shard_map/reduce_scatter | solution.py:25
  923.0 47.5 %copy-start.26 = (bf16[512,1536]{1,0:T(8,128)(2,1)S(1)}, bf16[512,1536]{1,0:T(8,128)(2,1)}, u32[]{:S(2)}) copy-start(bf16[512,1536]{1,0:T(8,128)(2,1)} %reduce-scatter.25.cloned.1.call-done) | copy-start | bytes 4718596
  923.0 47.5 %copy-start.110 = (f32[1536]{0:T(1024)S(1)}, f32[1536]{0:T(1024)}, u32[]{:S(2)}) copy-start(f32[1536]{0:T(1024)} %copy-done.109) | copy-start | bytes 18436
  923.1 101.3 %all-gather.15.cloned.1.call-start = ((), (), s32[]{:S(2)}) async-start(), calls=%async_computation.39 | async-start | bytes 4718592 | tf_op jit(solution)/shard_map/all_gather | solution.py:17
  975.8 76.1 %copy-start.10 = (bf16[512,384]{1,0:T(8,128)(2,1)S(1)}, bf16[512,384]{1,0:T(8,128)(2,1)}, u32[]{:S(2)}) copy-start(bf16[512,384]{1,0:T(8,128)(2,1)} %reduce-scatter.23.cloned.1.call-done) | copy-start | bytes 1179652
  975.8 76.1 %copy-start.126 = (f32[384]{0:T(512)S(1)}, f32[384]{0:T(512)}, u32[]{:S(2)}) copy-start(f32[384]{0:T(512)} %copy-done.125) | copy-start | bytes 4612
  975.8 76.1 %copy-start.132 = (f32[512]{0:T(512)S(1)}, f32[512]{0:T(512)}, u32[]{:S(2)}) copy-start(f32[512]{0:T(512)} %copy-done.131) | copy-start | bytes 6148
  975.8 76.1 %copy-start.134 = (f32[512]{0:T(512)S(1)}, f32[512]{0:T(512)}, u32[]{:S(2)}) copy-start(f32[512]{0:T(512)} %copy-done.133) | copy-start | bytes 6148
  975.8 76.1 %reduce-scatter.51.cloned.1.call-start = ((), (), s32[]{:S(2)}) async-start(), calls=%async_computation.40 | async-start | bytes 1179648 | tf_op jit(solution)/shard_map/reduce_scatter | solution.py:40
  1029.3 42.7 %copy-start.72 = (bf16[2,384,384]{2,1,0:T(8,128)(2,1)S(1)}, bf16[2,384,384]{2,1,0:T(8,128)(2,1)}, u32[]{:S(2)}) copy-start(bf16[2,384,384]{2,1,0:T(8,128)(2,1)} %param.24) | copy-start | bytes 1769476
  1029.3 65.9 %reduce-scatter.53.cloned.1.call-start = ((), (), s32[]{:S(2)}) async-start(), calls=%async_computation.41 | async-start | bytes 1179648 | tf_op jit(solution)/shard_map/reduce_scatter | solution.py:25
  1073.5 66.1 %reduce-scatter.55.cloned.1.call-start = ((), (), s32[]{:S(2)}) async-start(), calls=%async_computation.42 | async-start | bytes 1179648 | tf_op jit(solution)/shard_map/reduce_scatter | solution.py:288
  1118.6 44.8 %reduce-scatter.57.cloned.1.call-start = ((), (), s32[]{:S(2)}) async-start(), calls=%async_computation.43 | async-start | bytes 1179648 | tf_op jit(solution)/shard_map/reduce_scatter | solution.py:291
  1130.9 74.4 %all-gather.17.cloned.1.call-start = ((), (), s32[]{:S(2)}) async-start(), calls=%async_computation.44 | async-start | bytes 3538944 | tf_op jit(solution)/shard_map/all_gather | solution.py:17
  1165.5 66.4 %reduce-scatter.59.cloned.1.call-start = ((), (), s32[]{:S(2)}) async-start(), calls=%async_computation.45 | async-start | bytes 1179648 | tf_op jit(solution)/shard_map/reduce_scatter | solution.py:40
  1209.3 168.6 %all-reduce.13.cloned.1.call-start = ((), (), s32[]{:S(2)}) async-start(), calls=%async_computation.46 | async-start | bytes 14155776 | tf_op jit(solution)/shard_map/psum | solution.py:366
  1218.5 157.2 %copy-start.42 = (f32[512,384]{1,0:T(8,128)S(1)}, f32[512,384]{1,0:T(8,128)}, u32[]{:S(2)}) copy-start(f32[512,384]{1,0:T(8,128)} %get-tuple-element.212) | copy-start | bytes 2359300
  (155 other events, 1137.3 us)
Sparse Core Ops, SparseCore 0:
  33.7 41.7 reduce-scatter.20
  138.2 25.1 reduce-scatter.22
  185.9 47.3 reduce-scatter.24
  237.2 48.4 all-gather.6
  290.6 22.4 reduce-scatter.26
  332.5 38.6 reduce-scatter.28
  438.3 25.1 reduce-scatter.30
  466.5 52.6 reduce-scatter.36
  522.3 46.6 reduce-scatter.32
  574.9 48.4 all-gather.10
  625.7 48.4 all-gather.8
  676.9 22.4 reduce-scatter.38
  702.4 20.8 reduce-scatter.34
  741.6 20.2 reduce-scatter.40
  786.6 20.9 reduce-scatter.42
  810.3 20.9 reduce-scatter.44
  833.6 39.5 all-gather.12
  877.3 22.4 reduce-scatter.46
  923.2 47.3 reduce-scatter.48
  975.9 48.4 all-gather.14
  1029.4 22.4 reduce-scatter.50
  1073.7 21.4 reduce-scatter.52
  1118.6 20.9 reduce-scatter.54
  1142.4 20.9 reduce-scatter.56
  1165.7 39.5 all-gather.16
  1209.4 22.4 reduce-scatter.58
  1237.2 118.4 all-reduce.12
where the time goes:
time: 1410 us; the launch traced here: 1400 us
  waiting for transfers between devices  728 us (52%)
  blocking collectives  322 us (23%)
  matrix products  130 us (9%)
  other arithmetic  110 us (8%)
  local copies, waits for them, and re-layouts  87.6 us (6%)
  between operations  17 us (1%)
    reduce_scatter x8, waiting for transfers between devices, total_cols(): lax.psum_scatter(term(jnp.int32(0), lax.axis_size('col') * (whole.shape[0...  285 us
    all_gather x6, waiting for transfers between devices, spread_cols(): return lax.all_gather(value, 'col', axis=0, tiled=True)  253 us
    reduce_scatter x8, waiting for transfers between devices, total_rows(): lax.psum_scatter(term(jnp.int32(0), lax.axis_size('row') * (whole.shape[0...  150 us
    psum x1, blocking collectives, settle(): lax.psum(by_col.astype(jnp.bfloat16), 'dp').astype(jnp.float32)  124 us
    all_gather x8, blocking collectives, spread_rows(): return lax.all_gather(value, 'row', axis=0, tiled=True)  94.5 us
    reduce_scatter x2, waiting for transfers between devices, layer_backward(): lax.psum_scatter(value_part.astype(jnp.bfloat16), 'col', scatter_dimensio...  31.6 us
    dot_general x8, matrix products, times_transpose(): lax.dot_general(piece, weight, (((1,), (1,)), ((), ())), preferred_elemen...  29.1 us
  transfers between devices with their start and end apart: 27, of which 26 were waited for; matrix products, arithmetic and copies ran while one was open for 8% of the time, Pallas kernels for 0%

commit v1 on v0

v1 whole, which is shorter than its diff:
```python
import functools

import jax
import jax.numpy as jnp
from jax import lax
from jax.experimental import pallas as pl
from jax.experimental.pallas import tpu as pltpu
from jax.sharding import Mesh, PartitionSpec as P

HEAD_DIM = 64
EPS = 1e-06
LOG2E = 1.4426950408889634
BF = jnp.bfloat16
F32 = jnp.float32
GROUP = ("core", "row", "col")
BLOCK = 256


def place(core, row, col):
    return core * 4 + row * 2 + col


SPOTS = [(c, r, q) for c in range(2) for r in range(2) for q in range(2)]
OWN_IN = [(place(c, r, q), place(r, q ^ c, q)) for c, r, q in SPOTS]
OTHER_IN = [(place(c, r, q), place(r, 1 ^ q ^ c, 1 ^ q)) for c, r, q in SPOTS]
OWN_OUT = [(b, a) for a, b in OWN_IN]
CROSS = [(0, 3), (3, 0), (1, 2), (2, 1)]


def swap_core(value):
    return lax.ppermute(value, "core", [(0, 1), (1, 0)])


def swap_col(value):
    return lax.ppermute(value, "col", [(0, 1), (1, 0)])


def swap_cross(value):
    return lax.ppermute(value, ("row", "col"), CROSS)


def flip(value, axis):
    first, second = jnp.split(value, 2, axis=axis)
    return jnp.concatenate((second, first), axis=axis)


def dot(left, right, left_axis=1, right_axis=0):
    return lax.dot_general(
        left, right, (((left_axis,), (right_axis,)), ((), ())), preferred_element_type=F32
    )


def gather_core(value):
    return jnp.concatenate((value, swap_core(value)), axis=0)


def total_group(partial):
    rows = partial.shape[0] // 2
    chip = partial[:rows] + swap_core(partial[rows:].astype(BF)).astype(F32)
    return chip + flip(swap_cross(chip.astype(BF)), 1).astype(F32)


def norm(resid, gain, shift):
    mean = jnp.mean(resid, axis=1, keepdims=True)
    centred = resid - mean
    factor = lax.rsqrt(jnp.mean(centred * centred, axis=1, keepdims=True) + EPS)
    normal = centred * factor
    return normal, factor, (normal * gain + shift).astype(BF)


def norm_back(grad, normal, factor, gain):
    scaled = grad * gain
    first = jnp.mean(scaled, axis=1, keepdims=True)
    second = jnp.mean(scaled * normal, axis=1, keepdims=True)
    return factor * (scaled - first - normal * second)


def head_norm(values):
    mean = jnp.mean(values, axis=0, keepdims=True)
    centred = values - mean
    factor = lax.rsqrt(jnp.mean(centred * centred, axis=0, keepdims=True) + EPS)
    return centred * factor, factor


def head_norm_back(grad, normal, factor, gain):
    scaled = grad * gain
    first = jnp.mean(scaled, axis=0, keepdims=True)
    second = jnp.mean(scaled * normal, axis=0, keepdims=True)
    return factor * (scaled - first - normal * second)


SCALE2 = LOG2E * HEAD_DIM ** (-0.5)


def attend_kernel(qkv_ref, gain_ref, mixed_ref, total_ref):
    gains = gain_ref[...]
    query = (head_norm(qkv_ref[0, 0])[0] * gains[:, 0:1]).astype(BF)
    key_rows = (head_norm(qkv_ref[1, 0])[0] * gains[:, 1:2]).T.astype(BF)
    value = qkv_ref[2, 0].astype(BF)
    for at in range(0, query.shape[1], BLOCK):
        expo = jnp.exp2(dot(key_rows, query[:, at : at + BLOCK]) * SCALE2)
        total = jnp.sum(expo, axis=0, keepdims=True)
        mixed = dot(value, expo.astype(BF))
        mixed_ref[0, :, at : at + BLOCK] = (mixed * (1.0 / total)).astype(BF)
        total_ref[0, :, at : at + BLOCK] = jnp.log2(total)


def attend(qkv, gains):
    heads, rows = qkv.shape[1], qkv.shape[3]
    return pl.pallas_call(
        attend_kernel,
        grid=(heads,),
        in_specs=[
            pl.BlockSpec((3, 1, HEAD_DIM, rows), lambda h: (0, h, 0, 0)),
            pl.BlockSpec((HEAD_DIM, 2), lambda h: (0, 0)),
        ],
        out_specs=[
            pl.BlockSpec((1, HEAD_DIM, rows), lambda h: (h, 0, 0)),
            pl.BlockSpec((1, 1, rows), lambda h: (h, 0, 0)),
        ],
        out_shape=[
            jax.ShapeDtypeStruct((heads, HEAD_DIM, rows), BF),
            jax.ShapeDtypeStruct((heads, 1, rows), F32),
        ],
        compiler_params=pltpu.CompilerParams(vmem_limit_bytes=40 * 2**20),
        cost_estimate=pl.CostEstimate(
            flops=16 * heads * rows * rows * HEAD_DIM,
            bytes_accessed=heads * rows * HEAD_DIM * 16,
            transcendentals=heads * rows * rows,
        ),
        name="attend",
    )(qkv, gains)


def attend_back_kernel(qkv_ref, gain_ref, total_ref, grad_ref, out_ref, gain_out_ref):
    gains = gain_ref[...]
    query_normal, query_factor = head_norm(qkv_ref[0, 0])
    key_normal, key_factor = head_norm(qkv_ref[1, 0])
    query = (query_normal * gains[:, 0:1]).astype(BF)
    key_full = key_normal * gains[:, 1:2]
    key = key_full.astype(BF)
    key_rows = key_full.T.astype(BF)
    value_rows = qkv_ref[2, 0].T.astype(BF)
    key_sum = jnp.zeros(key.shape, F32)
    value_sum = jnp.zeros(key.shape, F32)
    query_parts = []
    for at in range(0, query.shape[1], BLOCK):
        here = slice(at, at + BLOCK)
        grad = grad_ref[0, :, here]
        probs = jnp.exp2(dot(key_rows, query[:, here]) * SCALE2 - total_ref[0, :, here])
        pulled = dot(value_rows, grad)
        delta = jnp.sum(probs * pulled, axis=0, keepdims=True)
        score_grad = (probs * (pulled - delta)).astype(BF)
        query_parts.append(dot(key, score_grad))
        key_sum = key_sum + dot(query[:, here], score_grad, 1, 1)
        value_sum = value_sum + dot(grad, probs.astype(BF), 1, 1)
    scale = HEAD_DIM ** (-0.5)
    query_sum = jnp.concatenate(query_parts, axis=1) * scale
    key_sum = key_sum * scale
    out_ref[0, 0] = head_norm_back(query_sum, query_normal, query_factor, gains[:, 0:1]).astype(BF)
    out_ref[1, 0] = head_norm_back(key_sum, key_normal, key_factor, gains[:, 1:2]).astype(BF)
    out_ref[2, 0] = value_sum.astype(BF)
    gain_out_ref[0] = jnp.concatenate(
        (
            jnp.sum(query_sum * query_normal, axis=1, keepdims=True),
            jnp.sum(key_sum * key_normal, axis=1, keepdims=True),
        ),
        axis=1,
    )


def attend_back(qkv, gains, total, grad):
    heads, rows = qkv.shape[1], qkv.shape[3]
    return pl.pallas_call(
        attend_back_kernel,
        grid=(heads,),
        in_specs=[
            pl.BlockSpec((3, 1, HEAD_DIM, rows), lambda h: (0, h, 0, 0)),
            pl.BlockSpec((HEAD_DIM, 2), lambda h: (0, 0)),
            pl.BlockSpec((1, 1, rows), lambda h: (h, 0, 0)),
            pl.BlockSpec((1, HEAD_DIM, rows), lambda h: (h, 0, 0)),
        ],
        out_specs=[
            pl.BlockSpec((3, 1, HEAD_DIM, rows), lambda h: (0, h, 0, 0)),
            pl.BlockSpec((1, HEAD_DIM, 2), lambda h: (h, 0, 0)),
        ],
        out_shape=[
            jax.ShapeDtypeStruct((3, heads, HEAD_DIM, rows), BF),
            jax.ShapeDtypeStruct((heads, HEAD_DIM, 2), F32),
        ],
        compiler_params=pltpu.CompilerParams(vmem_limit_bytes=48 * 2**20),
        cost_estimate=pl.CostEstimate(
            flops=40 * heads * rows * rows * HEAD_DIM,
            bytes_accessed=heads * rows * HEAD_DIM * 24,
            transcendentals=heads * rows * rows,
        ),
        name="attend_back",
    )(qkv, gains, total, grad)


def gelu_parts(hidden):
    square = hidden * hidden
    bent = jnp.tanh(0.7978845608 * hidden * (1.0 + 0.044715 * square))
    active = 0.5 * hidden * (1.0 + bent)
    slope = 0.5 * (1.0 + bent) + 0.5 * hidden * (1.0 - bent * bent) * (
        0.7978845608 * (1.0 + 3.0 * 0.044715 * square)
    )
    return active, slope


def layer_forward(resid, weights):
    w_qkv, gains, w_out, w_up, up_bias, w_down, vectors = weights
    rows = resid.shape[0]
    normal_one, factor_one, normed_one = norm(resid, vectors[0], vectors[1])
    seen_one = gather_core(normed_one)
    qkv = dot(w_qkv, seen_one, 1, 1).reshape(3, -1, HEAD_DIM, 2 * rows)
    mixed, total = attend(qkv, gains)
    mine = mixed.reshape(-1, 2 * rows)
    chip = jnp.concatenate((mine[:, :rows], swap_core(mine[:, rows:])), axis=0)
    joined = jnp.concatenate((chip, swap_cross(chip)), axis=0)
    resid_two = resid + dot(joined, w_out, 0, 0)
    normal_two, factor_two, normed_two = norm(resid_two, vectors[2], vectors[3])
    seen_two = gather_core(normed_two)
    hidden = dot(seen_two, w_up) + up_bias
    active = gelu_parts(hidden)[0].astype(BF)
    result = (resid_two + vectors[4]) + total_group(dot(active, w_down))
    cache = (
        normal_one, factor_one, seen_one, qkv, mixed, total,
        normal_two, factor_two, seen_two, hidden, active,
    )
    return result, cache


def layer_backward(grad, cache, weights, w_out_mine):
    w_qkv, gains, w_out, w_up, up_bias, w_down, vectors = weights
    (
        normal_one, factor_one, seen_one, qkv, mixed, total,
        normal_two, factor_two, seen_two, hidden, active,
    ) = cache
    rows = grad.shape[0]
    branch = grad.astype(BF)
    seen_branch = gather_core(branch)
    active_grad = dot(seen_branch, w_down, 1, 1)
    hidden_grad = (active_grad * gelu_parts(hidden)[1]).astype(BF)
    normed_two_grad = total_group(dot(hidden_grad, w_up, 1, 1))
    grad_down = dot(active, seen_branch, 0, 0)
    grad_up = dot(hidden_grad, seen_two, 0, 0)
    bias_up = jnp.sum(hidden_grad.astype(F32), axis=0)
    bias_down = jnp.sum(branch.astype(F32), axis=0)
    gain_two = jnp.sum(normed_two_grad * normal_two, axis=0)
    shift_two = jnp.sum(normed_two_grad, axis=0)
    resid_two_grad = grad + norm_back(normed_two_grad, normal_two, factor_two, vectors[2])
    seen_proj = gather_core(resid_two_grad.astype(BF))
    mine = mixed.reshape(-1, 2 * rows)
    mixed_grad = dot(w_out_mine, seen_proj, 1, 1).astype(BF).reshape(mixed.shape)
    grad_out = dot(mine, seen_proj)
    qkv_grad, gains_grad = attend_back(qkv, gains, total, mixed_grad)
    qkv_grad = qkv_grad.reshape(-1, 2 * rows)
    normed_one_grad = total_group(dot(qkv_grad, w_qkv, 0, 0))
    grad_qkv = dot(qkv_grad, seen_one)
    gain_one = jnp.sum(normed_one_grad * normal_one, axis=0)
    shift_one = jnp.sum(normed_one_grad, axis=0)
    resid_grad = resid_two_grad + norm_back(normed_one_grad, normal_one, factor_one, vectors[0])
    gains_grad = jnp.sum(gains_grad, axis=0).T.reshape(-1)
    small = jnp.stack((gain_one, shift_one, gain_two, shift_two, bias_down))
    return resid_grad, (grad_up, grad_down, grad_qkv, grad_out, small, bias_up, gains_grad)


def reduce_grads(grads):
    grad_up, grad_down, grad_qkv, grad_out, small, bias_up, gains_grad = grads
    half = grad_up.shape[1] // 2
    gains_low = gains_grad.astype(BF)
    gains_sum = gains_low.astype(F32) + swap_cross(gains_low).astype(F32)
    shared = jnp.concatenate(
        (
            bias_up.reshape(2, half),
            jnp.pad(gains_sum, (0, half - gains_sum.shape[0]))[None],
            jnp.zeros((8, half), F32),
        ),
        axis=0,
    )
    whole = jnp.concatenate((grad_up, grad_down, grad_qkv, grad_out, small), axis=0).astype(BF)
    shared = shared.astype(BF)
    other = jnp.concatenate((whole[:, half:], shared), axis=0)
    own = jnp.concatenate((whole[:, :half], shared), axis=0)
    summed = own.astype(F32) + swap_col(other).astype(F32)
    return summed.astype(BF)


def shards(
    tokens, ln1_gain, ln1_shift, w_query, w_key, w_value, query_gain, key_gain, w_out,
    ln2_gain, ln2_shift, w_up, up_bias, w_down, down_bias, cotangent,
):
    core = lax.axis_index("core")
    layers = w_query.shape[0]
    heads_here = w_query.shape[2] // 2
    units_here = w_up.shape[2] // 2

    def take(value, size, axis):
        return lax.dynamic_slice_in_dim(value, core * size, size, axis)

    def both(own, axis):
        return jnp.concatenate((own, swap_col(own)), axis=axis)

    def arrive(value):
        return jnp.concatenate(
            (lax.ppermute(value, GROUP, OWN_IN), lax.ppermute(value, GROUP, OTHER_IN)), axis=1
        ).astype(F32)

    resid = arrive(tokens)
    vectors = both(jnp.stack((ln1_gain, ln1_shift, ln2_gain, ln2_shift, down_bias), axis=1), 2)
    up_bias_here = take(up_bias, units_here, 1)
    weights, mine_out = [], []
    for at in range(layers):
        qkv_here = jnp.concatenate(
            [take(w[at], heads_here, 1).T for w in (w_query, w_key, w_value)], axis=0
        )
        out_here = both(take(w_out[at], heads_here, 0), 1)
        out_chip = jnp.concatenate((out_here, swap_core(out_here)), axis=0)
        out_all = jnp.concatenate((out_chip, flip(swap_cross(out_chip), 1)), axis=0)
        weights.append(
            (
                both(qkv_here, 1),
                jnp.stack((query_gain[at], key_gain[at]), axis=1),
                out_all,
                both(take(w_up[at], units_here, 1), 0),
                up_bias_here[at],
                both(take(w_down[at], units_here, 0), 1),
                vectors[at],
            )
        )
        mine_out.append(out_here)
    caches = []
    for at in range(layers):
        resid, cache = layer_forward(resid, weights[at])
        caches.append(cache)
    half = resid.shape[1] // 2
    result = lax.ppermute(resid[:, :half].astype(BF), GROUP, OWN_OUT)
    grad = arrive(cotangent)
    summed = [None] * layers
    for at in reversed(range(layers)):
        grad, grads = layer_backward(grad, caches[at], weights[at], mine_out[at])
        summed[at] = lax.psum(reduce_grads(grads), ("x", "z"))
    grad_tokens = lax.ppermute(grad[:, :half].astype(BF), GROUP, OWN_OUT).astype(F32)
    total = jnp.stack(summed)
    partner = swap_core(total)
    first = jnp.where(core == 0, total, partner).astype(F32)
    second = jnp.where(core == 0, partner, total).astype(F32)
    at_up, at_down = 0, units_here
    at_qkv = 2 * units_here
    at_out = at_qkv + 3 * heads_here
    at_small = at_out + heads_here

    def pair(start, size, axis):
        return jnp.concatenate(
            (first[:, start : start + size], second[:, start : start + size]), axis=axis
        )

    grad_up = jnp.swapaxes(pair(at_up, units_here, 1), 1, 2)
    grad_down = pair(at_down, units_here, 1)
    grad_q, grad_k, grad_v = (
        jnp.swapaxes(pair(at_qkv + i * heads_here, heads_here, 1), 1, 2) for i in range(3)
    )
    grad_out = pair(at_out, heads_here, 1)
    both_small = first[:, at_small : at_small + 8] + second[:, at_small : at_small + 8]
    bias_up = pair(at_small + 5, 2, 1).reshape(layers, -1)
    return (
        result,
        grad_tokens,
        both_small[:, 0],
        both_small[:, 1],
        grad_q,
        grad_k,
        grad_v,
        both_small[:, 7, :HEAD_DIM],
        both_small[:, 7, HEAD_DIM : 2 * HEAD_DIM],
        grad_out,
        both_small[:, 2],
        both_small[:, 3],
        grad_up,
        bias_up,
        grad_down,
        both_small[:, 4],
    )


def solution(mesh):
    fine = Mesh(mesh.devices.reshape(4, 4, 2, 2, 2), ("x", "z", "core", "row", "col"))
    rows = ("x", "z", "core", "row")
    in_specs = (
        P(rows, "col"),
        P(None, "col"),
        P(None, "col"),
        P(None, "col", "row"),
        P(None, "col", "row"),
        P(None, "col", "row"),
        P(),
        P(),
        P(None, "row", "col"),
        P(None, "col"),
        P(None, "col"),
        P(None, "col", "row"),
        P(None, "row"),
        P(None, "row", "col"),
        P(None, "col"),
        P(rows, "col"),
    )
    out_specs = (P(rows, "col"),) * 2 + in_specs[1:15]
    return jax.shard_map(shards, mesh=fine, in_specs=in_specs, out_specs=out_specs, check_vma=False)
```

time: 1410 us -> 671 us (0.48)
  waiting for transfers between devices: 728 us -> 300 us
  blocking collectives: 322 us -> 0 us
  other arithmetic: 110 us -> 49.8 us
  matrix products: 130 us -> 70.6 us
  starting transfers between devices: 2.16 us -> 59.6 us
  local copies, waits for them, and re-layouts: 87.6 us -> 126 us
  Pallas kernels: 0 us -> 37.6 us
    reduce_scatter x20 -> x0, waiting for transfers between devices: 474 us -> none  [the longest x8 285 us: total_cols(): lax.psum_scatter(term(jnp.int32(0), lax.axis_size('col') * (whole.shape[0...]
    all_gather x6 -> x0, waiting for transfers between devices: 253 us -> none  [spread_cols(): return lax.all_gather(value, 'col', axis=0, tiled=True)]
    ppermute x0 -> x48, waiting for transfers between devices: none -> 207 us  [the longest x12 116 us: swap_cross(): return lax.ppermute(value, ('row', 'col'), CROSS)]
    psum x10 -> x0, blocking collectives: 169 us -> none  [the longest x1 124 us: settle(): lax.psum(by_col.astype(jnp.bfloat16), 'dp').astype(jnp.float32)]
    all_gather x14 -> x0, blocking collectives: 153 us -> none  [the longest x8 94.5 us: spread_rows(): return lax.all_gather(value, 'row', axis=0, tiled=True)]
    psum x1, waiting for transfers between devices: 0.01 us -> 93.5 us  [shards(): summed[at] = lax.psum(reduce_grads(grads), ('x', 'z'))]
    concatenate x0 -> x7, local copies, waits for them, and re-layouts: none -> 67.5 us  [the longest x2 35.4 us: reduce_grads(): jnp.concatenate((grad_up, grad_down, grad_qkv, grad_out, small), axis=0)]
    dot_general x36 -> x24, matrix products: 130 us -> 70.6 us  [dot(): lax.dot_general(left, right, (((left_axis,), (right_axis,)), ((), ())), p...]
  transfers between devices with their start and end apart: 27 -> 49, of which waited for: 26 -> 28; matrix products, arithmetic and copies ran while one was open for 8% -> 26% of each run, Pallas kernels for 0% -> 2%
where the time goes in v1:
time: 671 us; the launch traced here: 660 us
  waiting for transfers between devices  300 us (45%)
  local copies, waits for them, and re-layouts  126 us (19%)
  matrix products  70.6 us (11%)
  starting transfers between devices  59.6 us (9%)
  other arithmetic  49.8 us (7%)
  Pallas kernels  37.6 us (6%)
  between operations  15.9 us (2%)
    ppermute x12, waiting for transfers between devices, swap_cross(): return lax.ppermute(value, ('row', 'col'), CROSS)  116 us
    psum x1, waiting for transfers between devices, shards(): summed[at] = lax.psum(reduce_grads(grads), ('x', 'z'))  93.5 us
    dot_general x24, matrix products, dot(): lax.dot_general(left, right, (((left_axis,), (right_axis,)), ((), ())), p...  70.6 us
    ppermute x11, waiting for transfers between devices, swap_col(): return lax.ppermute(value, 'col', [(0, 1), (1, 0)])  66 us
    concatenate x2, local copies, waits for them, and re-layouts, reduce_grads(): jnp.concatenate((grad_up, grad_down, grad_qkv, grad_out, small), axis=0)  35.4 us
    pallas_call x2, Pallas kernels, attend_back(): pl.pallas_call(attend_back_kernel, grid=(heads,), in_specs=[pl.BlockSpec(...  25.4 us
    unnamed x241, local copies, waits for them, and re-layouts  23.2 us
    ppermute x19, starting transfers between devices, swap_core(): return lax.ppermute(value, 'core', [(0, 1), (1, 0)])  20.9 us
  transfers between devices with their start and end apart: 49, of which 28 were waited for; matrix products, arithmetic and copies ran while one was open for 26% of the time, Pallas kernels for 2%

profile of v1, /device:TPU:1, one launch (start us, length us, event | category | flops | bytes accessed | tf_op | source)
XLA Modules:
  0.0 659.8 jit_solution(6884715602326155691)
XLA Ops:
  10.0 4.2 collective-permute-start
  26.7 10.7 %collective-permute-done.7 = bf16[192,384]{1,0:T(8,128)(2,1)S(1)} collective-permute-done((bf16[192,384]{1,0:T(8,128)(2,1)S(1)}, bf16[192,384]{1,0:T(8,128)(2,1)S(1)}, u32[]{:S(2)}, u32[]{:S(2)}) %collective-permute-start.7) | collective-permute-done | bytes 147488 | tf_op jit(solution)/shard_map/ppermute | solution.py:35
  41.7 6.1 attend.2
  56.6 9.2 %collective-permute-done.9 = bf16[384,768]{1,0:T(8,128)(2,1)} collective-permute-done((bf16[384,768]{1,0:T(8,128)(2,1)}, bf16[384,768]{1,0:T(8,128)(2,1)}, u32[]{:S(2)}, u32[]{:S(2)}) %collective-permute-start.9) | collective-permute-done | bytes 589856 | tf_op jit(solution)/shard_map/ppermute | solution.py:39
  66.9 7.3 %collective-permute-done.6 = bf16[384,512]{1,0:T(8,128)(2,1)} collective-permute-done((bf16[384,512]{1,0:T(8,128)(2,1)}, bf16[384,512]{1,0:T(8,128)(2,1)}, u32[]{:S(2)}, u32[]{:S(2)}) %collective-permute-start.6) | collective-permute-done | bytes 393248 | tf_op jit(solution)/shard_map/ppermute | solution.py:39
  84.5 10.9 %collective-permute-done.12 = bf16[768,384]{1,0:T(8,128)(2,1)} collective-permute-done((bf16[768,384]{1,0:T(8,128)(2,1)}, bf16[768,384]{1,0:T(8,128)(2,1)}, u32[]{:S(2)}, u32[]{:S(2)}) %collective-permute-start.12) | collective-permute-done | bytes 589856 | tf_op jit(solution)/shard_map/ppermute | solution.py:35
  95.5 3.3 fusion.49
  104.4 18.5 %collective-permute-done.14 = bf16[512,768]{1,0:T(8,128)(2,1)S(1)} collective-permute-done((bf16[512,768]{1,0:T(8,128)(2,1)S(1)}, bf16[512,768]{1,0:T(8,128)(2,1)S(1)}, u32[]{:S(2)}, u32[]{:S(2)}) %collective-permute-start.14) | collective-permute-done | bytes 786464 | tf_op jit(solution)/shard_map/ppermute | solution.py:39
  132.7 7.8 %collective-permute-done.15 = bf16[576,384]{0,1:T(8,128)(2,1)} collective-permute-done((bf16[576,384]{0,1:T(8,128)(2,1)}, bf16[576,384]{0,1:T(8,128)(2,1)}, u32[]{:S(2)}, u32[]{:S(2)}) %collective-permute-start.15) | collective-permute-done | bytes 442400 | tf_op jit(solution)/shard_map/ppermute | solution.py:35
  140.5 3.2 fusion.24
  143.7 6.1 attend.3
  153.4 4.7 collective-permute-start.28
  158.8 5.9 collective-permute-done.18
  172.9 4.0 collective-permute-done.23
  178.3 10.0 %collective-permute-done.24 = bf16[768,384]{1,0:T(8,128)(2,1)S(1)} collective-permute-done((bf16[768,384]{1,0:T(8,128)(2,1)S(1)}, bf16[768,384]{1,0:T(8,128)(2,1)S(1)}, u32[]{:S(2)}, u32[]{:S(2)}) %collective-permute-start.24) | collective-permute-done | bytes 589856 | tf_op jit(solution)/shard_map/ppermute | solution.py:35
  192.7 3.1 collective-permute-start.31
  198.8 19.2 %collective-permute-done.32 = bf16[512,768]{1,0:T(8,128)(2,1)S(1)} collective-permute-done((bf16[512,768]{1,0:T(8,128)(2,1)S(1)}, bf16[512,768]{1,0:T(8,128)(2,1)S(1)}, u32[]{:S(2)}, u32[]{:S(2)}) %collective-permute-start.32) | collective-permute-done | bytes 786464 | tf_op jit(solution)/shard_map/ppermute | solution.py:39
  223.9 12.7 %attend_back.2 = (bf16[3,3,64,1024]{3,2,1,0:T(8,128)(2,1)S(1)}, f32[3,64,2]{2,1,0:T(8,128)S(1)}) custom-call(f32[3,3,64,1024]{3,2,1,0:T(8,128)S(1)} %bitcast.117, f32[64,2]{1,0:T(8,128)S(1)} %copy.41.gain_ref, f32[3,1,1024]{2,1,0:T(1,128)S(1)} %get-tuple-element.26.total_ref, bf16[3,64,1024]{2,1,0:T(8,128)(2,1)S(1)} %bitcast.122), custom_call_target="tpu_custom_call" | custom-call | flops 8053063680 | bytes 4718592 | tf_op jit(solution)/shard_map/attend_back/pallas_call | solution.py:174
  243.1 19.2 %collective-permute-done.35 = bf16[512,768]{1,0:T(8,128)(2,1)S(1)} collective-permute-done((bf16[512,768]{1,0:T(8,128)(2,1)S(1)}, bf16[512,768]{1,0:T(8,128)(2,1)S(1)}, u32[]{:S(2)}, u32[]{:S(2)}) %collective-permute-start.35) | collective-permute-done | bytes 786464 | tf_op jit(solution)/shard_map/ppermute | solution.py:39
  268.2 4.3 fusion.130
  272.5 3.2 fusion.50
  281.7 5.4 convolution_convert_fusion
  287.1 12.8 %collective-permute-done.38 = bf16[512,768]{1,0:T(8,128)(2,1)} collective-permute-done((bf16[512,768]{1,0:T(8,128)(2,1)}, bf16[512,768]{1,0:T(8,128)(2,1)}, u32[]{:S(2)}, u32[]{:S(2)}) %collective-permute-start.38) | collective-permute-done | bytes 786464 | tf_op jit(solution)/shard_map/ppermute | solution.py:39
  309.7 3.7 convolution_convert_fusion.4
  314.7 19.8 %concatenate.204 = bf16[2309,768]{1,0:T(8,128)(2,1)} concatenate(bf16[768,768]{1,0:T(8,128)(2,1)} %convolution_convert_fusion.1, bf16[768,768]{1,0:T(8,128)(2,1)} %convolution_convert_fusion, bf16[576,768]{1,0:T(8,128)(2,1)} %convolution_convert_fusion.4, bf16[192,768]{1,0:T(8,128)(2,1)} %convolution_convert_fusion.8, bf16[1,768]{1,0:T(2,128)(2,1)S(1)} %stack.87, ...), dimensions={0} | concatenate | bytes 7093248 | tf_op jit(solution)/shard_map/concatenate | solution.py:282
  336.5 12.7 %attend_back.3 = (bf16[3,3,64,1024]{3,2,1,0:T(8,128)(2,1)S(1)}, f32[3,64,2]{2,1,0:T(8,128)S(1)}) custom-call(f32[3,3,64,1024]{3,2,1,0:T(8,128)S(1)} %bitcast.115, f32[64,2]{1,0:T(8,128)S(1)} %copy.40.gain_ref, f32[3,1,1024]{2,1,0:T(1,128)S(1)} %get-tuple-element.28.total_ref, bf16[3,64,1024]{2,1,0:T(8,128)(2,1)S(1)} %bitcast.123), custom_call_target="tpu_custom_call" | custom-call | flops 8053063680 | bytes 4718592 | tf_op jit(solution)/shard_map/attend_back/pallas_call | solution.py:174
  356.6 7.0 %concatenate.206 = bf16[2320,384]{1,0:T(8,128)(2,1)} concatenate(bf16[2309,384]{1,0:T(8,128)(2,1)S(1)} %get-tuple-element.126, bf16[2,384]{1,0:T(2,128)(2,1)S(1)} %reshape.194, bf16[1,384]{1,0:T(2,128)(2,1)S(1)} %broadcast_in_dim.7, bf16[8,384]{1,0:T(8,128)(2,1)S(1)} %broadcast.155), dimensions={0} | concatenate | bytes 3563520 | tf_op jit(solution)/shard_map/concatenate | solution.py:284
  363.6 5.4 convolution_convert_fusion.2
  373.2 3.8 convolution_convert_fusion.3
  385.8 6.3 collective-permute-done.43
  393.9 4.1 fusion.97
  399.1 15.7 %concatenate.201 = bf16[2309,768]{1,0:T(8,128)(2,1)S(1)} concatenate(bf16[768,768]{1,0:T(8,128)(2,1)} %convolution_convert_fusion.3, bf16[768,768]{1,0:T(8,128)(2,1)} %convolution_convert_fusion.2, bf16[576,768]{1,0:T(8,128)(2,1)} %convolution_convert_fusion.5, bf16[192,768]{1,0:T(8,128)(2,1)} %convolution_convert_fusion.9, bf16[1,768]{1,0:T(2,128)(2,1)} %stack.81, ...), dimensions={0} | concatenate | bytes 7093248 | tf_op jit(solution)/shard_map/concatenate | solution.py:282
  416.9 10.9 %concatenate.203 = bf16[2320,384]{1,0:T(8,128)(2,1)} concatenate(bf16[2309,384]{1,0:T(8,128)(2,1)} %get-tuple-element.128, bf16[2,384]{1,0:T(2,128)(2,1)} %reshape.193, bf16[1,384]{1,0:T(2,128)(2,1)} %broadcast_in_dim.6, bf16[8,384]{1,0:T(8,128)(2,1)} %copy-done.81), dimensions={0} | concatenate | bytes 3563520 | tf_op jit(solution)/shard_map/concatenate | solution.py:284
  427.8 7.1 %concatenate.205 = bf16[2320,384]{1,0:T(8,128)(2,1)S(1)} concatenate(bf16[2309,384]{1,0:T(8,128)(2,1)} %get-tuple-element.125, bf16[2,384]{1,0:T(2,128)(2,1)S(1)} %copy-done.84, bf16[1,384]{1,0:T(2,128)(2,1)S(1)} %copy-done.86, bf16[8,384]{1,0:T(8,128)(2,1)S(1)} %copy-done.82), dimensions={0} | concatenate | bytes 3563520 | tf_op jit(solution)/shard_map/concatenate | solution.py:285
  434.9 3.2 fusion.3
  438.1 7.1 %concatenate.202 = bf16[2320,384]{1,0:T(8,128)(2,1)S(1)} concatenate(bf16[2309,384]{1,0:T(8,128)(2,1)} %get-tuple-element.127, bf16[2,384]{1,0:T(2,128)(2,1)S(1)} %copy-done.87, bf16[1,384]{1,0:T(2,128)(2,1)S(1)} %copy-done.88, bf16[8,384]{1,0:T(8,128)(2,1)S(1)} %copy-done.82), dimensions={0} | concatenate | bytes 3563520 | tf_op jit(solution)/shard_map/concatenate | solution.py:285
  445.2 22.6 %collective-permute-done.44 = bf16[2320,384]{1,0:T(8,128)(2,1)} collective-permute-done((bf16[2320,384]{1,0:T(8,128)(2,1)}, bf16[2320,384]{1,0:T(8,128)(2,1)}, u32[]{:S(2)}, u32[]{:S(2)}) %collective-permute-start.44) | collective-permute-done | bytes 1781792 | tf_op jit(solution)/shard_map/ppermute | solution.py:35
  467.7 3.1 fusion.2
  471.6 4.2 fusion.47
  478.4 93.5 %all-reduce.5.cloned.1.call-done = (bf16[1,2320,384]{2,1,0:T(8,128)(2,1)}, bf16[1,2320,384]{2,1,0:T(8,128)(2,1)}) async-done(((bf16[1,2320,384]{2,1,0:T(8,128)(2,1)}, bf16[1,2320,384]{2,1,0:T(8,128)(2,1)}), (bf16[1,2320,384]{2,1,0:T(8,128)(2,1)}, bf16[1,2320,384]{2,1,0:T(8,128)(2,1)})) %all-reduce.5.cloned.1.call-update) | async-done | bytes 3563536 | tf_op jit(solution)/shard_map/psum | solution.py:343
  581.4 17.9 %collective-permute-done.26 = bf16[512,768]{1,0:T(8,128)(2,1)S(1)} collective-permute-done((bf16[512,768]{1,0:T(8,128)(2,1)S(1)}, bf16[512,768]{1,0:T(8,128)(2,1)S(1)}, u32[]{:S(2)}, u32[]{:S(2)}) %collective-permute-start.26) | collective-permute-done | bytes 786464 | tf_op jit(solution)/shard_map/ppermute | solution.py:39
  599.6 4.2 collective-permute-start.27
  604.2 3.2 collective-permute-start.42
  610.3 4.5 collective-permute-done.42
  615.7 4.0 select_convert_fusion.1
  636.3 4.2 maximum_bitcast_fusion
  640.5 6.2 copy.49
  646.7 4.3 pad_maximum_fusion
  (467 shorter events, 173.7 us)
Async XLA Ops:
  7.2 564.7 %all-reduce.5.cloned.1.call-start = ((), (), s32[]{:S(2)}) async-start(), calls=%async_computation | async-start | bytes 7127040 | tf_op jit(solution)/shard_map/psum | solution.py:343
  7.2 16.5 %collective-permute-start.1 = (bf16[512,384]{1,0:T(8,128)(2,1)}, bf16[512,384]{1,0:T(8,128)(2,1)S(1)}, u32[]{:S(2)}, u32[]{:S(2)}) collective-permute-start(bf16[512,384]{1,0:T(8,128)(2,1)} %param.16), channel_id=1, source_target_pairs={{0,3},{1,0},{2,7},{3,4},{4,1},{5,2},{6,5},{7,6},{8,11},{9,8},{10,1... | collective-permute-start | bytes 1179656 | tf_op jit(solution)/shard_map/ppermute | solution.py:307
  10.0 13.8 %collective-permute-start = (bf16[512,384]{1,0:T(8,128)(2,1)}, bf16[512,384]{1,0:T(8,128)(2,1)S(1)}, u32[]{:S(2)}, u32[]{:S(2)}) collective-permute-start(bf16[512,384]{1,0:T(8,128)(2,1)} %param.16), channel_id=1, source_target_pairs={{0,0},{1,3},{2,4},{3,7},{4,2},{5,1},{6,6},{7,5},{8,8},{9,11},{10,1... | collective-permute-start | bytes 1179656 | tf_op jit(solution)/shard_map/ppermute | solution.py:307
  17.7 5.4 collective-permute-start.3
  21.6 17.0 %collective-permute-start.2 = (bf16[576,384]{0,1:T(8,128)(2,1)S(1)}, bf16[576,384]{0,1:T(8,128)(2,1)}, u32[]{:S(2)}, u32[]{:S(2)}) collective-permute-start(bf16[576,384]{0,1:T(8,128)(2,1)S(1)} %pad_maximum_fusion.43), channel_id=1, source_target_pairs={{0,1},{1,0},{2,3},{3,2},{4,5},{5,4},{6,7},{7,6},{8,9},{9,8},{10,11... | collective-permute-start | bytes 1327112 | tf_op jit(solution)/shard_map/ppermute | solution.py:35
  24.8 13.8 %collective-permute-start.4 = (bf16[512,768]{1,0:T(8,128)(2,1)S(1)}, bf16[512,768]{1,0:T(8,128)(2,1)}, u32[]{:S(2)}, u32[]{:S(2)}) collective-permute-start(bf16[512,768]{1,0:T(8,128)(2,1)S(1)} %add_convert_fusion.5), channel_id=1, source_target_pairs={{0,4},{4,0},{1,5},{5,1},{2,6},{6,2},{3,7},{7,3},{8,12},{12,8},{9,1... | collective-permute-start | bytes 2359304 | tf_op jit(solution)/shard_map/ppermute | solution.py:31
  25.9 11.4 %collective-permute-start.7 = (bf16[192,384]{1,0:T(8,128)(2,1)S(1)}, bf16[192,384]{1,0:T(8,128)(2,1)S(1)}, u32[]{:S(2)}, u32[]{:S(2)}) collective-permute-start(bf16[192,384]{1,0:T(8,128)(2,1)S(1)} %dynamic-slice_bitcast_fusion.11), channel_id=1, source_target_pairs={{0,1},{1,0},{2,3},{3,2},{4,5},{5,4},{6,7},{7,6},{8,9},{9,8},{10,11... | collective-permute-start | bytes 442376 | tf_op jit(solution)/shard_map/ppermute | solution.py:35
  37.4 11.1 %collective-permute-start.8 = (bf16[192,768]{1,0:T(8,128)(2,1)S(1)}, bf16[192,768]{1,0:T(8,128)(2,1)S(1)}, u32[]{:S(2)}, u32[]{:S(2)}) collective-permute-start(bf16[192,768]{1,0:T(8,128)(2,1)S(1)} %pad_maximum_fusion.48), channel_id=1, source_target_pairs={{0,4},{4,0},{1,5},{5,1},{2,6},{6,2},{3,7},{7,3},{8,12},{12,8},{9,1... | collective-permute-start | bytes 884744 | tf_op jit(solution)/shard_map/ppermute | solution.py:31
  47.9 2.8 collective-permute-start.5
  49.3 16.4 %collective-permute-start.9 = (bf16[384,768]{1,0:T(8,128)(2,1)}, bf16[384,768]{1,0:T(8,128)(2,1)}, u32[]{:S(2)}, u32[]{:S(2)}) collective-permute-start(bf16[384,768]{1,0:T(8,128)(2,1)} %pad_maximum_fusion.41), channel_id=1, source_target_pairs={{0,3},{3,0},{1,2},{2,1},{4,7},{7,4},{5,6},{6,5},{8,11},{11,8},{9,1... | collective-permute-start | bytes 1769480 | tf_op jit(solution)/shard_map/ppermute | solution.py:39
  51.5 22.7 %collective-permute-start.6 = (bf16[384,512]{1,0:T(8,128)(2,1)}, bf16[384,512]{1,0:T(8,128)(2,1)}, u32[]{:S(2)}, u32[]{:S(2)}) collective-permute-start(bf16[384,512]{1,0:T(8,128)(2,1)} %pad_maximum_fusion.46), channel_id=1, source_target_pairs={{0,3},{3,0},{1,2},{2,1},{4,7},{7,4},{5,6},{6,5},{8,11},{11,8},{9,1... | collective-permute-start | bytes 1179656 | tf_op jit(solution)/shard_map/ppermute | solution.py:39
  56.4 25.0 %collective-permute-start.11 = (bf16[384,768]{1,0:T(8,128)(2,1)}, bf16[384,768]{1,0:T(8,128)(2,1)}, u32[]{:S(2)}, u32[]{:S(2)}) collective-permute-start(bf16[384,768]{1,0:T(8,128)(2,1)} %dynamic-slice_bitcast_fusion.3), channel_id=1, source_target_pairs={{0,1},{1,0},{2,3},{3,2},{4,5},{5,4},{6,7},{7,6},{8,9},{9,8},{10,11... | collective-permute-start | bytes 1769480 | tf_op jit(solution)/shard_map/ppermute | solution.py:35
  77.8 3.6 collective-permute-start.10
  80.9 14.5 %collective-permute-start.12 = (bf16[768,384]{1,0:T(8,128)(2,1)}, bf16[768,384]{1,0:T(8,128)(2,1)}, u32[]{:S(2)}, u32[]{:S(2)}) collective-permute-start(bf16[768,384]{1,0:T(8,128)(2,1)} %dynamic-slice_bitcast_fusion.2), channel_id=1, source_target_pairs={{0,1},{1,0},{2,3},{3,2},{4,5},{5,4},{6,7},{7,6},{8,9},{9,8},{10,11... | collective-permute-start | bytes 1769480 | tf_op jit(solution)/shard_map/ppermute | solution.py:35
  98.9 3.7 collective-permute-start.13
  102.8 20.0 %collective-permute-start.14 = (bf16[512,768]{1,0:T(8,128)(2,1)S(1)}, bf16[512,768]{1,0:T(8,128)(2,1)S(1)}, u32[]{:S(2)}, u32[]{:S(2)}) collective-permute-start(bf16[512,768]{1,0:T(8,128)(2,1)S(1)} %fusion.27), channel_id=1, source_target_pairs={{0,3},{3,0},{1,2},{2,1},{4,7},{7,4},{5,6},{6,5},{8,11},{11,8},{9,1... | collective-permute-start | bytes 2359304 | tf_op jit(solution)/shard_map/ppermute | solution.py:39
  104.3 23.2 %collective-permute-start.19 = (bf16[192,384]{1,0:T(8,128)(2,1)S(1)}, bf16[192,384]{1,0:T(8,128)(2,1)S(1)}, u32[]{:S(2)}, u32[]{:S(2)}) collective-permute-start(bf16[192,384]{1,0:T(8,128)(2,1)S(1)} %dynamic-slice_bitcast_fusion.10), channel_id=1, source_target_pairs={{0,1},{1,0},{2,3},{3,2},{4,5},{5,4},{6,7},{7,6},{8,9},{9,8},{10,11... | collective-permute-start | bytes 442376 | tf_op jit(solution)/shard_map/ppermute | solution.py:35
  125.0 15.5 %collective-permute-start.16 = (bf16[512,768]{1,0:T(8,128)(2,1)}, bf16[512,768]{1,0:T(8,128)(2,1)}, u32[]{:S(2)}, u32[]{:S(2)}) collective-permute-start(bf16[512,768]{1,0:T(8,128)(2,1)} %add_convert_fusion.3), channel_id=1, source_target_pairs={{0,4},{4,0},{1,5},{5,1},{2,6},{6,2},{3,7},{7,3},{8,12},{12,8},{9,1... | collective-permute-start | bytes 2359304 | tf_op jit(solution)/shard_map/ppermute | solution.py:31
  127.5 13.0 %collective-permute-start.15 = (bf16[576,384]{0,1:T(8,128)(2,1)}, bf16[576,384]{0,1:T(8,128)(2,1)}, u32[]{:S(2)}, u32[]{:S(2)}) collective-permute-start(bf16[576,384]{0,1:T(8,128)(2,1)} %pad_maximum_fusion.44), channel_id=1, source_target_pairs={{0,1},{1,0},{2,3},{3,2},{4,5},{5,4},{6,7},{7,6},{8,9},{9,8},{10,11... | collective-permute-start | bytes 1327112 | tf_op jit(solution)/shard_map/ppermute | solution.py:35
  131.2 27.5 %collective-permute-start.21 = (bf16[384,768]{1,0:T(8,128)(2,1)S(1)}, bf16[384,768]{1,0:T(8,128)(2,1)S(1)}, u32[]{:S(2)}, u32[]{:S(2)}) collective-permute-start(bf16[384,768]{1,0:T(8,128)(2,1)S(1)} %pad_maximum_fusion.42), channel_id=1, source_target_pairs={{0,3},{3,0},{1,2},{2,1},{4,7},{7,4},{5,6},{6,5},{8,11},{11,8},{9,1... | collective-permute-start | bytes 1769480 | tf_op jit(solution)/shard_map/ppermute | solution.py:39
  149.8 2.1 collective-permute-start.17
  152.0 12.7 %collective-permute-start.18 = (bf16[384,512]{1,0:T(8,128)(2,1)S(1)}, bf16[384,512]{1,0:T(8,128)(2,1)S(1)}, u32[]{:S(2)}, u32[]{:S(2)}) collective-permute-start(bf16[384,512]{1,0:T(8,128)(2,1)S(1)} %pad_maximum_fusion.47), channel_id=1, source_target_pairs={{0,3},{3,0},{1,2},{2,1},{4,7},{7,4},{5,6},{6,5},{8,11},{11,8},{9,1... | collective-permute-start | bytes 1179656 | tf_op jit(solution)/shard_map/ppermute | solution.py:39
  153.4 19.1 %collective-permute-start.29 = (bf16[512,384]{1,0:T(8,128)(2,1)S(1)}, bf16[512,384]{1,0:T(8,128)(2,1)S(1)}, u32[]{:S(2)}, u32[]{:S(2)}) collective-permute-start(bf16[512,384]{1,0:T(8,128)(2,1)S(1)} %copy-done.104), channel_id=1, source_target_pairs={{0,3},{1,0},{2,7},{3,4},{4,1},{5,2},{6,5},{7,6},{8,11},{9,8},{10,1... | collective-permute-start | bytes 1179656 | tf_op jit(solution)/shard_map/ppermute | solution.py:307
  153.4 17.2 %collective-permute-start.28 = (bf16[512,384]{1,0:T(8,128)(2,1)S(1)}, bf16[512,384]{1,0:T(8,128)(2,1)S(1)}, u32[]{:S(2)}, u32[]{:S(2)}) collective-permute-start(bf16[512,384]{1,0:T(8,128)(2,1)S(1)} %copy-done.104), channel_id=1, source_target_pairs={{0,0},{1,3},{2,4},{3,7},{4,2},{5,1},{6,6},{7,5},{8,8},{9,11},{10,1... | collective-permute-start | bytes 1179656 | tf_op jit(solution)/shard_map/ppermute | solution.py:307
  158.2 18.7 %collective-permute-start.23 = (bf16[384,768]{1,0:T(8,128)(2,1)S(1)}, bf16[384,768]{1,0:T(8,128)(2,1)S(1)}, u32[]{:S(2)}, u32[]{:S(2)}) collective-permute-start(bf16[384,768]{1,0:T(8,128)(2,1)S(1)} %dynamic-slice_bitcast_fusion.1), channel_id=1, source_target_pairs={{0,1},{1,0},{2,3},{3,2},{4,5},{5,4},{6,7},{7,6},{8,9},{9,8},{10,11... | collective-permute-start | bytes 1769480 | tf_op jit(solution)/shard_map/ppermute | solution.py:35
  167.3 9.6 %collective-permute-start.22 = (bf16[512,768]{1,0:T(8,128)(2,1)S(1)}, bf16[512,768]{1,0:T(8,128)(2,1)S(1)}, u32[]{:S(2)}, u32[]{:S(2)}) collective-permute-start(bf16[512,768]{1,0:T(8,128)(2,1)S(1)} %add_convert_fusion.2), channel_id=1, source_target_pairs={{0,4},{4,0},{1,5},{5,1},{2,6},{6,2},{3,7},{7,3},{8,12},{12,8},{9,1... | collective-permute-start | bytes 2359304 | tf_op jit(solution)/shard_map/ppermute | solution.py:31
  172.6 15.7 %collective-permute-start.30 = (bf16[512,768]{1,0:T(8,128)(2,1)S(1)}, bf16[512,768]{1,0:T(8,128)(2,1)S(1)}, u32[]{:S(2)}, u32[]{:S(2)}) collective-permute-start(bf16[512,768]{1,0:T(8,128)(2,1)S(1)} %constant_dynamic-update-slice_fusion.5), channel_id=1, source_target_pairs={{0,4},{4,0},{1,5},{5,1},{2,6},{6,2},{3,7},{7,3},{8,12},{12,8},{9,1... | collective-permute-start | bytes 2359304 | tf_op jit(solution)/shard_map/ppermute | solution.py:31
  172.8 15.5 %collective-permute-start.24 = (bf16[768,384]{1,0:T(8,128)(2,1)S(1)}, bf16[768,384]{1,0:T(8,128)(2,1)S(1)}, u32[]{:S(2)}, u32[]{:S(2)}) collective-permute-start(bf16[768,384]{1,0:T(8,128)(2,1)S(1)} %dynamic-slice_bitcast_fusion), channel_id=1, source_target_pairs={{0,1},{1,0},{2,3},{3,2},{4,5},{5,4},{6,7},{7,6},{8,9},{9,8},{10,11... | collective-permute-start | bytes 1769480 | tf_op jit(solution)/shard_map/ppermute | solution.py:35
  192.7 5.1 collective-permute-start.31
  197.9 20.0 %collective-permute-start.32 = (bf16[512,768]{1,0:T(8,128)(2,1)S(1)}, bf16[512,768]{1,0:T(8,128)(2,1)S(1)}, u32[]{:S(2)}, u32[]{:S(2)}) collective-permute-start(bf16[512,768]{1,0:T(8,128)(2,1)S(1)} %fusion.28), channel_id=1, source_target_pairs={{0,3},{3,0},{1,2},{2,1},{4,7},{7,4},{5,6},{6,5},{8,11},{11,8},{9,1... | collective-permute-start | bytes 2359304 | tf_op jit(solution)/shard_map/ppermute | solution.py:39
  219.6 3.4 collective-permute-start.33
  239.7 2.4 collective-permute-start.34
  242.2 20.0 %collective-permute-start.35 = (bf16[512,768]{1,0:T(8,128)(2,1)S(1)}, bf16[512,768]{1,0:T(8,128)(2,1)S(1)}, u32[]{:S(2)}, u32[]{:S(2)}) collective-permute-start(bf16[512,768]{1,0:T(8,128)(2,1)S(1)} %fusion.29), channel_id=1, source_target_pairs={{0,3},{3,0},{1,2},{2,1},{4,7},{7,4},{5,6},{6,5},{8,11},{11,8},{9,1... | collective-permute-start | bytes 2359304 | tf_op jit(solution)/shard_map/ppermute | solution.py:39
  265.1 3.1 collective-permute-start.36
  275.9 2.6 collective-permute-start.37
  279.6 20.3 %collective-permute-start.38 = (bf16[512,768]{1,0:T(8,128)(2,1)}, bf16[512,768]{1,0:T(8,128)(2,1)}, u32[]{:S(2)}, u32[]{:S(2)}) collective-permute-start(bf16[512,768]{1,0:T(8,128)(2,1)} %fusion.30), channel_id=1, source_target_pairs={{0,3},{3,0},{1,2},{2,1},{4,7},{7,4},{5,6},{6,5},{8,11},{11,8},{9,1... | collective-permute-start | bytes 2359304 | tf_op jit(solution)/shard_map/ppermute | solution.py:39
  304.5 29.9 %collective-permute-start.39 = (bf16[512,768]{1,0:T(8,128)(2,1)}, bf16[512,768]{1,0:T(8,128)(2,1)}, u32[]{:S(2)}, u32[]{:S(2)}) collective-permute-start(bf16[512,768]{1,0:T(8,128)(2,1)} %get-tuple-element.97), channel_id=1, source_target_pairs={{0,4},{4,0},{1,5},{5,1},{2,6},{6,2},{3,7},{7,3},{8,12},{12,8},{9,1... | collective-permute-start | bytes 2359304 | tf_op jit(solution)/shard_map/ppermute | solution.py:31
  308.4 6.1 collective-permute-start.45
  353.4 15.6 %collective-permute-start.40 = (bf16[512,768]{1,0:T(8,128)(2,1)}, bf16[512,768]{1,0:T(8,128)(2,1)}, u32[]{:S(2)}, u32[]{:S(2)}) collective-permute-start(bf16[512,768]{1,0:T(8,128)(2,1)} %slice.548), channel_id=1, source_target_pairs={{0,4},{4,0},{1,5},{5,1},{2,6},{6,2},{3,7},{7,3},{8,12},{12,8},{9,1... | collective-permute-start | bytes 2359304 | tf_op jit(solution)/shard_map/ppermute | solution.py:31
  363.6 71.4 %collective-permute-start.46 = (bf16[2320,384]{1,0:T(8,128)(2,1)}, bf16[2320,384]{1,0:T(8,128)(2,1)}, u32[]{:S(2)}, u32[]{:S(2)}) collective-permute-start(bf16[2320,384]{1,0:T(8,128)(2,1)} %concatenate.206), channel_id=1, source_target_pairs={{0,1},{1,0},{2,3},{3,2},{4,5},{5,4},{6,7},{7,6},{8,9},{9,8},{10,11... | collective-permute-start | bytes 5345288 | tf_op jit(solution)/shard_map/ppermute | solution.py:35
  371.3 21.3 %collective-permute-start.41 = (bf16[512,768]{1,0:T(8,128)(2,1)}, bf16[512,768]{1,0:T(8,128)(2,1)}, u32[]{:S(2)}, u32[]{:S(2)}) collective-permute-start(bf16[512,768]{1,0:T(8,128)(2,1)} %fusion.31), channel_id=1, source_target_pairs={{0,3},{3,0},{1,2},{2,1},{4,7},{7,4},{5,6},{6,5},{8,11},{11,8},{9,1... | collective-permute-start | bytes 2359304 | tf_op jit(solution)/shard_map/ppermute | solution.py:39
  379.0 13.1 %collective-permute-start.43 = (bf16[128]{0:T(256)(128)(2,1)S(1)}, bf16[128]{0:T(256)(128)(2,1)S(1)}, u32[]{:S(2)}, u32[]{:S(2)}) collective-permute-start(bf16[128]{0:T(256)(128)(2,1)S(1)} %convert_element_type.220), channel_id=1, source_target_pairs={{0,3},{3,0},{1,2},{2,1},{4,7},{7,4},{5,6},{6,5},{8,11},{11,8},{9,1... | collective-permute-start | bytes 776 | tf_op jit(solution)/shard_map/ppermute | solution.py:39
  427.8 39.9 %collective-permute-start.44 = (bf16[2320,384]{1,0:T(8,128)(2,1)}, bf16[2320,384]{1,0:T(8,128)(2,1)}, u32[]{:S(2)}, u32[]{:S(2)}) collective-permute-start(bf16[2320,384]{1,0:T(8,128)(2,1)} %concatenate.203), channel_id=1, source_target_pairs={{0,1},{1,0},{2,3},{3,2},{4,5},{5,4},{6,7},{7,6},{8,9},{9,8},{10,11... | collective-permute-start | bytes 5345288 | tf_op jit(solution)/shard_map/ppermute | solution.py:35
  476.8 100.6 %collective-permute-start.25 = (bf16[512,768]{1,0:T(8,128)(2,1)}, bf16[512,768]{1,0:T(8,128)(2,1)}, u32[]{:S(2)}, u32[]{:S(2)}) collective-permute-start(bf16[512,768]{1,0:T(8,128)(2,1)} %slice.552), channel_id=1, source_target_pairs={{0,4},{4,0},{1,5},{5,1},{2,6},{6,2},{3,7},{7,3},{8,12},{12,8},{9,1... | collective-permute-start | bytes 2359304 | tf_op jit(solution)/shard_map/ppermute | solution.py:31
  576.3 39.4 %collective-permute-start.47 = (bf16[2,2320,384]{2,1,0:T(8,128)(2,1)}, bf16[2,2320,384]{2,1,0:T(8,128)(2,1)}, u32[]{:S(2)}, u32[]{:S(2)}) collective-permute-start(bf16[2,2320,384]{2,1,0:T(8,128)(2,1)} %constant_dynamic-update-slice_fusion.7), channel_id=1, source_target_pairs={{0,4},{4,0},{1,5},{5,1},{2,6},{6,2},{3,7},{7,3},{8,12},{12,8},{9,1... | collective-permute-start | bytes 10690568 | tf_op jit(solution)/shard_map/ppermute | solution.py:31
  578.9 20.5 %collective-permute-start.26 = (bf16[512,768]{1,0:T(8,128)(2,1)S(1)}, bf16[512,768]{1,0:T(8,128)(2,1)S(1)}, u32[]{:S(2)}, u32[]{:S(2)}) collective-permute-start(bf16[512,768]{1,0:T(8,128)(2,1)S(1)} %get-tuple-element.104), channel_id=1, source_target_pairs={{0,3},{3,0},{1,2},{2,1},{4,7},{7,4},{5,6},{6,5},{8,11},{11,8},{9,1... | collective-permute-start | bytes 2359304 | tf_op jit(solution)/shard_map/ppermute | solution.py:39
  599.6 10.7 %collective-permute-start.27 = (bf16[512,384]{1,0:T(8,128)(2,1)S(1)}, bf16[512,384]{1,0:T(8,128)(2,1)S(1)}, u32[]{:S(2)}, u32[]{:S(2)}) collective-permute-start(bf16[512,384]{1,0:T(8,128)(2,1)S(1)} %fusion.36), channel_id=1, source_target_pairs={{0,0},{3,1},{4,2},{7,3},{2,4},{1,5},{6,6},{5,7},{8,8},{11,9},{12,1... | collective-permute-start | bytes 1179656 | tf_op jit(solution)/shard_map/ppermute | solution.py:338
  604.2 10.6 %collective-permute-start.42 = (bf16[512,384]{1,0:T(8,128)(2,1)S(1)}, bf16[512,384]{1,0:T(8,128)(2,1)S(1)}, u32[]{:S(2)}, u32[]{:S(2)}) collective-permute-start(bf16[512,384]{1,0:T(8,128)(2,1)S(1)} %fusion.32), channel_id=1, source_target_pairs={{0,0},{3,1},{4,2},{7,3},{2,4},{1,5},{6,6},{5,7},{8,8},{11,9},{12,1... | collective-permute-start | bytes 1179656 | tf_op jit(solution)/shard_map/ppermute | solution.py:344
  (113 other events, 1212.7 us)
Sparse Core Ops, SparseCore 0:
  471.0 100.8 all-reduce.4

commit v2 on v1

--- a/solution.py
+++ b/solution.py
@@ -244,7 +244,7 @@
     hidden_grad = (active_grad * gelu_parts(hidden)[1]).astype(BF)
     normed_two_grad = total_group(dot(hidden_grad, w_up, 1, 1))
     grad_down = dot(active, seen_branch, 0, 0)
-    grad_up = dot(hidden_grad, seen_two, 0, 0)
+    grad_up = dot(seen_two, hidden_grad, 0, 0)
     bias_up = jnp.sum(hidden_grad.astype(F32), axis=0)
     bias_down = jnp.sum(branch.astype(F32), axis=0)
     gain_two = jnp.sum(normed_two_grad * normal_two, axis=0)
@@ -266,25 +266,287 @@
     return resid_grad, (grad_up, grad_down, grad_qkv, grad_out, small, bias_up, gains_grad)
 
 
-def reduce_grads(grads):
+def link_bits():
+    x, z = lax.axis_index("x"), lax.axis_index("z")
+    col = lax.axis_index("col")
+    return {
+        "x1": ({"x": x + 1 - 2 * (x % 2)}, ((x + 1) // 2) % 2),
+        "x2": ({"x": 3 - x}, x // 2),
+        "z1": ({"z": z + 1 - 2 * (z % 2)}, ((z + 1) // 2) % 2),
+        "z2": ({"z": 3 - z}, z // 2),
+        "col": ({"col": 1 - col}, None),
+    }
+
+
+ORDERS = (
+    ("x1", "z1", "x2", "z2", "col"),
+    ("z1", "x2", "z2", "col", "x1"),
+    ("x2", "z2", "col", "x1", "z1"),
+    ("z2", "col", "x1", "z1", "x2"),
+    ("col", "x1", "z1", "x2", "z2"),
+    ("x1", "z1", "x2", "z2", "col"),
+    ("z1", "x2", "z2", "col", "x1"),
+    ("x2", "z2", "col", "x1", "z1"),
+    ("z2", "col", "x1", "z1", "x2"),
+    ("col", "x2", "z2", "x1", "z1"),
+)
+UNIT = 256
+
+
+def plan_chunks(rows):
+    units = rows // UNIT
+    count = min(units, len(ORDERS))
+    sizes = [units // count + (1 if i < units % count else 0) for i in range(count)]
+    chunks, start = [], 0
+    for size, order in zip(sizes, ORDERS):
+        chunks.append((start, size * UNIT, order))
+        start += size * UNIT
+    return chunks
+
+
+def step_shapes(rows, order, width):
+    shapes = []
+    for link in order:
+        if link == "col":
+            width //= 2
+        else:
+            rows //= 2
+        shapes.append((rows, width))
+    return shapes
+
+
+def add_into(target, other, row, col_size):
+    rows = target.shape[0]
+    block = min(rows, 64)
+
+    @pl.loop(0, rows // block)
+    def _(at):
+        here = pl.ds(pl.multiple_of(at * block, block), block)
+        there = pl.ds(pl.multiple_of(row + at * block, 16), block)
+        target[here, :] = (
+            target[here, :].astype(F32) + other[there, :col_size].astype(F32)
+        ).astype(BF)
+
+
+def reduce_kernel(chunks, copies, *refs):
+    inputs = refs[: copies["inputs"]]
+    both = refs[copies["inputs"]]
+    scratch = list(refs[copies["inputs"] + 1 :])
+    work = scratch.pop(0)
+    load_sem, send_sem, recv_sem, gather_send, gather_recv, core_send, core_recv = scratch[-7:]
+    landing = scratch[:-7]
+    core = lax.axis_index("core")
+    links = link_bits()
+    partner = {"core": 1 - core}
+
+    loads = []
+    for at, (source, rows, cols, row, col) in enumerate(copies["list"]):
+        load = pltpu.make_async_copy(
+            inputs[source].at[pl.ds(rows[0], rows[1]), pl.ds(cols[0], cols[1])],
+            work.at[pl.ds(row, rows[1]), pl.ds(col, cols[1])],
+            load_sem.at[at],
+        )
+        load.start()
+        loads.append(load)
+    barrier = pltpu.get_barrier_semaphore()
+    for device in [links[name][0] for name in ("x1", "x2", "z1", "z2", "col")] + [partner]:
+        pl.semaphore_signal(barrier, inc=1, device_id=device, device_id_type=pl.DeviceIdType.MESH)
+    for load in loads:
+        load.wait()
+    pl.semaphore_wait(barrier, 6)
+
+    sent = []
+    state, flight = [], []
+    for at, (start, rows, order) in enumerate(chunks):
+        state.append(work.at[pl.ds(start, rows), :])
+        flight.append(None)
+    for step in range(5):
+        for at, (start, rows, order) in enumerate(chunks):
+            if step > 0:
+                copy, keep_row, width = flight[at]
+                copy.wait_recv()
+                target = landing[at * 5 + step - 1]
+                add_into(target, state[at], keep_row, width)
+                state[at] = target
+            link = order[step]
+            device, bit = links[link]
+            landed = landing[at * 5 + step]
+            size, width = landed.shape
+            if link == "col":
+                source = state[at].at[:, pl.ds(width, width)]
+                keep_row = 0
+            else:
+                keep_row = bit * size
+                source = state[at].at[pl.ds(pl.multiple_of((1 - bit) * size, size), size), :]
+            copy = pltpu.make_async_remote_copy(
+                src_ref=source,
+                dst_ref=landed,
+                send_sem=send_sem.at[at, step],
+                recv_sem=recv_sem.at[at, step],
+                device_id=device,
+                device_id_type=pl.DeviceIdType.MESH,
+            )
+            copy.start()
+            sent.append(copy)
+            flight[at] = (copy, keep_row, width)
+    region = []
+    for at, (start, rows, order) in enumerate(chunks):
+        copy, keep_row, width = flight[at]
+        copy.wait_recv()
+        target = landing[at * 5 + 4]
+        add_into(target, state[at], keep_row, width)
+        offset, size = 0, rows
+        for link in order:
+            if link != "col":
+                size //= 2
+                offset = offset + links[link][1] * size
+        both[core, pl.ds(pl.multiple_of(start + offset, 16), size), :] = target[...]
+        region.append((start + offset, size))
+    back = [[link for link in reversed(order) if link != "col"] for _, _, order in chunks]
+    waiting = [None] * len(chunks)
+
+    def settle(at):
+        copy, bit, size = waiting[at]
+        copy.wait_recv()
+        lo, _ = region[at]
+        region[at] = (lo - bit * size, 2 * size)
+
+    for step in range(4):
+        for at in range(len(chunks)):
+            if step > 0:
+                settle(at)
+            lo, size = region[at]
+            device, bit = links[back[at][step]]
+            place_here = both.at[core, pl.ds(pl.multiple_of(lo, 16), size), :]
+            copy = pltpu.make_async_remote_copy(
+                src_ref=place_here,
+                dst_ref=place_here,
+                send_sem=gather_send.at[at, step],
+                recv_sem=gather_recv.at[at, step],
+                device_id=device,
+                device_id_type=pl.DeviceIdType.MESH,
+            )
+            copy.start()
+            sent.append(copy)
+            waiting[at] = (copy, bit, size)
+    last = []
+    for at, (start, rows, order) in enumerate(chunks):
+        settle(at)
+        place_here = both.at[core, pl.ds(start, rows), :]
+        copy = pltpu.make_async_remote_copy(
+            src_ref=place_here,
+            dst_ref=place_here,
+            send_sem=core_send.at[at],
+            recv_sem=core_recv.at[at],
+            device_id=partner,
+            device_id_type=pl.DeviceIdType.MESH,
+        )
+        copy.start()
+        last.append(copy)
+    for copy in last:
+        copy.wait_recv()
+    for copy in sent + last:
+        copy.wait_send()
+
+
+def reduce_all(parts, copies, rows, collective_id):
+    width = parts[0].shape[1]
+    chunks = plan_chunks(rows)
+    landing = [
+        pltpu.VMEM(shape, BF)
+        for _, size, order in chunks
+        for shape in step_shapes(size, order, width)
+    ]
+    count = len(chunks)
+    return pl.pallas_call(
+        functools.partial(reduce_kernel, chunks, {"inputs": len(parts), "list": copies}),
+        in_specs=[pl.BlockSpec(memory_space=pl.ANY)] * len(parts),
+        out_specs=pl.BlockSpec(memory_space=pltpu.VMEM),
+        out_shape=jax.ShapeDtypeStruct((2, rows, width // 2), BF),
+        scratch_shapes=[pltpu.VMEM((rows, width), BF)]
+        + landing
+        + [
+            pltpu.SemaphoreType.DMA((len(copies),)),
+            pltpu.SemaphoreType.DMA((count, 5)),
+            pltpu.SemaphoreType.DMA((count, 5)),
+            pltpu.SemaphoreType.DMA((count, 4)),
+            pltpu.SemaphoreType.DMA((count, 4)),
+            pltpu.SemaphoreType.DMA((count,)),
+            pltpu.SemaphoreType.DMA((count,)),
+        ],
+        compiler_params=pltpu.CompilerParams(
+            collective_id=collective_id, has_side_effects=True, vmem_limit_bytes=48 * 2**20
+        ),
+        cost_estimate=pl.CostEstimate(
+            flops=rows * width * 400, bytes_accessed=rows * width * 40, transcendentals=0
+        ),
+        name="reduce_all",
+    )(*parts)
+
+
+def finish_kernel(both_ref, up_ref, down_ref, q_ref, k_ref, v_ref, out_ref, small_ref):
+    units = down_ref.shape[1] // 2
+    half = up_ref.shape[1]
+    heads = out_ref.shape[1] // 2
+    for core in range(2):
+        for part in range(units // half):
+            up_ref[0, :, pl.ds(core * units + part * half, half)] = both_ref[
+                core, 0, pl.ds(part * half, half), :
+            ].astype(F32)
+        down_ref[0, pl.ds(core * units, units), :] = both_ref[core, 0, pl.ds(units, units), :].astype(F32)
+        out_ref[0, pl.ds(core * heads, heads), :] = both_ref[
+            core, 0, pl.ds(2 * units + 3 * heads, heads), :
+        ].astype(F32)
+        small_ref[0, core] = both_ref[core, 0, pl.ds(2 * units + 4 * heads, 16), :].astype(F32)
+    for at, ref in enumerate((q_ref, k_ref, v_ref)):
+        here = pl.ds(2 * units + at * heads, heads)
+        ref[0] = jnp.concatenate((both_ref[0, 0, here, :], both_ref[1, 0, here, :]), axis=0).astype(F32).T
+
+
+def finish(both, units, heads):
+    _, layers, rows, half = both.shape
+    shapes = [(half, 2 * units), (2 * units, half)] + [(half, 2 * heads)] * 3 + [(2 * heads, half)]
+
+    def spec(shape):
+        return pl.BlockSpec((1,) + shape, lambda l: (l,) + (0,) * len(shape))
+
+    small = (2, 16, half)
+    return pl.pallas_call(
+        finish_kernel,
+        grid=(layers,),
+        in_specs=[pl.BlockSpec((2, 1, rows, half), lambda l: (0, l, 0, 0))],
+        out_specs=[spec(shape) for shape in shapes] + [spec(small)],
+        out_shape=[jax.ShapeDtypeStruct((layers,) + s, F32) for s in shapes + [small]],
+        compiler_params=pltpu.CompilerParams(vmem_limit_bytes=48 * 2**20),
+        name="finish",
+    )(both)
+
+
+def pack_grads(grads):
     grad_up, grad_down, grad_qkv, grad_out, small, bias_up, gains_grad = grads
     half = grad_up.shape[1] // 2
     gains_low = gains_grad.astype(BF)
     gains_sum = gains_low.astype(F32) + swap_cross(gains_low).astype(F32)
-    shared = jnp.concatenate(
-        (
-            bias_up.reshape(2, half),
-            jnp.pad(gains_sum, (0, half - gains_sum.shape[0]))[None],
-            jnp.zeros((8, half), F32),
-        ),
-        axis=0,
-    )
-    whole = jnp.concatenate((grad_up, grad_down, grad_qkv, grad_out, small), axis=0).astype(BF)
-    shared = shared.astype(BF)
-    other = jnp.concatenate((whole[:, half:], shared), axis=0)
-    own = jnp.concatenate((whole[:, :half], shared), axis=0)
-    summed = own.astype(F32) + swap_col(other).astype(F32)
-    return summed.astype(BF)
+    bias_rows = jnp.concatenate((bias_up.reshape(2, half),) * 2, axis=1)
+    gains_row = jnp.concatenate((jnp.pad(gains_sum, (0, half - gains_sum.shape[0])),) * 2)[None]
+    small = jnp.concatenate((small, bias_rows, gains_row, jnp.zeros((8, 2 * half), F32)), axis=0)
+    return [value.astype(BF) for value in (grad_up, grad_down, grad_qkv, grad_out, small)]
+
+
+LAYER_ROWS = 2432
+
+
+def pack_copies(first, base, units, heads, width):
+    half = width // 2
+    copies = []
+    for i in range(2):
+        for j in range(2):
+            copies.append((first, (i * half, half), (j * half, half), base + j * half, i * half))
+    row = base + units
+    for at, size in ((1, units), (2, 3 * heads), (3, heads), (4, 16)):
+        copies.append((first + at, (0, size), (0, width), row, 0))
+        row += size
+    return copies
 
 
 def shards(
@@ -337,33 +599,21 @@
     half = resid.shape[1] // 2
     result = lax.ppermute(resid[:, :half].astype(BF), GROUP, OWN_OUT)
     grad = arrive(cotangent)
-    summed = [None] * layers
+    parts, copies = [], []
     for at in reversed(range(layers)):
         grad, grads = layer_backward(grad, caches[at], weights[at], mine_out[at])
-        summed[at] = lax.psum(reduce_grads(grads), ("x", "z"))
+        if at == layers - 1:
+            grad, result = lax.optimization_barrier((grad, result))
+        copies += pack_copies(len(parts), at * LAYER_ROWS, units_here, heads_here, 2 * half)
+        parts += pack_grads(grads)
     grad_tokens = lax.ppermute(grad[:, :half].astype(BF), GROUP, OWN_OUT).astype(F32)
-    total = jnp.stack(summed)
-    partner = swap_core(total)
-    first = jnp.where(core == 0, total, partner).astype(F32)
-    second = jnp.where(core == 0, partner, total).astype(F32)
-    at_up, at_down = 0, units_here
-    at_qkv = 2 * units_here
-    at_out = at_qkv + 3 * heads_here
-    at_small = at_out + heads_here
-
-    def pair(start, size, axis):
-        return jnp.concatenate(
-            (first[:, start : start + size], second[:, start : start + size]), axis=axis
-        )
-
-    grad_up = jnp.swapaxes(pair(at_up, units_here, 1), 1, 2)
-    grad_down = pair(at_down, units_here, 1)
-    grad_q, grad_k, grad_v = (
-        jnp.swapaxes(pair(at_qkv + i * heads_here, heads_here, 1), 1, 2) for i in range(3)
+    both_cores = reduce_all(parts, copies, layers * LAYER_ROWS, 1)
+    both_cores = both_cores.reshape(2, layers, LAYER_ROWS, half)
+    grad_up, grad_down, grad_q, grad_k, grad_v, grad_out, small = finish(
+        both_cores, units_here, heads_here
     )
-    grad_out = pair(at_out, heads_here, 1)
-    both_small = first[:, at_small : at_small + 8] + second[:, at_small : at_small + 8]
-    bias_up = pair(at_small + 5, 2, 1).reshape(layers, -1)
+    both_small = small[:, 0] + small[:, 1]
+    bias_up = small[:, :, 5:7].reshape(layers, -1)
     return (
         result,
         grad_tokens,

time: 671 us -> 515 us (0.77)
  waiting for transfers between devices: 300 us -> 182 us
  Pallas kernels: 37.6 us -> 124 us
  local copies, waits for them, and re-layouts: 126 us -> 45.7 us
  other arithmetic: 49.8 us -> 32.3 us
  between operations: 15.9 us -> 2.72 us
  matrix products: 70.6 us -> 63.3 us
    psum x1 -> x0, waiting for transfers between devices: 93.5 us -> none  [shards(): summed[at] = lax.psum(reduce_grads(grads), ('x', 'z'))]
    pallas_call x0 -> x2, Pallas kernels: none -> 86.7 us  [the longest x1 78.5 us: reduce_all(): pl.pallas_call(functools.partial(reduce_kernel, chunks, {'inputs': len(pa...]
    concatenate x6 -> x2, local copies, waits for them, and re-layouts: 67.5 us -> 3.24 us  [pack_grads(): jnp.concatenate((small, bias_rows, gains_row, jnp.zeros((8, 2 * half), F3...]
    ppermute x11 -> x9, waiting for transfers between devices: 66 us -> 45.3 us  [swap_col(): return lax.ppermute(value, 'col', [(0, 1), (1, 0)])]
    slice x8 -> x1, local copies, waits for them, and re-layouts: 10.9 us -> 0.01 us  [shards(): bias_up = small[:, :, 5:7].reshape(layers, -1)]
    dot_general x24, matrix products: 70.6 us -> 63.3 us  [dot(): lax.dot_general(left, right, (((left_axis,), (right_axis,)), ((), ())), p...]
    ppermute x19 -> x18, waiting for transfers between devices: 14.2 us -> 9.49 us  [swap_core(): return lax.ppermute(value, 'core', [(0, 1), (1, 0)])]
    unnamed x241 -> x213, local copies, waits for them, and re-layouts: 23.2 us -> 19.7 us
  transfers between devices with their start and end apart: 49 -> 45, of which waited for: 28 -> 23; matrix products, arithmetic and copies ran while one was open for 26% -> 18% of each run, Pallas kernels for 2% -> 5%
where the time goes in v2:
time: 515 us; the launch traced here: 506 us
  waiting for transfers between devices  182 us (35%)
  Pallas kernels  124 us (24%)
  matrix products  63.3 us (12%)
  starting transfers between devices  55.2 us (11%)
  local copies, waits for them, and re-layouts  45.7 us (9%)
  other arithmetic  32.3 us (6%)
    ppermute x12, waiting for transfers between devices, swap_cross(): return lax.ppermute(value, ('row', 'col'), CROSS)  120 us
    pallas_call x1, Pallas kernels, reduce_all(): pl.pallas_call(functools.partial(reduce_kernel, chunks, {'inputs': len(pa...  78.5 us
    dot_general x24, matrix products, dot(): lax.dot_general(left, right, (((left_axis,), (right_axis,)), ((), ())), p...  63.3 us
    ppermute x9, waiting for transfers between devices, swap_col(): return lax.ppermute(value, 'col', [(0, 1), (1, 0)])  45.3 us
    pallas_call x2, Pallas kernels, attend_back(): pl.pallas_call(attend_back_kernel, grid=(heads,), in_specs=[pl.BlockSpec(...  25.4 us
    unnamed x213, local copies, waits for them, and re-layouts  19.7 us
    ppermute x18, starting transfers between devices, swap_core(): return lax.ppermute(value, 'core', [(0, 1), (1, 0)])  17.8 us
    ppermute x12, starting transfers between devices, swap_cross(): return lax.ppermute(value, ('row', 'col'), CROSS)  16.3 us
  transfers between devices with their start and end apart: 45, of which 23 were waited for; matrix products, arithmetic and copies ran while one was open for 18% of the time, Pallas kernels for 5%

profile of v2, /device:TPU:1, one launch (start us, length us, event | category | flops | bytes accessed | tf_op | source)
XLA Modules:
  0.0 505.5 jit_solution(14221219760728188791)
XLA Ops:
  0.7 2.8 collective-permute-start.3
  3.4 4.2 collective-permute-start.2
  18.8 12.1 %collective-permute-done.9 = bf16[192,384]{1,0:T(8,128)(2,1)S(1)} collective-permute-done((bf16[192,384]{1,0:T(8,128)(2,1)S(1)}, bf16[192,384]{1,0:T(8,128)(2,1)S(1)}, u32[]{:S(2)}, u32[]{:S(2)}) %collective-permute-start.9) | collective-permute-done | bytes 147488 | tf_op jit(solution)/shard_map/ppermute | solution.py:35
  32.2 2.8 fusion.24
  35.0 6.1 %attend.2 = (bf16[3,64,1024]{2,1,0:T(8,128)(2,1)S(1)}, f32[3,1,1024]{2,1,0:T(1,128)S(1)}) custom-call(f32[3,3,64,1024]{3,2,1,0:T(8,128)S(1)} %bitcast.102, f32[64,2]{1,0:T(8,128)S(1)} %copy.38.gain_ref), custom_call_target="tpu_custom_call" | custom-call | flops 3221225472 | bytes 3145728 | tf_op jit(solution)/shard_map/attend/pallas_call | solution.py:110
  48.7 10.2 %collective-permute-done.11 = bf16[384,768]{1,0:T(8,128)(2,1)} collective-permute-done((bf16[384,768]{1,0:T(8,128)(2,1)}, bf16[384,768]{1,0:T(8,128)(2,1)}, u32[]{:S(2)}, u32[]{:S(2)}) %collective-permute-start.11) | collective-permute-done | bytes 589856 | tf_op jit(solution)/shard_map/ppermute | solution.py:39
  60.0 7.3 %collective-permute-done.8 = bf16[384,512]{1,0:T(8,128)(2,1)} collective-permute-done((bf16[384,512]{1,0:T(8,128)(2,1)}, bf16[384,512]{1,0:T(8,128)(2,1)}, u32[]{:S(2)}, u32[]{:S(2)}) %collective-permute-start.8) | collective-permute-done | bytes 393248 | tf_op jit(solution)/shard_map/ppermute | solution.py:39
  73.9 2.9 fusion.23
  76.9 10.1 %collective-permute-done.14 = bf16[768,384]{1,0:T(8,128)(2,1)} collective-permute-done((bf16[768,384]{1,0:T(8,128)(2,1)S(1)}, bf16[768,384]{1,0:T(8,128)(2,1)}, u32[]{:S(2)}, u32[]{:S(2)}) %collective-permute-start.14) | collective-permute-done | bytes 589856 | tf_op jit(solution)/shard_map/ppermute | solution.py:35
  87.0 3.2 fusion.47
  90.2 2.3 collective-permute-start.15
  96.3 18.5 %collective-permute-done.16 = bf16[512,768]{1,0:T(8,128)(2,1)S(1)} collective-permute-done((bf16[512,768]{1,0:T(8,128)(2,1)S(1)}, bf16[512,768]{1,0:T(8,128)(2,1)S(1)}, u32[]{:S(2)}, u32[]{:S(2)}) %collective-permute-start.16) | collective-permute-done | bytes 786464 | tf_op jit(solution)/shard_map/ppermute | solution.py:39
  123.5 9.1 %collective-permute-done.17 = bf16[576,384]{0,1:T(8,128)(2,1)} collective-permute-done((bf16[576,384]{0,1:T(8,128)(2,1)}, bf16[576,384]{0,1:T(8,128)(2,1)}, u32[]{:S(2)}, u32[]{:S(2)}) %collective-permute-start.17) | collective-permute-done | bytes 442400 | tf_op jit(solution)/shard_map/ppermute | solution.py:35
  132.6 3.0 fusion.22
  135.6 6.1 %attend.3 = (bf16[3,64,1024]{2,1,0:T(8,128)(2,1)S(1)}, f32[3,1,1024]{2,1,0:T(1,128)S(1)}) custom-call(f32[3,3,64,1024]{3,2,1,0:T(8,128)S(1)} %bitcast.104, f32[64,2]{1,0:T(8,128)S(1)} %copy.41.gain_ref), custom_call_target="tpu_custom_call" | custom-call | flops 3221225472 | bytes 3145728 | tf_op jit(solution)/shard_map/attend/pallas_call | solution.py:110
  145.1 4.7 collective-permute-start
  150.3 5.9 %collective-permute-done.20 = bf16[384,512]{1,0:T(8,128)(2,1)S(1)} collective-permute-done((bf16[384,512]{1,0:T(8,128)(2,1)S(1)}, bf16[384,512]{1,0:T(8,128)(2,1)S(1)}, u32[]{:S(2)}, u32[]{:S(2)}) %collective-permute-start.20) | collective-permute-done | bytes 393248 | tf_op jit(solution)/shard_map/ppermute | solution.py:39
  157.8 2.1 collective-permute-start.26
  159.9 2.7 collective-permute-done
  164.6 4.0 collective-permute-done.27
  170.0 10.0 %collective-permute-done.25 = bf16[768,384]{1,0:T(8,128)(2,1)S(1)} collective-permute-done((bf16[768,384]{1,0:T(8,128)(2,1)S(1)}, bf16[768,384]{1,0:T(8,128)(2,1)S(1)}, u32[]{:S(2)}, u32[]{:S(2)}) %collective-permute-start.25) | collective-permute-done | bytes 589856 | tf_op jit(solution)/shard_map/ppermute | solution.py:35
  180.0 2.8 fusion.122
  185.6 3.1 collective-permute-start.28
  191.7 19.1 %collective-permute-done.29 = bf16[512,768]{1,0:T(8,128)(2,1)S(1)} collective-permute-done((bf16[512,768]{1,0:T(8,128)(2,1)S(1)}, bf16[512,768]{1,0:T(8,128)(2,1)S(1)}, u32[]{:S(2)}, u32[]{:S(2)}) %collective-permute-start.29) | collective-permute-done | bytes 786464 | tf_op jit(solution)/shard_map/ppermute | solution.py:39
  218.2 12.7 %attend_back.2 = (bf16[3,3,64,1024]{3,2,1,0:T(8,128)(2,1)S(1)}, f32[3,64,2]{2,1,0:T(8,128)S(1)}) custom-call(f32[3,3,64,1024]{3,2,1,0:T(8,128)S(1)} %bitcast.105, f32[64,2]{1,0:T(8,128)S(1)} %copy.41.gain_ref, f32[3,1,1024]{2,1,0:T(1,128)S(1)} %get-tuple-element.35.total_ref, bf16[3,64,1024]{2,1,0:T(8,128)(2,1)S(1)} %bitcast.110), custom_call_target="tpu_custom_call" | custom-call | flops 8053063680 | bytes 4718592 | tf_op jit(solution)/shard_map/attend_back/pallas_call | solution.py:174
  230.9 3.0 fusion.49
  239.0 17.4 %collective-permute-done.34 = bf16[512,768]{1,0:T(8,128)(2,1)S(1)} collective-permute-done((bf16[512,768]{1,0:T(8,128)(2,1)S(1)}, bf16[512,768]{1,0:T(8,128)(2,1)S(1)}, u32[]{:S(2)}, u32[]{:S(2)}) %collective-permute-start.34) | collective-permute-done | bytes 786464 | tf_op jit(solution)/shard_map/ppermute | solution.py:39
  258.6 18.9 %collective-permute-done.32 = bf16[512,768]{1,0:T(8,128)(2,1)S(1)} collective-permute-done((bf16[512,768]{1,0:T(8,128)(2,1)S(1)}, bf16[512,768]{1,0:T(8,128)(2,1)S(1)}, u32[]{:S(2)}, u32[]{:S(2)}) %collective-permute-start.32) | collective-permute-done | bytes 786464 | tf_op jit(solution)/shard_map/ppermute | solution.py:39
  283.4 4.7 fusion.123
  289.3 4.3 fusion.48
  297.6 2.7 fusion.28
  302.6 4.2 convolution_convert_fusion.2.refs_1_
  309.0 11.6 %collective-permute-done.38 = bf16[512,768]{1,0:T(8,128)(2,1)} collective-permute-done((bf16[512,768]{1,0:T(8,128)(2,1)}, bf16[512,768]{1,0:T(8,128)(2,1)}, u32[]{:S(2)}, u32[]{:S(2)}) %collective-permute-start.38) | collective-permute-done | bytes 786464 | tf_op jit(solution)/shard_map/ppermute | solution.py:39
  321.8 3.3 multiply_reduce_fusion
  328.5 3.4 convolution_convert_fusion.5.refs_2_
  335.0 2.2 convolution_convert_fusion.6
  337.2 12.7 %attend_back.3 = (bf16[3,3,64,1024]{3,2,1,0:T(8,128)(2,1)S(1)}, f32[3,64,2]{2,1,0:T(8,128)S(1)}) custom-call(f32[3,3,64,1024]{3,2,1,0:T(8,128)S(1)} %bitcast.103, f32[64,2]{1,0:T(8,128)S(1)} %copy.38.gain_ref, f32[3,1,1024]{2,1,0:T(1,128)S(1)} %get-tuple-element.39.total_ref, bf16[3,64,1024]{2,1,0:T(8,128)(2,1)S(1)} %bitcast.111), custom_call_target="tpu_custom_call" | custom-call | flops 8053063680 | bytes 4718592 | tf_op jit(solution)/shard_map/attend_back/pallas_call | solution.py:174
  350.0 3.0 fusion.50
  359.7 5.3 %convolution_convert_fusion.refs_6_ = bf16[768,768]{1,0:T(8,128)(2,1)} fusion(bf16[512,768]{1,0:T(8,128)(2,1)} %copy-done.91, bf16[512,768]{1,0:T(8,128)(2,1)} %copy-done.46, f32[1024,768]{1,0:T(8,128)} %copy-done.94, f32[768]{0:T(1024)} %copy-done.80), kind=kOutput, calls=%fused_computation.55 | convolution fusion | flops 1219559424 | bytes 5901312 | tf_op jit(solution)/shard_map/dot_general | solution.py:48
  372.9 2.2 collective-permute-start.41
  375.1 3.1 convolution_convert_fusion.4.refs_7_
  378.2 2.7 convolution_convert_fusion.8.refs_8_
  381.6 11.5 %collective-permute-done.41 = bf16[512,768]{1,0:T(8,128)(2,1)S(1)} collective-permute-done((bf16[512,768]{1,0:T(8,128)(2,1)S(1)}, bf16[512,768]{1,0:T(8,128)(2,1)S(1)}, u32[]{:S(2)}, u32[]{:S(2)}) %collective-permute-start.41) | collective-permute-done | bytes 786464 | tf_op jit(solution)/shard_map/ppermute | solution.py:39
  393.2 4.1 fusion.95
  405.6 78.5 %reduce_all.1 = bf16[2,4864,384]{2,1,0:T(8,128)(2,1)} custom-call(bf16[768,768]{1,0:T(8,128)(2,1)S(1)} %convolution_convert_fusion.3.refs_0_, bf16[768,768]{1,0:T(8,128)(2,1)S(1)} %convolution_convert_fusion.2.refs_1_, bf16[576,768]{1,0:T(8,128)(2,1)S(1)} %copy-done, bf16[192,768]{1,0:T(8,128)(2,1)S(1)} %copy-done.4, bf16[16,768]{1,0:T(8,128)(2,1)S(1)} %copy-done.6, ...), custom_call_target="tpu_custom_call" | custom-call | flops 1494220800 | bytes 149422080 | tf_op jit(solution)/shard_map/reduce_all/pallas_call | solution.py:461
  484.2 8.2 %finish.1 = (f32[2,384,1536]{2,1,0:T(8,128)}, f32[2,1536,384]{2,1,0:T(8,128)}, f32[2,384,384]{2,1,0:T(8,128)}, f32[2,384,384]{2,1,0:T(8,128)}, f32[2,384,384]{2,...) custom-call(bf16[2,2,2432,384]{3,2,1,0:T(8,128)(2,1)} %bitcast.112), custom_call_target="tpu_custom_call" | custom-call | tf_op jit(solution)/shard_map/finish/pallas_call | solution.py:514
  492.8 4.0 collective-permute-start.42
  501.0 2.4 collective-permute-done.42
  (416 shorter events, 121.5 us)
Async XLA Ops:
  0.7 16.0 %collective-permute-start.3 = (bf16[512,384]{1,0:T(8,128)(2,1)}, bf16[512,384]{1,0:T(8,128)(2,1)S(1)}, u32[]{:S(2)}, u32[]{:S(2)}) collective-permute-start(bf16[512,384]{1,0:T(8,128)(2,1)} %param.16), channel_id=1, source_target_pairs={{0,3},{1,0},{2,7},{3,4},{4,1},{5,2},{6,5},{7,6},{8,11},{9,8},{10,1... | collective-permute-start | bytes 1179656 | tf_op jit(solution)/shard_map/ppermute | solution.py:569
  3.4 13.2 %collective-permute-start.2 = (bf16[512,384]{1,0:T(8,128)(2,1)}, bf16[512,384]{1,0:T(8,128)(2,1)S(1)}, u32[]{:S(2)}, u32[]{:S(2)}) collective-permute-start(bf16[512,384]{1,0:T(8,128)(2,1)} %param.16), channel_id=1, source_target_pairs={{0,0},{1,3},{2,4},{3,7},{4,2},{5,1},{6,6},{7,5},{8,8},{9,11},{10,1... | collective-permute-start | bytes 1179656 | tf_op jit(solution)/shard_map/ppermute | solution.py:569
  11.1 5.4 %collective-permute-start.5 = (f32[2,5,384]{2,0,1:T(2,128)S(1)}, f32[2,5,384]{2,0,1:T(2,128)S(1)}, u32[]{:S(2)}, u32[]{:S(2)}) collective-permute-start(f32[2,5,384]{2,0,1:T(2,128)S(1)} %constant_dynamic-update-slice_fusion.2), channel_id=1, source_target_pairs={{0,1},{1,0},{2,3},{3,2},{4,5},{5,4},{6,7},{7,6},{8,9},{9,8},{10,11... | collective-permute-start | bytes 46088 | tf_op jit(solution)/shard_map/ppermute | solution.py:35
  15.1 17.1 %collective-permute-start.4 = (bf16[576,384]{0,1:T(8,128)(2,1)}, bf16[576,384]{0,1:T(8,128)(2,1)}, u32[]{:S(2)}, u32[]{:S(2)}) collective-permute-start(bf16[576,384]{0,1:T(8,128)(2,1)} %pad_maximum_fusion.41), channel_id=1, source_target_pairs={{0,1},{1,0},{2,3},{3,2},{4,5},{5,4},{6,7},{7,6},{8,9},{9,8},{10,11... | collective-permute-start | bytes 1327112 | tf_op jit(solution)/shard_map/ppermute | solution.py:35
  16.7 50.6 %copy-start.20 = (bf16[512,384]{1,0:T(8,128)(2,1)}, bf16[512,384]{1,0:T(8,128)(2,1)S(1)}, u32[]{:S(2)}) copy-start(bf16[512,384]{1,0:T(8,128)(2,1)S(1)} %collective-permute-done.3) | copy-start | bytes 1179652
  16.7 50.6 %copy-start.22 = (bf16[512,384]{1,0:T(8,128)(2,1)}, bf16[512,384]{1,0:T(8,128)(2,1)S(1)}, u32[]{:S(2)}) copy-start(bf16[512,384]{1,0:T(8,128)(2,1)S(1)} %collective-permute-done.2) | copy-start | bytes 1179652
  17.7 14.6 %collective-permute-start.6 = (bf16[512,768]{1,0:T(8,128)(2,1)S(1)}, bf16[512,768]{1,0:T(8,128)(2,1)}, u32[]{:S(2)}, u32[]{:S(2)}) collective-permute-start(bf16[512,768]{1,0:T(8,128)(2,1)S(1)} %add_convert_fusion.3), channel_id=1, source_target_pairs={{0,4},{4,0},{1,5},{5,1},{2,6},{6,2},{3,7},{7,3},{8,12},{12,8},{9,1... | collective-permute-start | bytes 2359304 | tf_op jit(solution)/shard_map/ppermute | solution.py:31
  18.1 12.9 %collective-permute-start.9 = (bf16[192,384]{1,0:T(8,128)(2,1)S(1)}, bf16[192,384]{1,0:T(8,128)(2,1)S(1)}, u32[]{:S(2)}, u32[]{:S(2)}) collective-permute-start(bf16[192,384]{1,0:T(8,128)(2,1)S(1)} %dynamic-slice_bitcast_fusion.11), channel_id=1, source_target_pairs={{0,1},{1,0},{2,3},{3,2},{4,5},{5,4},{6,7},{7,6},{8,9},{9,8},{10,11... | collective-permute-start | bytes 442376 | tf_op jit(solution)/shard_map/ppermute | solution.py:35
  31.0 11.0 %collective-permute-start.10 = (bf16[192,768]{1,0:T(8,128)(2,1)S(1)}, bf16[192,768]{1,0:T(8,128)(2,1)S(1)}, u32[]{:S(2)}, u32[]{:S(2)}) collective-permute-start(bf16[192,768]{1,0:T(8,128)(2,1)S(1)} %pad_maximum_fusion.46), channel_id=1, source_target_pairs={{0,4},{4,0},{1,5},{5,1},{2,6},{6,2},{3,7},{7,3},{8,12},{12,8},{9,1... | collective-permute-start | bytes 884744 | tf_op jit(solution)/shard_map/ppermute | solution.py:31
  41.9 2.4 collective-permute-start.7
  42.9 15.9 %collective-permute-start.11 = (bf16[384,768]{1,0:T(8,128)(2,1)}, bf16[384,768]{1,0:T(8,128)(2,1)}, u32[]{:S(2)}, u32[]{:S(2)}) collective-permute-start(bf16[384,768]{1,0:T(8,128)(2,1)} %pad_maximum_fusion.39), channel_id=1, source_target_pairs={{0,3},{3,0},{1,2},{2,1},{4,7},{7,4},{5,6},{6,5},{8,11},{11,8},{9,1... | collective-permute-start | bytes 1769480 | tf_op jit(solution)/shard_map/ppermute | solution.py:39
  45.0 22.3 %collective-permute-start.8 = (bf16[384,512]{1,0:T(8,128)(2,1)}, bf16[384,512]{1,0:T(8,128)(2,1)}, u32[]{:S(2)}, u32[]{:S(2)}) collective-permute-start(bf16[384,512]{1,0:T(8,128)(2,1)} %pad_maximum_fusion.44), channel_id=1, source_target_pairs={{0,3},{3,0},{1,2},{2,1},{4,7},{7,4},{5,6},{6,5},{8,11},{11,8},{9,1... | collective-permute-start | bytes 1179656 | tf_op jit(solution)/shard_map/ppermute | solution.py:39
  48.4 25.5 %collective-permute-start.13 = (bf16[384,768]{1,0:T(8,128)(2,1)}, bf16[384,768]{1,0:T(8,128)(2,1)}, u32[]{:S(2)}, u32[]{:S(2)}) collective-permute-start(bf16[384,768]{1,0:T(8,128)(2,1)} %dynamic-slice_bitcast_fusion.3), channel_id=1, source_target_pairs={{0,1},{1,0},{2,3},{3,2},{4,5},{5,4},{6,7},{7,6},{8,9},{9,8},{10,11... | collective-permute-start | bytes 1769480 | tf_op jit(solution)/shard_map/ppermute | solution.py:35
  70.5 3.4 collective-permute-start.12
  73.1 13.9 %collective-permute-start.14 = (bf16[768,384]{1,0:T(8,128)(2,1)S(1)}, bf16[768,384]{1,0:T(8,128)(2,1)}, u32[]{:S(2)}, u32[]{:S(2)}) collective-permute-start(bf16[768,384]{1,0:T(8,128)(2,1)S(1)} %dynamic-slice_bitcast_fusion.2), channel_id=1, source_target_pairs={{0,1},{1,0},{2,3},{3,2},{4,5},{5,4},{6,7},{7,6},{8,9},{9,8},{10,11... | collective-permute-start | bytes 1769480 | tf_op jit(solution)/shard_map/ppermute | solution.py:35
  73.9 209.6 %copy-start.80 = (f32[768]{0:T(1024)}, f32[768]{0:T(1024)S(1)}, u32[]{:S(2)}) copy-start(f32[768]{0:T(1024)S(1)} %get-tuple-element.76) | copy-start | bytes 9220
  90.2 4.2 collective-permute-start.15
  94.7 20.0 %collective-permute-start.16 = (bf16[512,768]{1,0:T(8,128)(2,1)S(1)}, bf16[512,768]{1,0:T(8,128)(2,1)S(1)}, u32[]{:S(2)}, u32[]{:S(2)}) collective-permute-start(bf16[512,768]{1,0:T(8,128)(2,1)S(1)} %fusion.25), channel_id=1, source_target_pairs={{0,3},{3,0},{1,2},{2,1},{4,7},{7,4},{5,6},{6,5},{8,11},{11,8},{9,1... | collective-permute-start | bytes 2359304 | tf_op jit(solution)/shard_map/ppermute | solution.py:39
  96.2 23.2 %collective-permute-start.21 = (bf16[192,384]{1,0:T(8,128)(2,1)S(1)}, bf16[192,384]{1,0:T(8,128)(2,1)S(1)}, u32[]{:S(2)}, u32[]{:S(2)}) collective-permute-start(bf16[192,384]{1,0:T(8,128)(2,1)S(1)} %dynamic-slice_bitcast_fusion.10), channel_id=1, source_target_pairs={{0,1},{1,0},{2,3},{3,2},{4,5},{5,4},{6,7},{7,6},{8,9},{9,8},{10,11... | collective-permute-start | bytes 442376 | tf_op jit(solution)/shard_map/ppermute | solution.py:35
  116.9 15.6 %collective-permute-start.18 = (bf16[512,768]{1,0:T(8,128)(2,1)}, bf16[512,768]{1,0:T(8,128)(2,1)}, u32[]{:S(2)}, u32[]{:S(2)}) collective-permute-start(bf16[512,768]{1,0:T(8,128)(2,1)} %add_convert_fusion.1), channel_id=1, source_target_pairs={{0,4},{4,0},{1,5},{5,1},{2,6},{6,2},{3,7},{7,3},{8,12},{12,8},{9,1... | collective-permute-start | bytes 2359304 | tf_op jit(solution)/shard_map/ppermute | solution.py:31
  119.4 13.2 %collective-permute-start.17 = (bf16[576,384]{0,1:T(8,128)(2,1)}, bf16[576,384]{0,1:T(8,128)(2,1)}, u32[]{:S(2)}, u32[]{:S(2)}) collective-permute-start(bf16[576,384]{0,1:T(8,128)(2,1)} %pad_maximum_fusion.42), channel_id=1, source_target_pairs={{0,1},{1,0},{2,3},{3,2},{4,5},{5,4},{6,7},{7,6},{8,9},{9,8},{10,11... | collective-permute-start | bytes 1327112 | tf_op jit(solution)/shard_map/ppermute | solution.py:35
  119.4 1.7 collective-permute-start.22
  122.1 28.1 %collective-permute-start.23 = (bf16[384,768]{1,0:T(8,128)(2,1)S(1)}, bf16[384,768]{1,0:T(8,128)(2,1)S(1)}, u32[]{:S(2)}, u32[]{:S(2)}) collective-permute-start(bf16[384,768]{1,0:T(8,128)(2,1)S(1)} %pad_maximum_fusion.40), channel_id=1, source_target_pairs={{0,3},{3,0},{1,2},{2,1},{4,7},{7,4},{5,6},{6,5},{8,11},{11,8},{9,1... | collective-permute-start | bytes 1769480 | tf_op jit(solution)/shard_map/ppermute | solution.py:39
  141.7 2.0 collective-permute-start.19
  143.7 12.5 %collective-permute-start.20 = (bf16[384,512]{1,0:T(8,128)(2,1)S(1)}, bf16[384,512]{1,0:T(8,128)(2,1)S(1)}, u32[]{:S(2)}, u32[]{:S(2)}) collective-permute-start(bf16[384,512]{1,0:T(8,128)(2,1)S(1)} %pad_maximum_fusion.45), channel_id=1, source_target_pairs={{0,3},{3,0},{1,2},{2,1},{4,7},{7,4},{5,6},{6,5},{8,11},{11,8},{9,1... | collective-permute-start | bytes 1179656 | tf_op jit(solution)/shard_map/ppermute | solution.py:39
  145.1 19.1 %collective-permute-start.1 = (bf16[512,384]{1,0:T(8,128)(2,1)S(1)}, bf16[512,384]{1,0:T(8,128)(2,1)S(1)}, u32[]{:S(2)}, u32[]{:S(2)}) collective-permute-start(bf16[512,384]{1,0:T(8,128)(2,1)S(1)} %copy-done.92), channel_id=1, source_target_pairs={{0,3},{1,0},{2,7},{3,4},{4,1},{5,2},{6,5},{7,6},{8,11},{9,8},{10,1... | collective-permute-start | bytes 1179656 | tf_op jit(solution)/shard_map/ppermute | solution.py:569
  145.1 17.4 %collective-permute-start = (bf16[512,384]{1,0:T(8,128)(2,1)S(1)}, bf16[512,384]{1,0:T(8,128)(2,1)S(1)}, u32[]{:S(2)}, u32[]{:S(2)}) collective-permute-start(bf16[512,384]{1,0:T(8,128)(2,1)S(1)} %copy-done.92), channel_id=1, source_target_pairs={{0,0},{1,3},{2,4},{3,7},{4,2},{5,1},{6,6},{7,5},{8,8},{9,11},{10,1... | collective-permute-start | bytes 1179656 | tf_op jit(solution)/shard_map/ppermute | solution.py:569
  149.9 18.7 %collective-permute-start.27 = (bf16[384,768]{1,0:T(8,128)(2,1)S(1)}, bf16[384,768]{1,0:T(8,128)(2,1)S(1)}, u32[]{:S(2)}, u32[]{:S(2)}) collective-permute-start(bf16[384,768]{1,0:T(8,128)(2,1)S(1)} %dynamic-slice_bitcast_fusion), channel_id=1, source_target_pairs={{0,1},{1,0},{2,3},{3,2},{4,5},{5,4},{6,7},{7,6},{8,9},{9,8},{10,11... | collective-permute-start | bytes 1769480 | tf_op jit(solution)/shard_map/ppermute | solution.py:35
  157.8 10.8 %collective-permute-start.26 = (bf16[512,768]{1,0:T(8,128)(2,1)S(1)}, bf16[512,768]{1,0:T(8,128)(2,1)S(1)}, u32[]{:S(2)}, u32[]{:S(2)}) collective-permute-start(bf16[512,768]{1,0:T(8,128)(2,1)S(1)} %add_convert_fusion), channel_id=1, source_target_pairs={{0,4},{4,0},{1,5},{5,1},{2,6},{6,2},{3,7},{7,3},{8,12},{12,8},{9,1... | collective-permute-start | bytes 2359304 | tf_op jit(solution)/shard_map/ppermute | solution.py:31
  164.3 15.7 %collective-permute-start.24 = (bf16[512,768]{1,0:T(8,128)(2,1)S(1)}, bf16[512,768]{1,0:T(8,128)(2,1)S(1)}, u32[]{:S(2)}, u32[]{:S(2)}) collective-permute-start(bf16[512,768]{1,0:T(8,128)(2,1)S(1)} %constant_dynamic-update-slice_fusion), channel_id=1, source_target_pairs={{0,4},{4,0},{1,5},{5,1},{2,6},{6,2},{3,7},{7,3},{8,12},{12,8},{9,1... | collective-permute-start | bytes 2359304 | tf_op jit(solution)/shard_map/ppermute | solution.py:31
  164.5 15.5 %collective-permute-start.25 = (bf16[768,384]{1,0:T(8,128)(2,1)S(1)}, bf16[768,384]{1,0:T(8,128)(2,1)S(1)}, u32[]{:S(2)}, u32[]{:S(2)}) collective-permute-start(bf16[768,384]{1,0:T(8,128)(2,1)S(1)} %dynamic-slice_bitcast_fusion.1), channel_id=1, source_target_pairs={{0,1},{1,0},{2,3},{3,2},{4,5},{5,4},{6,7},{7,6},{8,9},{9,8},{10,11... | collective-permute-start | bytes 1769480 | tf_op jit(solution)/shard_map/ppermute | solution.py:35
  185.6 5.0 collective-permute-start.28
  190.8 20.0 %collective-permute-start.29 = (bf16[512,768]{1,0:T(8,128)(2,1)S(1)}, bf16[512,768]{1,0:T(8,128)(2,1)S(1)}, u32[]{:S(2)}, u32[]{:S(2)}) collective-permute-start(bf16[512,768]{1,0:T(8,128)(2,1)S(1)} %fusion.26), channel_id=1, source_target_pairs={{0,3},{3,0},{1,2},{2,1},{4,7},{7,4},{5,6},{6,5},{8,11},{11,8},{9,1... | collective-permute-start | bytes 2359304 | tf_op jit(solution)/shard_map/ppermute | solution.py:39
  212.4 4.8 collective-permute-start.30
  216.9 17.8 %collective-permute-start.33 = (bf16[512,768]{1,0:T(8,128)(2,1)}, bf16[512,768]{1,0:T(8,128)(2,1)}, u32[]{:S(2)}, u32[]{:S(2)}) collective-permute-start(bf16[512,768]{1,0:T(8,128)(2,1)} %slice.462), channel_id=1, source_target_pairs={{0,4},{4,0},{1,5},{5,1},{2,6},{6,2},{3,7},{7,3},{8,12},{12,8},{9,1... | collective-permute-start | bytes 2359304 | tf_op jit(solution)/shard_map/ppermute | solution.py:31
  234.1 2.8 collective-permute-start.31
  236.0 20.4 %collective-permute-start.34 = (bf16[512,768]{1,0:T(8,128)(2,1)S(1)}, bf16[512,768]{1,0:T(8,128)(2,1)S(1)}, u32[]{:S(2)}, u32[]{:S(2)}) collective-permute-start(bf16[512,768]{1,0:T(8,128)(2,1)S(1)} %get-tuple-element.83), channel_id=1, source_target_pairs={{0,3},{3,0},{1,2},{2,1},{4,7},{7,4},{5,6},{6,5},{8,11},{11,8},{9,1... | collective-permute-start | bytes 2359304 | tf_op jit(solution)/shard_map/ppermute | solution.py:39
  237.1 40.4 %collective-permute-start.32 = (bf16[512,768]{1,0:T(8,128)(2,1)S(1)}, bf16[512,768]{1,0:T(8,128)(2,1)S(1)}, u32[]{:S(2)}, u32[]{:S(2)}) collective-permute-start(bf16[512,768]{1,0:T(8,128)(2,1)S(1)} %fusion.27), channel_id=1, source_target_pairs={{0,3},{3,0},{1,2},{2,1},{4,7},{7,4},{5,6},{6,5},{8,11},{11,8},{9,1... | collective-permute-start | bytes 2359304 | tf_op jit(solution)/shard_map/ppermute | solution.py:39
  256.6 22.5 %collective-permute-start.35 = (bf16[512,384]{1,0:T(8,128)(2,1)S(1)}, bf16[512,384]{1,0:T(8,128)(2,1)S(1)}, u32[]{:S(2)}, u32[]{:S(2)}) collective-permute-start(bf16[512,384]{1,0:T(8,128)(2,1)S(1)} %fusion.34), channel_id=1, source_target_pairs={{0,0},{3,1},{4,2},{7,3},{2,4},{1,5},{6,6},{5,7},{8,8},{11,9},{12,1... | collective-permute-start | bytes 1179656 | tf_op jit(solution)/shard_map/ppermute | solution.py:600
  280.5 3.0 collective-permute-start.36
  295.2 2.4 collective-permute-start.37
  300.3 20.3 %collective-permute-start.38 = (bf16[512,768]{1,0:T(8,128)(2,1)}, bf16[512,768]{1,0:T(8,128)(2,1)}, u32[]{:S(2)}, u32[]{:S(2)}) collective-permute-start(bf16[512,768]{1,0:T(8,128)(2,1)} %fusion.28), channel_id=1, source_target_pairs={{0,3},{3,0},{1,2},{2,1},{4,7},{7,4},{5,6},{6,5},{8,11},{11,8},{9,1... | collective-permute-start | bytes 2359304 | tf_op jit(solution)/shard_map/ppermute | solution.py:39
  307.1 26.0 %collective-permute-start.43 = (bf16[128]{0:T(256)(128)(2,1)S(1)}, bf16[128]{0:T(256)(128)(2,1)S(1)}, u32[]{:S(2)}, u32[]{:S(2)}) collective-permute-start(bf16[128]{0:T(256)(128)(2,1)S(1)} %convert_element_type.221), channel_id=1, source_target_pairs={{0,3},{3,0},{1,2},{2,1},{4,7},{7,4},{5,6},{6,5},{8,11},{11,8},{9,1... | collective-permute-start | bytes 776 | tf_op jit(solution)/shard_map/ppermute | solution.py:39
  327.1 7.9 %collective-permute-start.39 = (bf16[512,768]{1,0:T(8,128)(2,1)}, bf16[512,768]{1,0:T(8,128)(2,1)}, u32[]{:S(2)}, u32[]{:S(2)}) collective-permute-start(bf16[512,768]{1,0:T(8,128)(2,1)} %get-tuple-element.80), channel_id=1, source_target_pairs={{0,4},{4,0},{1,5},{5,1},{2,6},{6,2},{3,7},{7,3},{8,12},{12,8},{9,1... | collective-permute-start | bytes 2359304 | tf_op jit(solution)/shard_map/ppermute | solution.py:31
  354.0 17.0 %collective-permute-start.40 = (bf16[512,768]{1,0:T(8,128)(2,1)}, bf16[512,768]{1,0:T(8,128)(2,1)}, u32[]{:S(2)}, u32[]{:S(2)}) collective-permute-start(bf16[512,768]{1,0:T(8,128)(2,1)} %slice.460), channel_id=1, source_target_pairs={{0,4},{4,0},{1,5},{5,1},{2,6},{6,2},{3,7},{7,3},{8,12},{12,8},{9,1... | collective-permute-start | bytes 2359304 | tf_op jit(solution)/shard_map/ppermute | solution.py:31
  370.2 10.7 %collective-permute-start.44 = (bf16[128]{0:T(256)(128)(2,1)}, bf16[128]{0:T(256)(128)(2,1)S(1)}, u32[]{:S(2)}, u32[]{:S(2)}) collective-permute-start(bf16[128]{0:T(256)(128)(2,1)} %convert_element_type.232), channel_id=1, source_target_pairs={{0,3},{3,0},{1,2},{2,1},{4,7},{7,4},{5,6},{6,5},{8,11},{11,8},{9,1... | collective-permute-start | bytes 776 | tf_op jit(solution)/shard_map/ppermute | solution.py:39
  372.9 20.2 %collective-permute-start.41 = (bf16[512,768]{1,0:T(8,128)(2,1)S(1)}, bf16[512,768]{1,0:T(8,128)(2,1)S(1)}, u32[]{:S(2)}, u32[]{:S(2)}) collective-permute-start(bf16[512,768]{1,0:T(8,128)(2,1)S(1)} %fusion.29), channel_id=1, source_target_pairs={{0,3},{3,0},{1,2},{2,1},{4,7},{7,4},{5,6},{6,5},{8,11},{11,8},{9,1... | collective-permute-start | bytes 2359304 | tf_op jit(solution)/shard_map/ppermute | solution.py:39
  492.8 10.6 %collective-permute-start.42 = (bf16[512,384]{1,0:T(8,128)(2,1)S(1)}, bf16[512,384]{1,0:T(8,128)(2,1)S(1)}, u32[]{:S(2)}, u32[]{:S(2)}) collective-permute-start(bf16[512,384]{1,0:T(8,128)(2,1)S(1)} %fusion.30), channel_id=1, source_target_pairs={{0,0},{3,1},{4,2},{7,3},{2,4},{1,5},{6,6},{5,7},{8,8},{11,9},{12,1... | collective-permute-start | bytes 1179656 | tf_op jit(solution)/shard_map/ppermute | solution.py:609
  (98 other events, 751.4 us)

commit v3 on v2

--- a/solution.py
+++ b/solution.py
@@ -50,22 +50,15 @@
     )
 
 
-def gather_core(value):
-    return jnp.concatenate((value, swap_core(value)), axis=0)
-
-
-def total_group(partial):
-    rows = partial.shape[0] // 2
-    chip = partial[:rows] + swap_core(partial[rows:].astype(BF)).astype(F32)
-    return chip + flip(swap_cross(chip.astype(BF)), 1).astype(F32)
-
-
-def norm(resid, gain, shift):
+MESH = pl.DeviceIdType.MESH
+ROWS = 256
+
+
+def norm(resid):
     mean = jnp.mean(resid, axis=1, keepdims=True)
     centred = resid - mean
     factor = lax.rsqrt(jnp.mean(centred * centred, axis=1, keepdims=True) + EPS)
-    normal = centred * factor
-    return normal, factor, (normal * gain + shift).astype(BF)
+    return centred * factor, factor
 
 
 def norm_back(grad, normal, factor, gain):
@@ -90,112 +83,6 @@
 
 
 SCALE2 = LOG2E * HEAD_DIM ** (-0.5)
-
-
-def attend_kernel(qkv_ref, gain_ref, mixed_ref, total_ref):
-    gains = gain_ref[...]
-    query = (head_norm(qkv_ref[0, 0])[0] * gains[:, 0:1]).astype(BF)
-    key_rows = (head_norm(qkv_ref[1, 0])[0] * gains[:, 1:2]).T.astype(BF)
-    value = qkv_ref[2, 0].astype(BF)
-    for at in range(0, query.shape[1], BLOCK):
-        expo = jnp.exp2(dot(key_rows, query[:, at : at + BLOCK]) * SCALE2)
-        total = jnp.sum(expo, axis=0, keepdims=True)
-        mixed = dot(value, expo.astype(BF))
-        mixed_ref[0, :, at : at + BLOCK] = (mixed * (1.0 / total)).astype(BF)
-        total_ref[0, :, at : at + BLOCK] = jnp.log2(total)
-
-
-def attend(qkv, gains):
-    heads, rows = qkv.shape[1], qkv.shape[3]
-    return pl.pallas_call(
-        attend_kernel,
-        grid=(heads,),
-        in_specs=[
-            pl.BlockSpec((3, 1, HEAD_DIM, rows), lambda h: (0, h, 0, 0)),
-            pl.BlockSpec((HEAD_DIM, 2), lambda h: (0, 0)),
-        ],
-        out_specs=[
-            pl.BlockSpec((1, HEAD_DIM, rows), lambda h: (h, 0, 0)),
-            pl.BlockSpec((1, 1, rows), lambda h: (h, 0, 0)),
-        ],
-        out_shape=[
-            jax.ShapeDtypeStruct((heads, HEAD_DIM, rows), BF),
-            jax.ShapeDtypeStruct((heads, 1, rows), F32),
-        ],
-        compiler_params=pltpu.CompilerParams(vmem_limit_bytes=40 * 2**20),
-        cost_estimate=pl.CostEstimate(
-            flops=16 * heads * rows * rows * HEAD_DIM,
-            bytes_accessed=heads * rows * HEAD_DIM * 16,
-            transcendentals=heads * rows * rows,
-        ),
-        name="attend",
-    )(qkv, gains)
-
-
-def attend_back_kernel(qkv_ref, gain_ref, total_ref, grad_ref, out_ref, gain_out_ref):
-    gains = gain_ref[...]
-    query_normal, query_factor = head_norm(qkv_ref[0, 0])
-    key_normal, key_factor = head_norm(qkv_ref[1, 0])
-    query = (query_normal * gains[:, 0:1]).astype(BF)
-    key_full = key_normal * gains[:, 1:2]
-    key = key_full.astype(BF)
-    key_rows = key_full.T.astype(BF)
-    value_rows = qkv_ref[2, 0].T.astype(BF)
-    key_sum = jnp.zeros(key.shape, F32)
-    value_sum = jnp.zeros(key.shape, F32)
-    query_parts = []
-    for at in range(0, query.shape[1], BLOCK):
-        here = slice(at, at + BLOCK)
-        grad = grad_ref[0, :, here]
-        probs = jnp.exp2(dot(key_rows, query[:, here]) * SCALE2 - total_ref[0, :, here])
-        pulled = dot(value_rows, grad)
-        delta = jnp.sum(probs * pulled, axis=0, keepdims=True)
-        score_grad = (probs * (pulled - delta)).astype(BF)
-        query_parts.append(dot(key, score_grad))
-        key_sum = key_sum + dot(query[:, here], score_grad, 1, 1)
-        value_sum = value_sum + dot(grad, probs.astype(BF), 1, 1)
-    scale = HEAD_DIM ** (-0.5)
-    query_sum = jnp.concatenate(query_parts, axis=1) * scale
-    key_sum = key_sum * scale
-    out_ref[0, 0] = head_norm_back(query_sum, query_normal, query_factor, gains[:, 0:1]).astype(BF)
-    out_ref[1, 0] = head_norm_back(key_sum, key_normal, key_factor, gains[:, 1:2]).astype(BF)
-    out_ref[2, 0] = value_sum.astype(BF)
-    gain_out_ref[0] = jnp.concatenate(
-        (
-            jnp.sum(query_sum * query_normal, axis=1, keepdims=True),
-            jnp.sum(key_sum * key_normal, axis=1, keepdims=True),
-        ),
-        axis=1,
-    )
-
-
-def attend_back(qkv, gains, total, grad):
-    heads, rows = qkv.shape[1], qkv.shape[3]
-    return pl.pallas_call(
-        attend_back_kernel,
-        grid=(heads,),
-        in_specs=[
-            pl.BlockSpec((3, 1, HEAD_DIM, rows), lambda h: (0, h, 0, 0)),
-            pl.BlockSpec((HEAD_DIM, 2), lambda h: (0, 0)),
-            pl.BlockSpec((1, 1, rows), lambda h: (h, 0, 0)),
-            pl.BlockSpec((1, HEAD_DIM, rows), lambda h: (h, 0, 0)),
-        ],
-        out_specs=[
-            pl.BlockSpec((3, 1, HEAD_DIM, rows), lambda h: (0, h, 0, 0)),
-            pl.BlockSpec((1, HEAD_DIM, 2), lambda h: (h, 0, 0)),
-        ],
-        out_shape=[
-            jax.ShapeDtypeStruct((3, heads, HEAD_DIM, rows), BF),
-            jax.ShapeDtypeStruct((heads, HEAD_DIM, 2), F32),
-        ],
-        compiler_params=pltpu.CompilerParams(vmem_limit_bytes=48 * 2**20),
-        cost_estimate=pl.CostEstimate(
-            flops=40 * heads * rows * rows * HEAD_DIM,
-            bytes_accessed=heads * rows * HEAD_DIM * 24,
-            transcendentals=heads * rows * rows,
-        ),
-        name="attend_back",
-    )(qkv, gains, total, grad)
 
 
 def gelu_parts(hidden):
@@ -208,62 +95,422 @@
     return active, slope
 
 
-def layer_forward(resid, weights):
+def partners():
+    core, row, col = (lax.axis_index(name) for name in GROUP)
+    return (
+        {"core": 1 - core},
+        {"row": 1 - row, "col": 1 - col},
+        {"core": 1 - core, "row": 1 - row, "col": 1 - col},
+    )
+
+
+def greet(devices):
+    barrier = pltpu.get_barrier_semaphore()
+    for device in devices:
+        pl.semaphore_signal(barrier, inc=1, device_id=device, device_id_type=MESH)
+
+
+def meet(devices):
+    pl.semaphore_wait(pltpu.get_barrier_semaphore(), len(devices))
+
+
+def send(source, target, sems, at, device):
+    copy = pltpu.make_async_remote_copy(
+        src_ref=source,
+        dst_ref=target,
+        send_sem=sems.at[0, at],
+        recv_sem=sems.at[1, at],
+        device_id=device,
+        device_id_type=MESH,
+    )
+    copy.start()
+    return copy
+
+
+class Totals:
+    def __init__(self, chip, core_out, core_in, cross_out, cross_in, sems, partner, cross):
+        self.refs = (chip, core_out, core_in, cross_out, cross_in)
+        self.sems, self.partner, self.cross = sems, partner, cross
+        self.copies = []
+
+    def run(self, compute, ready):
+        chip, core_out, core_in, cross_out, cross_in = self.refs
+        rows = chip.shape[0]
+        count = rows // ROWS
+        core_copies, cross_copies = [], []
+
+        def pass_on(at):
+            here = pl.ds(at * ROWS, ROWS)
+            core_copies[at].wait_recv()
+            total = chip[here, :] + core_in[here, :].astype(F32)
+            chip[here, :] = total
+            if cross_out is not None:
+                cross_out[here, :] = total.astype(BF)
+                cross_copies.append(
+                    send(cross_out.at[here, :], cross_in.at[here, :], self.sems, count + at, self.cross)
+                )
+
+        for at in range(count):
+            here = pl.ds(at * ROWS, ROWS)
+            chip[here, :] = compute(at * ROWS)
+            if at > 0:
+                pass_on(at - 1)
+            ready(at)
+            core_out[here, :] = compute(rows + at * ROWS).astype(BF)
+            core_copies.append(
+                send(core_out.at[here, :], core_in.at[here, :], self.sems, at, self.partner)
+            )
+        pass_on(count - 1)
+        self.cross_copies = cross_copies
+        self.copies = core_copies + cross_copies
+
+    def chunk(self, at):
+        chip, _, _, _, cross_in = self.refs
+        here = pl.ds(at * ROWS, ROWS)
+        self.cross_copies[at].wait_recv()
+        half = chip.shape[1] // 2
+        other = cross_in[here, :].astype(F32)
+        return chip[here, :] + jnp.concatenate((other[:, half:], other[:, :half]), axis=1)
+
+    def close(self):
+        for copy in self.copies:
+            copy.wait_send()
+
+
+def spread(fill, whole, sems, partner):
+    rows = whole.shape[0] // 2
+    copies = []
+    for at in range(rows // ROWS):
+        here = pl.ds(at * ROWS, ROWS)
+        whole[here, :] = fill(at * ROWS)
+        if at == 0:
+            yield None
+        copies.append(
+            send(whole.at[here, :], whole.at[pl.ds(rows + at * ROWS, ROWS), :], sems, at, partner)
+        )
+    yield copies
+
+
+def fill_and_send(fill, whole, sems, devices):
+    steps = spread(fill, whole, sems, devices[0])
+    next(steps)
+    meet(devices)
+    return next(steps)
+
+
+def attend_forward_kernel(
+    resid_ref, w_qkv_ref, gain_ref, w_out_ref, vector_ref,
+    out_ref, seen_ref, qkv_ref, mixed_ref, total_ref,
+    joined, seen_sems, head_sems,
+):
+    near, cross, far = partners()
+    devices = (near, cross, far)
+    greet(devices)
+    rows = resid_ref.shape[0]
+    heads = mixed_ref.shape[0] // HEAD_DIM
+    span = heads * HEAD_DIM
+
+    def fill(row):
+        normal, _ = norm(resid_ref[pl.ds(row, ROWS), :])
+        return (normal * vector_ref[0:1, :] + vector_ref[1:2, :]).astype(BF)
+
+    copies = fill_and_send(fill, seen_ref, seen_sems, devices)
+    for at in range(2 * rows // ROWS):
+        if at * ROWS >= rows:
+            copies[at - rows // ROWS].wait_recv()
+        here = pl.ds(at * ROWS, ROWS)
+        qkv_ref[:, here] = dot(w_qkv_ref[...], seen_ref[here, :], 1, 1)
+    gains = gain_ref[...]
+    for head in range(heads):
+        own = pl.ds(head * HEAD_DIM, HEAD_DIM)
+        query = (head_norm(qkv_ref[own, :])[0] * gains[:, 0:1]).astype(BF)
+        key = head_norm(qkv_ref[pl.ds(span + head * HEAD_DIM, HEAD_DIM), :])[0] * gains[:, 1:2]
+        key_rows = key.T.astype(BF)
+        value = qkv_ref[pl.ds(2 * span + head * HEAD_DIM, HEAD_DIM), :].astype(BF)
+        for at in range(0, 2 * rows, BLOCK):
+            expo = jnp.exp2(dot(key_rows, query[:, at : at + BLOCK]) * SCALE2)
+            total = jnp.sum(expo, axis=0, keepdims=True)
+            mixed = (dot(value, expo.astype(BF)) * (1.0 / total)).astype(BF)
+            mixed_ref[own, at : at + BLOCK] = mixed
+            if at < rows:
+                joined[own, at : at + BLOCK] = mixed
+            total_ref[head : head + 1, at : at + BLOCK] = jnp.log2(total)
+        mine, others = pl.ds(0, rows), pl.ds(rows, rows)
+        for spot, (device, columns) in enumerate(((near, others), (cross, mine), (far, others))):
+            copies.append(
+                send(
+                    mixed_ref.at[own, columns],
+                    joined.at[pl.ds((spot + 1) * span + head * HEAD_DIM, HEAD_DIM), :],
+                    head_sems,
+                    head * 3 + spot,
+                    device,
+                )
+            )
+    for copy in copies[-3 * heads :]:
+        copy.wait_recv()
+    for at in range(rows // ROWS):
+        here = pl.ds(at * ROWS, ROWS)
+        out_ref[here, :] = resid_ref[here, :] + dot(joined[:, here], w_out_ref[...], 0, 0)
+    for copy in copies:
+        copy.wait_send()
+
+
+def feed_forward_kernel(last, resid_ref, w_up_ref, bias_ref, w_down_ref, vector_ref, *refs):
+    out_ref, seen_ref, active_ref, slope_ref = refs[:4]
+    chip, core_out, core_in = refs[4:7]
+    cross_out, cross_in = (None, None) if last else refs[7:9]
+    seen_sems, total_sems = refs[-2:]
+    near, cross, _ = partners()
+    devices = (near,) if last else (near, cross)
+    greet(devices)
+
+    def fill(row):
+        normal, _ = norm(resid_ref[pl.ds(row, ROWS), :])
+        return (normal * vector_ref[2:3, :] + vector_ref[3:4, :]).astype(BF)
+
+    copies = fill_and_send(fill, seen_ref, seen_sems, devices)
+
+    def compute(row):
+        here = pl.ds(row, ROWS)
+        hidden = dot(seen_ref[here, :], w_up_ref[...]) + bias_ref[...]
+        active, slope = gelu_parts(hidden)
+        active = active.astype(BF)
+        active_ref[here, :] = active
+        slope_ref[here, :] = slope.astype(BF)
+        return dot(active, w_down_ref[...])
+
+    totals = Totals(chip, core_out, core_in, cross_out, cross_in, total_sems, near, cross)
+    totals.run(compute, lambda at: copies[at].wait_recv())
+    for at in range(resid_ref.shape[0] // ROWS):
+        here = pl.ds(at * ROWS, ROWS)
+        total = chip[here, :] if last else totals.chunk(at)
+        out_ref[here, :] = total if last else resid_ref[here, :] + (total + vector_ref[4:5, :])
+    for copy in copies:
+        copy.wait_send()
+    totals.close()
+
+
+def feed_backward_kernel(
+    grad_ref, resid_ref, seen_ref, active_ref, slope_ref, w_up_ref, w_down_ref, vector_ref,
+    out_ref, up_ref, down_ref, small_ref,
+    branch, hidden, chip, core_out, core_in, cross_out, cross_in, seen_sems, total_sems,
+):
+    near, cross, _ = partners()
+    devices = (near, cross)
+    greet(devices)
+    width = grad_ref.shape[1]
+    copies = fill_and_send(
+        lambda row: grad_ref[pl.ds(row, ROWS), :].astype(BF), branch, seen_sems, devices
+    )
+
+    def compute(row):
+        here = pl.ds(row, ROWS)
+        active_grad = dot(branch[here, :], w_down_ref[...], 1, 1)
+        low = (active_grad * slope_ref[here, :].astype(F32)).astype(BF)
+        hidden[here, :] = low
+        return dot(low, w_up_ref[...], 1, 1)
+
+    totals = Totals(chip, core_out, core_in, cross_out, cross_in, total_sems, near, cross)
+    totals.run(compute, lambda at: copies[at].wait_recv())
+    rows = grad_ref.shape[0]
+    for at in range(0, width, ROWS):
+        down_ref[at : at + ROWS, :] = dot(active_ref[:, at : at + ROWS], branch[...], 0, 0).astype(BF)
+        up_ref[at : at + ROWS, :] = dot(seen_ref[:, at : at + ROWS], hidden[...], 0, 0).astype(BF)
+    small_ref[2:3, :] = jnp.sum(branch[0:rows, :].astype(F32), axis=0, keepdims=True)
+    small_ref[3:4, :] = jnp.sum(hidden[...].astype(F32), axis=0, keepdims=True)
+    gain_sum = jnp.zeros((1, width), F32)
+    shift_sum = jnp.zeros((1, width), F32)
+    for at in range(rows // ROWS):
+        here = pl.ds(at * ROWS, ROWS)
+        grad = totals.chunk(at)
+        normal, factor = norm(resid_ref[here, :])
+        gain_sum = gain_sum + jnp.sum(grad * normal, axis=0, keepdims=True)
+        shift_sum = shift_sum + jnp.sum(grad, axis=0, keepdims=True)
+        out_ref[here, :] = grad_ref[here, :] + norm_back(grad, normal, factor, vector_ref[2:3, :])
+    small_ref[0:1, :] = gain_sum
+    small_ref[1:2, :] = shift_sum
+    for copy in copies:
+        copy.wait_send()
+    totals.close()
+
+
+def attend_backward_kernel(
+    grad_ref, resid_ref, seen_ref, qkv_ref, mixed_ref, total_ref, w_qkv_ref, w_out_ref, gain_ref,
+    vector_ref, out_ref, grad_qkv_ref, grad_out_ref, small_ref, gains_ref,
+    proj, mixed_grad, qkv_grad, chip, core_out, core_in, cross_out, cross_in, seen_sems, total_sems,
+):
+    near, cross, _ = partners()
+    devices = (near, cross)
+    greet(devices)
+    rows, width = grad_ref.shape
+    copies = fill_and_send(
+        lambda row: grad_ref[pl.ds(row, ROWS), :].astype(BF), proj, seen_sems, devices
+    )
+    for at in range(2 * rows // ROWS):
+        if at * ROWS >= rows:
+            copies[at - rows // ROWS].wait_recv()
+        here = pl.ds(at * ROWS, ROWS)
+        mixed_grad[:, here] = dot(w_out_ref[...], proj[here, :], 1, 1).astype(BF)
+    gains = gain_ref[...]
+    span = mixed_ref.shape[0]
+    scale = HEAD_DIM ** (-0.5)
+    gains_sum = jnp.zeros((HEAD_DIM, 2), F32)
+    for head in range(span // HEAD_DIM):
+        own = pl.ds(head * HEAD_DIM, HEAD_DIM)
+        key_at = pl.ds(span + head * HEAD_DIM, HEAD_DIM)
+        value_at = pl.ds(2 * span + head * HEAD_DIM, HEAD_DIM)
+        query_normal, query_factor = head_norm(qkv_ref[own, :])
+        key_normal, key_factor = head_norm(qkv_ref[key_at, :])
+        query = (query_normal * gains[:, 0:1]).astype(BF)
+        key_full = key_normal * gains[:, 1:2]
+        key = key_full.astype(BF)
+        key_rows = key_full.T.astype(BF)
+        value_rows = qkv_ref[value_at, :].T.astype(BF)
+        key_sum = jnp.zeros(key.shape, F32)
+        value_sum = jnp.zeros(key.shape, F32)
+        query_parts = []
+        for at in range(0, 2 * rows, BLOCK):
+            grad = mixed_grad[own, at : at + BLOCK]
+            logits = dot(key_rows, query[:, at : at + BLOCK]) * SCALE2
+            probs = jnp.exp2(logits - total_ref[head : head + 1, at : at + BLOCK])
+            pulled = dot(value_rows, grad)
+            delta = jnp.sum(probs * pulled, axis=0, keepdims=True)
+            score_grad = (probs * (pulled - delta)).astype(BF)
+            query_parts.append(dot(key, score_grad))
+            key_sum = key_sum + dot(query[:, at : at + BLOCK], score_grad, 1, 1)
+            value_sum = value_sum + dot(grad, probs.astype(BF), 1, 1)
+        query_sum = jnp.concatenate(query_parts, axis=1) * scale
+        key_sum = key_sum * scale
+        qkv_grad[own, :] = head_norm_back(query_sum, query_normal, query_factor, gains[:, 0:1]).astype(BF)
+        qkv_grad[key_at, :] = head_norm_back(key_sum, key_normal, key_factor, gains[:, 1:2]).astype(BF)
+        qkv_grad[value_at, :] = value_sum.astype(BF)
+        gains_sum = gains_sum + jnp.concatenate(
+            (
+                jnp.sum(query_sum * query_normal, axis=1, keepdims=True),
+                jnp.sum(key_sum * key_normal, axis=1, keepdims=True),
+            ),
+            axis=1,
+        )
+    gains_ref[...] = gains_sum
+
+    def compute(row):
+        return dot(qkv_grad[:, pl.ds(row, ROWS)], w_qkv_ref[...], 0, 0)
+
+    totals = Totals(chip, core_out, core_in, cross_out, cross_in, total_sems, near, cross)
+    totals.run(compute, lambda at: None)
+    for at in range(0, 3 * span, span):
+        here = pl.ds(at, span)
+        grad_qkv_ref[here, :] = dot(qkv_grad[here, :], seen_ref[...]).astype(BF)
+    grad_out_ref[...] = dot(mixed_ref[...], proj[...]).astype(BF)
+    gain_sum = jnp.zeros((1, width), F32)
+    shift_sum = jnp.zeros((1, width), F32)
+    for at in range(rows // ROWS):
+        here = pl.ds(at * ROWS, ROWS)
+        grad = totals.chunk(at)
+        normal, factor = norm(resid_ref[here, :])
+        gain_sum = gain_sum + jnp.sum(grad * normal, axis=0, keepdims=True)
+        shift_sum = shift_sum + jnp.sum(grad, axis=0, keepdims=True)
+        out_ref[here, :] = grad_ref[here, :] + norm_back(grad, normal, factor, vector_ref[0:1, :])
+    small_ref[0:1, :] = gain_sum
+    small_ref[1:2, :] = shift_sum
+    for copy in copies:
+        copy.wait_send()
+    totals.close()
+
+
+def call(kernel, name, collective_id, inputs, outs, scratch):
+    vmem = pl.BlockSpec(memory_space=pltpu.VMEM)
+    return pl.pallas_call(
+        kernel,
+        in_specs=[vmem] * len(inputs),
+        out_specs=[vmem] * len(outs),
+        out_shape=[jax.ShapeDtypeStruct(*out) for out in outs],
+        scratch_shapes=scratch,
+        compiler_params=pltpu.CompilerParams(
+            collective_id=collective_id, has_side_effects=True, vmem_limit_bytes=48 * 2**20
+        ),
+        name=name,
+    )(*inputs)
+
+
+def pair_sems(count):
+    return pltpu.SemaphoreType.DMA((2, count))
+
+
+def total_scratch(rows, width, last=False):
+    low = pltpu.VMEM((rows, width), BF)
+    count = rows // ROWS
+    return [pltpu.VMEM((rows, width), F32)] + [low] * (2 if last else 4) + [
+        pair_sems(count),
+        pair_sems(2 * count),
+    ]
+
+
+def layer_forward(resid, weights, last):
     w_qkv, gains, w_out, w_up, up_bias, w_down, vectors = weights
-    rows = resid.shape[0]
-    normal_one, factor_one, normed_one = norm(resid, vectors[0], vectors[1])
-    seen_one = gather_core(normed_one)
-    qkv = dot(w_qkv, seen_one, 1, 1).reshape(3, -1, HEAD_DIM, 2 * rows)
-    mixed, total = attend(qkv, gains)
-    mine = mixed.reshape(-1, 2 * rows)
-    chip = jnp.concatenate((mine[:, :rows], swap_core(mine[:, rows:])), axis=0)
-    joined = jnp.concatenate((chip, swap_cross(chip)), axis=0)
-    resid_two = resid + dot(joined, w_out, 0, 0)
-    normal_two, factor_two, normed_two = norm(resid_two, vectors[2], vectors[3])
-    seen_two = gather_core(normed_two)
-    hidden = dot(seen_two, w_up) + up_bias
-    active = gelu_parts(hidden)[0].astype(BF)
-    result = (resid_two + vectors[4]) + total_group(dot(active, w_down))
-    cache = (
-        normal_one, factor_one, seen_one, qkv, mixed, total,
-        normal_two, factor_two, seen_two, hidden, active,
-    )
+    rows, width = resid.shape
+    span = w_qkv.shape[0] // 3
+    units = w_up.shape[1]
+    resid_two, seen_one, qkv, mixed, total = call(
+        attend_forward_kernel,
+        "attend_forward",
+        2,
+        (resid, w_qkv, gains, w_out, vectors),
+        [
+            ((rows, width), F32),
+            ((2 * rows, width), BF),
+            ((3 * span, 2 * rows), F32),
+            ((span, 2 * rows), BF),
+            ((span // HEAD_DIM, 2 * rows), F32),
+        ],
+        [pltpu.VMEM((4 * span, rows), BF), pair_sems(rows // ROWS), pair_sems(3 * span // HEAD_DIM)],
+    )
+    result, seen_two, active, slope = call(
+        functools.partial(feed_forward_kernel, last),
+        "feed_forward",
+        4 if last else 3,
+        (resid_two, w_up, up_bias[None], w_down, vectors),
+        [((rows, width), F32), ((2 * rows, width), BF)] + [((2 * rows, units), BF)] * 2,
+        total_scratch(rows, width, last),
+    )
+    cache = (resid, seen_one, qkv, mixed, total, resid_two, seen_two, active, slope)
     return result, cache
 
 
 def layer_backward(grad, cache, weights, w_out_mine):
     w_qkv, gains, w_out, w_up, up_bias, w_down, vectors = weights
-    (
-        normal_one, factor_one, seen_one, qkv, mixed, total,
-        normal_two, factor_two, seen_two, hidden, active,
-    ) = cache
-    rows = grad.shape[0]
-    branch = grad.astype(BF)
-    seen_branch = gather_core(branch)
-    active_grad = dot(seen_branch, w_down, 1, 1)
-    hidden_grad = (active_grad * gelu_parts(hidden)[1]).astype(BF)
-    normed_two_grad = total_group(dot(hidden_grad, w_up, 1, 1))
-    grad_down = dot(active, seen_branch, 0, 0)
-    grad_up = dot(seen_two, hidden_grad, 0, 0)
-    bias_up = jnp.sum(hidden_grad.astype(F32), axis=0)
-    bias_down = jnp.sum(branch.astype(F32), axis=0)
-    gain_two = jnp.sum(normed_two_grad * normal_two, axis=0)
-    shift_two = jnp.sum(normed_two_grad, axis=0)
-    resid_two_grad = grad + norm_back(normed_two_grad, normal_two, factor_two, vectors[2])
-    seen_proj = gather_core(resid_two_grad.astype(BF))
-    mine = mixed.reshape(-1, 2 * rows)
-    mixed_grad = dot(w_out_mine, seen_proj, 1, 1).astype(BF).reshape(mixed.shape)
-    grad_out = dot(mine, seen_proj)
-    qkv_grad, gains_grad = attend_back(qkv, gains, total, mixed_grad)
-    qkv_grad = qkv_grad.reshape(-1, 2 * rows)
-    normed_one_grad = total_group(dot(qkv_grad, w_qkv, 0, 0))
-    grad_qkv = dot(qkv_grad, seen_one)
-    gain_one = jnp.sum(normed_one_grad * normal_one, axis=0)
-    shift_one = jnp.sum(normed_one_grad, axis=0)
-    resid_grad = resid_two_grad + norm_back(normed_one_grad, normal_one, factor_one, vectors[0])
-    gains_grad = jnp.sum(gains_grad, axis=0).T.reshape(-1)
-    small = jnp.stack((gain_one, shift_one, gain_two, shift_two, bias_down))
-    return resid_grad, (grad_up, grad_down, grad_qkv, grad_out, small, bias_up, gains_grad)
+    resid, seen_one, qkv, mixed, total, resid_two, seen_two, active, slope = cache
+    rows, width = grad.shape
+    units = w_up.shape[1]
+    span = mixed.shape[0]
+    low = pltpu.VMEM((2 * rows, width), BF)
+    resid_two_grad, grad_up, grad_down, small_two = call(
+        feed_backward_kernel,
+        "feed_backward",
+        5,
+        (grad, resid_two, seen_two, active, slope, w_up, w_down, vectors),
+        [((rows, width), F32), ((width, units), BF), ((units, width), BF), ((4, width), F32)],
+        [low, pltpu.VMEM((2 * rows, units), BF)] + total_scratch(rows, width),
+    )
+    resid_grad, grad_qkv, grad_out, small_one, gains_grad = call(
+        attend_backward_kernel,
+        "attend_backward",
+        6,
+        (resid_two_grad, resid, seen_one, qkv, mixed, total, w_qkv, w_out_mine, gains, vectors),
+        [
+            ((rows, width), F32),
+            ((3 * span, width), BF),
+            ((span, width), BF),
+            ((2, width), F32),
+            ((HEAD_DIM, 2), F32),
+        ],
+        [low, pltpu.VMEM((span, 2 * rows), BF), pltpu.VMEM((3 * span, 2 * rows), BF)]
+        + total_scratch(rows, width),
+    )
+    small = jnp.concatenate((small_one, small_two[:3]), axis=0)
+    return resid_grad, (
+        grad_up, grad_down, grad_qkv, grad_out, small, small_two[3], gains_grad.T.reshape(-1),
+    )
 
 
 def link_bits():
@@ -594,16 +841,18 @@
         mine_out.append(out_here)
     caches = []
     for at in range(layers):
-        resid, cache = layer_forward(resid, weights[at])
+        last = at == layers - 1
+        total, cache = layer_forward(resid, weights[at], last)
         caches.append(cache)
-    half = resid.shape[1] // 2
-    result = lax.ppermute(resid[:, :half].astype(BF), GROUP, OWN_OUT)
+        resid = None if last else total
+    half = total.shape[1] // 2
+    resid = caches[-1][5][:, :half] + vectors[-1][4:5, :half] + total[:, :half]
+    resid = resid + swap_cross(total[:, half:].astype(BF)).astype(F32)
+    result = lax.ppermute(resid.astype(BF), GROUP, OWN_OUT)
     grad = arrive(cotangent)
     parts, copies = [], []
     for at in reversed(range(layers)):
         grad, grads = layer_backward(grad, caches[at], weights[at], mine_out[at])
-        if at == layers - 1:
-            grad, result = lax.optimization_barrier((grad, result))
         copies += pack_copies(len(parts), at * LAYER_ROWS, units_here, heads_here, 2 * half)
         parts += pack_grads(grads)
     grad_tokens = lax.ppermute(grad[:, :half].astype(BF), GROUP, OWN_OUT).astype(F32)

time: 515 us -> 499 us (0.969)
  Pallas kernels: 124 us -> 308 us
  waiting for transfers between devices: 182 us -> 64.2 us
  matrix products: 63.3 us -> 0 us
  starting transfers between devices: 55.2 us -> 31.5 us
  local copies, waits for them, and re-layouts: 45.7 us -> 64.8 us
  other arithmetic: 32.3 us -> 20.5 us
    pallas_call x4 -> x8, Pallas kernels: 37.6 us -> 221 us  [call(): pl.pallas_call(kernel, in_specs=[vmem] * len(inputs), out_specs=[vmem] *...]
    ppermute x12 -> x5, waiting for transfers between devices: 120 us -> 2.9 us  [swap_cross(): return lax.ppermute(value, ('row', 'col'), CROSS)]
    dot_general x24 -> x0, matrix products: 63.3 us -> none  [dot(): lax.dot_general(left, right, (((left_axis,), (right_axis,)), ((), ())), p...]
    ppermute x18 -> x2, starting transfers between devices: 17.8 us -> 0.86 us  [swap_core(): return lax.ppermute(value, 'core', [(0, 1), (1, 0)])]
    dynamic_slice x6 -> x15, local copies, waits for them, and re-layouts: 1.07 us -> 14.4 us  [take(): return lax.dynamic_slice_in_dim(value, core * size, size, axis)]
    reduce_sum x14 -> x0, other arithmetic: 13 us -> none  [the longest x2 4.2 us: layer_backward(): gain_two = jnp.sum(normed_two_grad * normal_two, axis=0)]
    ppermute x12 -> x5, starting transfers between devices: 16.3 us -> 4.73 us  [swap_cross(): return lax.ppermute(value, ('row', 'col'), CROSS)]
    ppermute x9, waiting for transfers between devices: 45.3 us -> 55.6 us  [swap_col(): return lax.ppermute(value, 'col', [(0, 1), (1, 0)])]
  transfers between devices with their start and end apart: 45 -> 22, of which waited for: 23 -> 9; matrix products, arithmetic and copies ran while one was open for 18% -> 12% of each run, Pallas kernels for 5% -> 36%
where the time goes in v3:
time: 499 us; the launch traced here: 491 us
  Pallas kernels  308 us (62%)
  local copies, waits for them, and re-layouts  64.8 us (13%)
  waiting for transfers between devices  64.2 us (13%)
  starting transfers between devices  31.5 us (6%)
  other arithmetic  20.5 us (4%)
    pallas_call x8, Pallas kernels, call(): pl.pallas_call(kernel, in_specs=[vmem] * len(inputs), out_specs=[vmem] *...  221 us
    pallas_call x1, Pallas kernels, reduce_all(): pl.pallas_call(functools.partial(reduce_kernel, chunks, {'inputs': len(pa...  79.3 us
    ppermute x9, waiting for transfers between devices, swap_col(): return lax.ppermute(value, 'col', [(0, 1), (1, 0)])  55.6 us
    unnamed x108, local copies, waits for them, and re-layouts  23.6 us
    dynamic_slice x15, local copies, waits for them, and re-layouts, take(): return lax.dynamic_slice_in_dim(value, core * size, size, axis)  14.4 us
  transfers between devices with their start and end apart: 22, of which 9 were waited for; matrix products, arithmetic and copies ran while one was open for 12% of the time, Pallas kernels for 36%

profile of v3, /device:TPU:1, one launch (start us, length us, event | category | flops | bytes accessed | tf_op | source)
XLA Modules:
  0.0 491.0 jit_solution(12142955551055952714)
XLA Ops:
  0.7 2.8 collective-permute-start.1
  3.4 4.2 collective-permute-start
  13.5 1.5 collective-permute-start.6
  20.7 1.8 fusion.4
  22.5 2.9 fusion.3
  26.9 1.7 copy.50
  28.6 1.8 constant_dynamic-slice_fusion.2
  30.5 1.8 copy.49
  32.3 1.7 copy.48
  36.2 4.4 collective-permute-start.18
  41.4 1.9 collective-permute-start.17
  45.0 1.4 collective-permute-start.9
  47.7 2.4 maximum_convert_fusion.resid_ref
  50.1 1.4 collective-permute-start.8
  51.5 5.0 %collective-permute-done.17 = bf16[512,384]{1,0:T(8,128)(2,1)S(1)} collective-permute-done((bf16[512,384]{1,0:T(8,128)(2,1)}, bf16[512,384]{1,0:T(8,128)(2,1)S(1)}, u32[]{:S(2)}, u32[]{:S(2)}) %collective-permute-start.17) | collective-permute-done | bytes 393248 | tf_op jit(solution)/shard_map/ppermute | solution.py:816
  56.5 1.3 maximum_convert_fusion.1.grad_ref
  57.7 6.2 %collective-permute-done.2 = bf16[576,384]{1,0:T(8,128)(2,1)S(1)} collective-permute-done((bf16[576,384]{1,0:T(8,128)(2,1)S(1)}, bf16[576,384]{1,0:T(8,128)(2,1)S(1)}, u32[]{:S(2)}, u32[]{:S(2)}) %collective-permute-start.2) | collective-permute-done | bytes 442400 | tf_op jit(solution)/shard_map/ppermute | solution.py:35
  64.8 8.5 %collective-permute-done.9 = bf16[576,384]{1,0:T(8,128)(2,1)S(1)} collective-permute-done((bf16[576,384]{1,0:T(8,128)(2,1)S(1)}, bf16[576,384]{1,0:T(8,128)(2,1)S(1)}, u32[]{:S(2)}, u32[]{:S(2)}) %collective-permute-start.9) | collective-permute-done | bytes 442400 | tf_op jit(solution)/shard_map/ppermute | solution.py:35
  73.4 2.2 collective-permute-start.13
  77.9 8.1 %collective-permute-done.7 = bf16[384,768]{1,0:T(8,128)(2,1)S(1)} collective-permute-done((bf16[384,768]{1,0:T(8,128)(2,1)S(1)}, bf16[384,768]{1,0:T(8,128)(2,1)S(1)}, u32[]{:S(2)}, u32[]{:S(2)}) %collective-permute-start.7) | collective-permute-done | bytes 589856 | tf_op jit(solution)/shard_map/ppermute | solution.py:35
  86.3 12.3 %collective-permute-done.8 = bf16[768,384]{1,0:T(8,128)(2,1)S(1)} collective-permute-done((bf16[768,384]{1,0:T(8,128)(2,1)S(1)}, bf16[768,384]{1,0:T(8,128)(2,1)S(1)}, u32[]{:S(2)}, u32[]{:S(2)}) %collective-permute-start.8) | collective-permute-done | bytes 589856 | tf_op jit(solution)/shard_map/ppermute | solution.py:35
  98.7 12.5 %collective-permute-done.13 = bf16[384,768]{1,0:T(8,128)(2,1)S(1)} collective-permute-done((bf16[384,768]{1,0:T(8,128)(2,1)S(1)}, bf16[384,768]{1,0:T(8,128)(2,1)S(1)}, u32[]{:S(2)}, u32[]{:S(2)}) %collective-permute-start.13) | collective-permute-done | bytes 589856 | tf_op jit(solution)/shard_map/ppermute | solution.py:35
  111.4 7.9 %collective-permute-done.14 = bf16[768,384]{1,0:T(8,128)(2,1)S(1)} collective-permute-done((bf16[768,384]{1,0:T(8,128)(2,1)S(1)}, bf16[768,384]{1,0:T(8,128)(2,1)S(1)}, u32[]{:S(2)}, u32[]{:S(2)}) %collective-permute-start.14) | collective-permute-done | bytes 589856 | tf_op jit(solution)/shard_map/ppermute | solution.py:35
  120.5 21.8 %attend_forward.2 = (f32[512,768]{1,0:T(8,128)S(1)}, bf16[1024,768]{1,0:T(8,128)(2,1)S(1)}, f32[576,1024]{1,0:T(8,128)}, bf16[192,1024]{1,0:T(8,128)(2,1)S(1)}, f32[3,1024]{1,0:T(4,128)S(1)}) custom-call(f32[512,768]{1,0:T(8,128)} %maximum_convert_fusion.resid_ref, bf16[576,768]{1,0:T(8,128)(2,1)S(1)} %pad_maximum_fusion.4.w_qkv_ref, ...), custom_call_target="tpu_custom_call" | custom-call | tf_op jit(solution)/shard_map/attend_forward/pallas_call | solution.py:423
  143.5 1.2 copy-done.4
  144.7 28.6 %feed_forward.2 = (f32[512,768]{1,0:T(8,128)S(1)}, bf16[1024,768]{1,0:T(8,128)(2,1)S(1)}, bf16[1024,768]{1,0:T(8,128)(2,1)}, bf16[1024,768]{1,0:T(8,128)(2,1)}) custom-call(f32[512,768]{1,0:T(8,128)} %copy-done.3, bf16[768,768]{1,0:T(8,128)(2,1)S(1)} %pad_maximum_fusion.w_up_ref, f32[1,768]{1,0:T(1,128)S(1)} %get-tuple-element.128.bias_ref, ...), custom_call_target="tpu_custom_call" | custom-call | tf_op jit(solution)/shard_map/feed_forward/pallas_call | solution.py:423
  173.4 1.4 maximum_maximum_fusion.1.w_out_ref
  175.0 21.0 %attend_forward.3 = (f32[512,768]{1,0:T(8,128)S(1)}, bf16[1024,768]{1,0:T(8,128)(2,1)S(1)}, f32[576,1024]{1,0:T(8,128)}, bf16[192,1024]{1,0:T(8,128)(2,1)S(1)}, f32[3,1024]{1,0:T(4,128)S(1)}) custom-call(f32[512,768]{1,0:T(8,128)} %copy-done.2, bf16[576,768]{1,0:T(8,128)(2,1)S(1)} %pad_maximum_fusion.5.w_qkv_ref, f32[64,2]{1,0:T(8,128)S(1)} %copy.51.gain_ref, ...), custom_call_target="tpu_custom_call" | custom-call | tf_op jit(solution)/shard_map/attend_forward/pallas_call | solution.py:423
  198.3 10.8 %feed_forward.3 = (f32[512,768]{1,0:T(8,128)S(1)}, bf16[1024,768]{1,0:T(8,128)(2,1)S(1)}, bf16[1024,768]{1,0:T(8,128)(2,1)}, bf16[1024,768]{1,0:T(8,128)(2,1)}) custom-call(f32[512,768]{1,0:T(8,128)} %copy-done, bf16[768,768]{1,0:T(8,128)(2,1)S(1)} %pad_maximum_fusion.2.w_up_ref, f32[1,768]{1,0:T(1,128)S(1)} %get-tuple-element.127.bias_ref, ...), custom_call_target="tpu_custom_call" | custom-call | tf_op jit(solution)/shard_map/feed_forward/pallas_call | solution.py:423
  210.2 29.8 %feed_backward.2 = (f32[512,768]{1,0:T(8,128)}, bf16[768,768]{1,0:T(8,128)(2,1)S(1)}, bf16[768,768]{1,0:T(8,128)(2,1)S(1)}, f32[4,768]{1,0:T(4,128)S(1)}) custom-call(f32[512,768]{1,0:T(8,128)} %maximum_convert_fusion.1.grad_ref, f32[512,768]{1,0:T(8,128)} %copy-done, bf16[1024,768]{1,0:T(8,128)(2,1)} %copy-done.10, ...), custom_call_target="tpu_custom_call" | custom-call | tf_op jit(solution)/shard_map/feed_backward/pallas_call | solution.py:423
  240.6 1.4 copy-done.7
  242.0 39.4 %attend_backward.2 = (f32[512,768]{1,0:T(8,128)S(1)}, bf16[576,768]{1,0:T(8,128)(2,1)S(1)}, bf16[192,768]{1,0:T(8,128)(2,1)S(1)}, f32[2,768]{1,0:T(2,128)S(1)}, f32[64,2]{1,0:T(8,128)S(1)}) custom-call(f32[512,768]{1,0:T(8,128)S(1)} %copy-done.7, f32[512,768]{1,0:T(8,128)} %copy-done.2, bf16[1024,768]{1,0:T(8,128)(2,1)} %copy-done.5, ...), custom_call_target="tpu_custom_call" | custom-call | tf_op jit(solution)/shard_map/attend_backward/pallas_call | solution.py:423
  283.6 30.5 %feed_backward.3 = (f32[512,768]{1,0:T(8,128)}, bf16[768,768]{1,0:T(8,128)(2,1)S(1)}, bf16[768,768]{1,0:T(8,128)(2,1)S(1)}, f32[4,768]{1,0:T(4,128)S(1)}) custom-call(f32[512,768]{1,0:T(8,128)} %copy-done.9, f32[512,768]{1,0:T(8,128)} %copy-done.3, bf16[1024,768]{1,0:T(8,128)(2,1)} %copy-done.8, bf16[1024,768]{1,0:T(8,128)(2,1)} %get-tuple-element.73.active_ref, ...), custom_call_target="tpu_custom_call" | custom-call | tf_op jit(solution)/shard_map/feed_backward/pallas_call | solution.py:423
  316.3 1.9 slice.199
  319.1 1.4 copy-done.6
  320.5 39.5 %attend_backward.3 = (f32[512,768]{1,0:T(8,128)S(1)}, bf16[576,768]{1,0:T(8,128)(2,1)S(1)}, bf16[192,768]{1,0:T(8,128)(2,1)S(1)}, f32[2,768]{1,0:T(2,128)S(1)}, f32[64,2]{1,0:T(8,128)S(1)}) custom-call(f32[512,768]{1,0:T(8,128)S(1)} %copy-done.6, f32[512,768]{1,0:T(8,128)} %maximum_convert_fusion.resid_ref, bf16[1024,768]{1,0:T(8,128)(2,1)} %copy-done.4, ...), custom_call_target="tpu_custom_call" | custom-call | tf_op jit(solution)/shard_map/attend_backward/pallas_call | solution.py:423
  362.5 1.9 collective-permute-start.19
  366.3 1.4 convert_bitcast_fusion.1
  369.1 3.6 collective-permute-start.20
  373.9 1.4 convert_bitcast_fusion
  377.5 2.9 collective-permute-done.21
  381.5 1.9 concatenate.104.refs_4_
  383.5 2.0 concatenate.107.refs_9_
  385.5 1.2 copy-done.13
  391.2 79.3 %reduce_all.1 = bf16[2,4864,384]{2,1,0:T(8,128)(2,1)} custom-call(bf16[768,768]{1,0:T(8,128)(2,1)S(1)} %get-tuple-element.81.refs_0_, bf16[768,768]{1,0:T(8,128)(2,1)S(1)} %get-tuple-element.82.refs_1_, bf16[576,768]{1,0:T(8,128)(2,1)S(1)} %copy-done.13, bf16[192,768]{1,0:T(8,128)(2,1)S(1)} %copy-done.23, bf16[16,768]{1,0:T(8,128)(2,1)S(1)} %copy-done.26, ...), custom_call_target="tpu_custom_call" | custom-call | flops 1494220800 | bytes 149422080 | tf_op jit(solution)/shard_map/reduce_all/pallas_call | solution.py:708
  470.5 7.7 %finish.1 = (f32[2,384,1536]{2,1,0:T(8,128)}, f32[2,1536,384]{2,1,0:T(8,128)}, f32[2,384,384]{2,1,0:T(8,128)}, f32[2,384,384]{2,1,0:T(8,128)}, f32[2,384,384]{2,...) custom-call(bf16[2,2,2432,384]{3,2,1,0:T(8,128)(2,1)} %bitcast.66), custom_call_target="tpu_custom_call" | custom-call | tf_op jit(solution)/shard_map/finish/pallas_call | solution.py:761
  479.4 3.8 collective-permute-start.16
  487.3 1.9 convert_element_type.56
  (203 shorter events, 56.2 us)
Async XLA Ops:
  0.6 15.0 %copy-start.44 = (bf16[2,384,384]{2,1,0:T(8,128)(2,1)S(1)}, bf16[2,384,384]{2,1,0:T(8,128)(2,1)}, u32[]{:S(2)}) copy-start(bf16[2,384,384]{2,1,0:T(8,128)(2,1)} %param.21) | copy-start | bytes 1769476
  0.7 44.4 %collective-permute-start.1 = (bf16[512,384]{1,0:T(8,128)(2,1)}, bf16[512,384]{1,0:T(8,128)(2,1)}, u32[]{:S(2)}, u32[]{:S(2)}) collective-permute-start(bf16[512,384]{1,0:T(8,128)(2,1)} %param.16), channel_id=1, source_target_pairs={{0,3},{1,0},{2,7},{3,4},{4,1},{5,2},{6,5},{7,6},{8,11},{9,8},{10,1... | collective-permute-start | bytes 1179656 | tf_op jit(solution)/shard_map/ppermute | solution.py:816
  3.4 44.1 %collective-permute-start = (bf16[512,384]{1,0:T(8,128)(2,1)}, bf16[512,384]{1,0:T(8,128)(2,1)}, u32[]{:S(2)}, u32[]{:S(2)}) collective-permute-start(bf16[512,384]{1,0:T(8,128)(2,1)} %param.16), channel_id=1, source_target_pairs={{0,0},{1,3},{2,4},{3,7},{4,2},{5,1},{6,6},{7,5},{8,8},{9,11},{10,1... | collective-permute-start | bytes 1179656 | tf_op jit(solution)/shard_map/ppermute | solution.py:816
  8.8 8.6 %copy-start.45 = (bf16[2,384,384]{2,1,0:T(8,128)(2,1)S(1)}, bf16[2,384,384]{2,1,0:T(8,128)(2,1)}, u32[]{:S(2)}) copy-start(bf16[2,384,384]{2,1,0:T(8,128)(2,1)} %param.20) | copy-start | bytes 1769476
  9.5 31.9 %collective-permute-start.3 = (bf16[192,384]{1,0:T(8,128)(2,1)}, bf16[192,384]{1,0:T(8,128)(2,1)}, u32[]{:S(2)}, u32[]{:S(2)}) collective-permute-start(bf16[192,384]{1,0:T(8,128)(2,1)} %dynamic-slice_bitcast_fusion.5), channel_id=1, source_target_pairs={{0,1},{1,0},{2,3},{3,2},{4,5},{5,4},{6,7},{7,6},{8,9},{9,8},{10,11... | collective-permute-start | bytes 442376 | tf_op jit(solution)/shard_map/ppermute | solution.py:35
  13.5 22.7 %collective-permute-start.6 = (f32[2,5,384]{2,1,0:T(8,128)}, f32[2,5,384]{2,1,0:T(8,128)}, u32[]{:S(2)}, u32[]{:S(2)}) collective-permute-start(f32[2,5,384]{2,1,0:T(8,128)} %stack.30), channel_id=1, source_target_pairs={{0,1},{1,0},{2,3},{3,2},{4,5},{5,4},{6,7},{7,6},{8,9},{9,8},{10,11... | collective-permute-start | bytes 46088 | tf_op jit(solution)/shard_map/ppermute | solution.py:35
  15.7 2.5 copy-start.46
  15.7 28.2 %collective-permute-start.10 = (bf16[192,384]{1,0:T(8,128)(2,1)}, bf16[192,384]{1,0:T(8,128)(2,1)}, u32[]{:S(2)}, u32[]{:S(2)}) collective-permute-start(bf16[192,384]{1,0:T(8,128)(2,1)} %dynamic-slice_bitcast_fusion.4), channel_id=1, source_target_pairs={{0,1},{1,0},{2,3},{3,2},{4,5},{5,4},{6,7},{7,6},{8,9},{9,8},{10,11... | collective-permute-start | bytes 442376 | tf_op jit(solution)/shard_map/ppermute | solution.py:35
  26.2 2.4 copy-start.43
  30.4 5.3 %copy-start.49 = (f32[2,64]{1,0:T(2,128)S(1)}, f32[2,64]{1,0:T(2,128)}, u32[]{:S(2)}) copy-start(f32[2,64]{1,0:T(2,128)} %param.23) | copy-start | bytes 1540
  30.4 5.3 %copy-start.50 = (f32[2,64]{1,0:T(2,128)S(1)}, f32[2,64]{1,0:T(2,128)}, u32[]{:S(2)}) copy-start(f32[2,64]{1,0:T(2,128)} %param.22) | copy-start | bytes 1540
  30.4 5.3 %copy-start.48 = (f32[2,1536]{1,0:T(2,128)S(1)}, f32[2,1536]{1,0:T(2,128)}, u32[]{:S(2)}) copy-start(f32[2,1536]{1,0:T(2,128)} %param.28) | copy-start | bytes 36868
  30.4 5.4 %copy-start.34 = (bf16[1,384,192]{1,2,0:T(8,128)(2,1)S(1)}, bf16[1,384,192]{1,2,0:T(8,128)(2,1)}, u32[]{:S(2)}) copy-start(bf16[1,384,192]{1,2,0:T(8,128)(2,1)} %copy.46) | copy-start | bytes 442372
  30.5 5.4 %copy-start.35 = (bf16[1,384,192]{1,2,0:T(8,128)(2,1)S(1)}, bf16[1,384,192]{1,2,0:T(8,128)(2,1)}, u32[]{:S(2)}) copy-start(bf16[1,384,192]{1,2,0:T(8,128)(2,1)} %copy.45) | copy-start | bytes 442372
  30.5 5.4 %copy-start.36 = (bf16[1,384,192]{1,2,0:T(8,128)(2,1)S(1)}, bf16[1,384,192]{1,2,0:T(8,128)(2,1)}, u32[]{:S(2)}) copy-start(bf16[1,384,192]{1,2,0:T(8,128)(2,1)} %copy.44) | copy-start | bytes 442372
  35.8 11.7 %copy-start.31 = (bf16[384,768]{1,0:T(8,128)(2,1)S(1)}, bf16[384,768]{1,0:T(8,128)(2,1)}, u32[]{:S(2)}) copy-start(bf16[384,768]{1,0:T(8,128)(2,1)} %dynamic-slice_bitcast_fusion.3) | copy-start | bytes 1769476
  36.1 84.4 %copy-start.20 = (f32[64,2]{1,0:T(8,128)}, f32[64,2]{1,0:T(8,128)S(1)}, u32[]{:S(2)}) copy-start(f32[64,2]{1,0:T(8,128)S(1)} %copy.47.gain_ref) | copy-start | bytes 1540
  36.2 13.8 %collective-permute-start.18 = (bf16[512,384]{1,0:T(8,128)(2,1)}, bf16[512,384]{1,0:T(8,128)(2,1)S(1)}, u32[]{:S(2)}, u32[]{:S(2)}) collective-permute-start(bf16[512,384]{1,0:T(8,128)(2,1)} %param.31), channel_id=1, source_target_pairs={{0,3},{1,0},{2,7},{3,4},{4,1},{5,2},{6,5},{7,6},{8,11},{9,8},{10,1... | collective-permute-start | bytes 1179656 | tf_op jit(solution)/shard_map/ppermute | solution.py:816
  41.4 15.1 %collective-permute-start.17 = (bf16[512,384]{1,0:T(8,128)(2,1)}, bf16[512,384]{1,0:T(8,128)(2,1)S(1)}, u32[]{:S(2)}, u32[]{:S(2)}) collective-permute-start(bf16[512,384]{1,0:T(8,128)(2,1)} %param.31), channel_id=1, source_target_pairs={{0,0},{1,3},{2,4},{3,7},{4,2},{5,1},{6,6},{7,5},{8,8},{9,11},{10,1... | collective-permute-start | bytes 1179656 | tf_op jit(solution)/shard_map/ppermute | solution.py:816
  43.9 20.0 %collective-permute-start.2 = (bf16[576,384]{1,0:T(8,128)(2,1)S(1)}, bf16[576,384]{1,0:T(8,128)(2,1)S(1)}, u32[]{:S(2)}, u32[]{:S(2)}) collective-permute-start(bf16[576,384]{1,0:T(8,128)(2,1)S(1)} %pad_maximum_fusion.8), channel_id=1, source_target_pairs={{0,1},{1,0},{2,3},{3,2},{4,5},{5,4},{6,7},{7,6},{8,9},{9,8},{10,11... | collective-permute-start | bytes 1327112 | tf_op jit(solution)/shard_map/ppermute | solution.py:35
  45.0 28.3 %collective-permute-start.9 = (bf16[576,384]{1,0:T(8,128)(2,1)S(1)}, bf16[576,384]{1,0:T(8,128)(2,1)S(1)}, u32[]{:S(2)}, u32[]{:S(2)}) collective-permute-start(bf16[576,384]{1,0:T(8,128)(2,1)S(1)} %pad_maximum_fusion.9), channel_id=1, source_target_pairs={{0,1},{1,0},{2,3},{3,2},{4,5},{5,4},{6,7},{7,6},{8,9},{9,8},{10,11... | collective-permute-start | bytes 1327112 | tf_op jit(solution)/shard_map/ppermute | solution.py:35
  47.5 38.5 %collective-permute-start.7 = (bf16[384,768]{1,0:T(8,128)(2,1)S(1)}, bf16[384,768]{1,0:T(8,128)(2,1)S(1)}, u32[]{:S(2)}, u32[]{:S(2)}) collective-permute-start(bf16[384,768]{1,0:T(8,128)(2,1)S(1)} %copy-done.31), channel_id=1, source_target_pairs={{0,1},{1,0},{2,3},{3,2},{4,5},{5,4},{6,7},{7,6},{8,9},{9,8},{10,11... | collective-permute-start | bytes 1769480 | tf_op jit(solution)/shard_map/ppermute | solution.py:35
  50.0 23.3 %copy-start.33 = (bf16[384,768]{1,0:T(8,128)(2,1)S(1)}, bf16[384,768]{1,0:T(8,128)(2,1)}, u32[]{:S(2)}) copy-start(bf16[384,768]{1,0:T(8,128)(2,1)} %dynamic-slice_bitcast_fusion.1) | copy-start | bytes 1769476
  50.0 25.5 %copy-start.38 = (bf16[1,384,192]{1,2,0:T(8,128)(2,1)S(1)}, bf16[1,384,192]{1,2,0:T(8,128)(2,1)}, u32[]{:S(2)}) copy-start(bf16[1,384,192]{1,2,0:T(8,128)(2,1)} %copy.50) | copy-start | bytes 442372
  50.1 25.5 %copy-start.40 = (bf16[1,384,192]{1,2,0:T(8,128)(2,1)S(1)}, bf16[1,384,192]{1,2,0:T(8,128)(2,1)}, u32[]{:S(2)}) copy-start(bf16[1,384,192]{1,2,0:T(8,128)(2,1)} %copy.49) | copy-start | bytes 442372
  50.1 25.5 %copy-start.42 = (bf16[1,384,192]{1,2,0:T(8,128)(2,1)S(1)}, bf16[1,384,192]{1,2,0:T(8,128)(2,1)}, u32[]{:S(2)}) copy-start(bf16[1,384,192]{1,2,0:T(8,128)(2,1)} %copy.48) | copy-start | bytes 442372
  50.1 48.6 %collective-permute-start.8 = (bf16[768,384]{1,0:T(8,128)(2,1)S(1)}, bf16[768,384]{1,0:T(8,128)(2,1)S(1)}, u32[]{:S(2)}, u32[]{:S(2)}) collective-permute-start(bf16[768,384]{1,0:T(8,128)(2,1)S(1)} %dynamic-slice_bitcast_fusion.2), channel_id=1, source_target_pairs={{0,1},{1,0},{2,3},{3,2},{4,5},{5,4},{6,7},{7,6},{8,9},{9,8},{10,11... | collective-permute-start | bytes 1769480 | tf_op jit(solution)/shard_map/ppermute | solution.py:35
  56.4 19.2 %collective-permute-start.4 = (bf16[192,768]{1,0:T(8,128)(2,1)S(1)}, bf16[192,768]{1,0:T(8,128)(2,1)S(1)}, u32[]{:S(2)}, u32[]{:S(2)}) collective-permute-start(bf16[192,768]{1,0:T(8,128)(2,1)S(1)} %pad_maximum_fusion.10.w_out_ref), channel_id=1, source_target_pairs={{0,4},{4,0},{1,5},{5,1},{2,6},{6,2},{3,7},{7,3},{8,12},{12,8},{9,1... | collective-permute-start | bytes 884744 | tf_op jit(solution)/shard_map/ppermute | solution.py:31
  57.7 18.0 %copy-start.32 = (bf16[768,384]{1,0:T(8,128)(2,1)S(1)}, bf16[768,384]{1,0:T(8,128)(2,1)}, u32[]{:S(2)}) copy-start(bf16[768,384]{1,0:T(8,128)(2,1)} %dynamic-slice_bitcast_fusion) | copy-start | bytes 1769476
  63.9 12.9 %collective-permute-start.11 = (bf16[192,768]{1,0:T(8,128)(2,1)S(1)}, bf16[192,768]{1,0:T(8,128)(2,1)S(1)}, u32[]{:S(2)}, u32[]{:S(2)}) collective-permute-start(bf16[192,768]{1,0:T(8,128)(2,1)S(1)} %pad_maximum_fusion.11.w_out_ref), channel_id=1, source_target_pairs={{0,4},{4,0},{1,5},{5,1},{2,6},{6,2},{3,7},{7,3},{8,12},{12,8},{9,1... | collective-permute-start | bytes 884744 | tf_op jit(solution)/shard_map/ppermute | solution.py:31
  73.4 37.9 %collective-permute-start.13 = (bf16[384,768]{1,0:T(8,128)(2,1)S(1)}, bf16[384,768]{1,0:T(8,128)(2,1)S(1)}, u32[]{:S(2)}, u32[]{:S(2)}) collective-permute-start(bf16[384,768]{1,0:T(8,128)(2,1)S(1)} %copy-done.33), channel_id=1, source_target_pairs={{0,1},{1,0},{2,3},{3,2},{4,5},{5,4},{6,7},{7,6},{8,9},{9,8},{10,11... | collective-permute-start | bytes 1769480 | tf_op jit(solution)/shard_map/ppermute | solution.py:35
  75.7 43.6 %collective-permute-start.14 = (bf16[768,384]{1,0:T(8,128)(2,1)S(1)}, bf16[768,384]{1,0:T(8,128)(2,1)S(1)}, u32[]{:S(2)}, u32[]{:S(2)}) collective-permute-start(bf16[768,384]{1,0:T(8,128)(2,1)S(1)} %copy-done.32), channel_id=1, source_target_pairs={{0,1},{1,0},{2,3},{3,2},{4,5},{5,4},{6,7},{7,6},{8,9},{9,8},{10,11... | collective-permute-start | bytes 1769480 | tf_op jit(solution)/shard_map/ppermute | solution.py:35
  76.8 42.5 %collective-permute-start.5 = (bf16[384,768]{1,0:T(8,128)(2,1)S(1)}, bf16[384,768]{1,0:T(8,128)(2,1)S(1)}, u32[]{:S(2)}, u32[]{:S(2)}) collective-permute-start(bf16[384,768]{1,0:T(8,128)(2,1)S(1)} %pad_maximum_fusion.6), channel_id=1, source_target_pairs={{0,3},{3,0},{1,2},{2,1},{4,7},{7,4},{5,6},{6,5},{8,11},{11,8},{9,1... | collective-permute-start | bytes 1769480 | tf_op jit(solution)/shard_map/ppermute | solution.py:39
  86.0 87.3 %collective-permute-start.12 = (bf16[384,768]{1,0:T(8,128)(2,1)S(1)}, bf16[384,768]{1,0:T(8,128)(2,1)S(1)}, u32[]{:S(2)}, u32[]{:S(2)}) collective-permute-start(bf16[384,768]{1,0:T(8,128)(2,1)S(1)} %pad_maximum_fusion.7), channel_id=1, source_target_pairs={{0,3},{3,0},{1,2},{2,1},{4,7},{7,4},{5,6},{6,5},{8,11},{11,8},{9,1... | collective-permute-start | bytes 1769480 | tf_op jit(solution)/shard_map/ppermute | solution.py:39
  144.7 28.6 %copy-start.18 = (bf16[192,1024]{1,0:T(8,128)(2,1)}, bf16[192,1024]{1,0:T(8,128)(2,1)S(1)}, u32[]{:S(2)}) copy-start(bf16[192,1024]{1,0:T(8,128)(2,1)S(1)} %get-tuple-element.78.mixed_ref) | copy-start | bytes 1179652
  210.2 29.8 %copy-start.16 = (f32[512,768]{1,0:T(8,128)}, f32[512,768]{1,0:T(8,128)S(1)}, u32[]{:S(2)}) copy-start(f32[512,768]{1,0:T(8,128)S(1)} %get-tuple-element.62) | copy-start | bytes 4718596
  283.6 30.5 %copy-start.22 = (bf16[192,768]{1,0:T(8,128)(2,1)}, bf16[192,768]{1,0:T(8,128)(2,1)S(1)}, u32[]{:S(2)}) copy-start(bf16[192,768]{1,0:T(8,128)(2,1)S(1)} %get-tuple-element.84.refs_3_) | copy-start | bytes 884740
  283.6 30.5 %copy-start.28 = (f32[64,2]{1,0:T(8,128)}, f32[64,2]{1,0:T(8,128)S(1)}, u32[]{:S(2)}) copy-start(f32[64,2]{1,0:T(8,128)S(1)} %get-tuple-element.87) | copy-start | bytes 1540
  283.6 35.5 %copy-start.19 = (bf16[192,1024]{1,0:T(8,128)(2,1)S(1)}, bf16[192,1024]{1,0:T(8,128)(2,1)}, u32[]{:S(2)}) copy-start(bf16[192,1024]{1,0:T(8,128)(2,1)} %copy-done.18) | copy-start | bytes 1179652
  283.6 35.5 %copy-start.21 = (f32[64,2]{1,0:T(8,128)S(1)}, f32[64,2]{1,0:T(8,128)}, u32[]{:S(2)}) copy-start(f32[64,2]{1,0:T(8,128)} %copy-done.20) | copy-start | bytes 1540
  318.2 160.0 %collective-permute-start.15 = (bf16[512,384]{1,0:T(8,128)(2,1)}, bf16[512,384]{1,0:T(8,128)(2,1)}, u32[]{:S(2)}, u32[]{:S(2)}) collective-permute-start(bf16[512,384]{1,0:T(8,128)(2,1)} %slice.199), channel_id=1, source_target_pairs={{0,3},{3,0},{1,2},{2,1},{4,7},{7,4},{5,6},{6,5},{8,11},{11,8},{9,1... | collective-permute-start | bytes 1179656 | tf_op jit(solution)/shard_map/ppermute | solution.py:39
  362.5 124.9 %collective-permute-start.19 = (bf16[512,384]{1,0:T(8,128)(2,1)}, bf16[512,384]{1,0:T(8,128)(2,1)}, u32[]{:S(2)}, u32[]{:S(2)}) collective-permute-start(bf16[512,384]{1,0:T(8,128)(2,1)} %slice.198), channel_id=1, source_target_pairs={{0,0},{3,1},{4,2},{7,3},{2,4},{1,5},{6,6},{5,7},{8,8},{11,9},{12,1... | collective-permute-start | bytes 1179656 | tf_op jit(solution)/shard_map/ppermute | solution.py:858
  369.1 7.7 %collective-permute-start.20 = (bf16[128]{0:T(256)(128)(2,1)}, bf16[128]{0:T(256)(128)(2,1)}, u32[]{:S(2)}, u32[]{:S(2)}) collective-permute-start(bf16[128]{0:T(256)(128)(2,1)} %convert_element_type.59), channel_id=1, source_target_pairs={{0,3},{3,0},{1,2},{2,1},{4,7},{7,4},{5,6},{6,5},{8,11},{11,8},{9,1... | collective-permute-start | bytes 776 | tf_op jit(solution)/shard_map/ppermute | solution.py:39
  376.7 3.6 collective-permute-start.21
  470.5 7.7 %copy-start.1 = (f32[512,768]{1,0:T(8,128)S(1)}, f32[512,768]{1,0:T(8,128)}, u32[]{:S(2)}) copy-start(f32[512,768]{1,0:T(8,128)} %copy-done) | copy-start | bytes 4718596
  470.5 7.7 %copy-start.17 = (f32[512,768]{1,0:T(8,128)S(1)}, f32[512,768]{1,0:T(8,128)}, u32[]{:S(2)}) copy-start(f32[512,768]{1,0:T(8,128)} %copy-done.16) | copy-start | bytes 4718596
  470.5 7.7 %copy-start.47 = (f32[384]{0:T(512)S(1)}, f32[384]{0:T(512)}, u32[]{:S(2)}) copy-start(f32[384]{0:T(512)} %slice_reduce_fusion) | copy-start | bytes 4612
  479.4 10.6 %collective-permute-start.16 = (bf16[512,384]{1,0:T(8,128)(2,1)S(1)}, bf16[512,384]{1,0:T(8,128)(2,1)S(1)}, u32[]{:S(2)}, u32[]{:S(2)}) collective-permute-start(bf16[512,384]{1,0:T(8,128)(2,1)S(1)} %add_convert_fusion), channel_id=1, source_target_pairs={{0,0},{3,1},{4,2},{7,3},{2,4},{1,5},{6,6},{5,7},{8,8},{11,9},{12,1... | collective-permute-start | bytes 1179656 | tf_op jit(solution)/shard_map/ppermute | solution.py:851
  (25 other events, 30.4 us)
